TPU v7x, 32 devices: a whole 2x2x4 slice. The times are simulated.
32 devices in a mesh: space: 8 (over z, x), blk: 4 (over y, core).
Axes of the slice: x: 2, y: 2, z: 4, core: 2. Of those that a mesh axis runs over, the one named last changes fastest.
Arguments:
- snapshots: float32 [64, 16, 16, 512], P('space', None, None, 'blk'), may hold values from -40 to 40, as said below
Outputs:
- rotated: float32 [64, 16, 16, 512], P('space', None, None, 'blk')
Inputs may be any that keep to these rules, and one draw needn't show every extreme that they name: `snapshots`: snapshot values are finite reals.
All inputs are finite; a program needn't handle non-finite values.
Results may differ from a plain program's by a relative error of at most 0.0003.
Values sent between devices are 32-bit elements; how exact they have to be, the bound alone decides.
No kernel may reach another device: no remote copies, remote signals or barrier semaphores. Data moves between devices by JAX's collectives and lax.ppermute only.
A program may use at most 64 MiB of HBM per device.

v0:
```python
import jax
import jax.numpy as jnp
from jax import lax
from jax.sharding import PartitionSpec as P

ROUNDS = 2


def padded_2(shard, sides, width):
    for axis, dim in sides:
        size, length = (lax.axis_size(axis), shard.shape[dim])
        up = [(i, (i + 1) % size) for i in range(size - 1)]
        down = [(j, i) for i, j in up]
        last = lax.slice_in_dim(shard, length - width, length, axis=dim)
        first = lax.slice_in_dim(shard, 0, width, axis=dim)
        before = lax.ppermute(last, axis, up)
        after = lax.ppermute(first, axis, down)
        shard = jnp.concatenate([before, shard, after], axis=dim)
    return shard


def from_partner(block, axis, stride):
    count = lax.axis_size(axis)
    route = []
    for low in range(count):
        high = low | 1 << stride
        if high != low and high < count:
            route += [(low, high), (high, low)]
    return lax.ppermute(block, axis, route)


def weighted(block):
    padded = padded_2(block, (("space", 0),), 1)
    layers = block.shape[0]
    cells_y = block.shape[1]
    cells_z = block.shape[2]
    sides = jnp.pad(block, ((0, 0), (1, 1), (1, 1), (0, 0)))
    near = padded[2:] + padded[:-2]
    near = near + sides[:, 2:, 1:-1] + sides[:, :-2, 1:-1]
    near = near + sides[:, 1:-1, 2:] + sides[:, 1:-1, :-2]
    total_x = layers * lax.axis_size("space")
    pos_x = lax.axis_index("space") * layers + jnp.arange(layers, dtype=jnp.int32)
    pos_y = jnp.arange(cells_y, dtype=jnp.int32)
    pos_z = jnp.arange(cells_z, dtype=jnp.int32)
    deg_x = (pos_x > 0).astype(jnp.float32) + (pos_x < total_x - 1).astype(jnp.float32)
    deg_y = (pos_y > 0).astype(jnp.float32) + (pos_y < cells_y - 1).astype(jnp.float32)
    deg_z = (pos_z > 0).astype(jnp.float32) + (pos_z < cells_z - 1).astype(jnp.float32)
    degree = deg_x[:, None, None] + deg_y[None, :, None] + deg_z[None, None, :]
    return block + (degree[..., None] * block - near)


def gram_of(left, right):
    width = left.shape[-1]
    return lax.dot_general(
        left.reshape(-1, width),
        right.reshape(-1, width),
        (((0,), (0,)), ((), ())),
        precision=lax.Precision.HIGHEST,
        preferred_element_type=jnp.float32,
    )


def rotation(own_diag, peer_diag, cross, parity):
    denom = jnp.diagonal(own_diag)[:, None] + jnp.diagonal(peer_diag)[None, :]
    ratios = cross / denom
    eye_mat = jnp.eye(cross.shape[0], dtype=jnp.float32)
    normal_mat = eye_mat + jnp.dot(
        ratios, ratios.T, precision=lax.Precision.HIGHEST, preferred_element_type=jnp.float32
    )
    factor = jnp.linalg.cholesky(normal_mat)
    inverse = jax.scipy.linalg.cho_solve((factor, True), eye_mat)
    solved = jax.scipy.linalg.cho_solve((factor, True), ratios)
    keep_mat = 2.0 * inverse - eye_mat
    take_mat = 2.0 * parity * solved.T
    return (keep_mat, take_mat)


def mix_blocks(own_block, peer_block, keep_mat, take_mat):
    width = own_block.shape[-1]
    first = jnp.dot(
        own_block.reshape(-1, width),
        keep_mat,
        precision=lax.Precision.HIGHEST,
        preferred_element_type=jnp.float32,
    )
    second = jnp.dot(
        peer_block.reshape(-1, width),
        take_mat,
        precision=lax.Precision.HIGHEST,
        preferred_element_type=jnp.float32,
    )
    return (first + second).reshape(own_block.shape)


def shards(snapshots):
    own_block = snapshots
    for sweep_round in range(ROUNDS):
        parity = ((lax.axis_index("blk") >> sweep_round & 1) * 2 - 1).astype(jnp.float32)
        outgoing = own_block
        incoming = from_partner(outgoing, "blk", sweep_round)
        image = weighted(own_block)
        local_diag = gram_of(image, own_block)
        local_cross = gram_of(image, incoming)
        own_diag, cross = lax.psum((local_diag, local_cross), "space")
        peer_diag = from_partner(own_diag, "blk", sweep_round)
        keep_mat, take_mat = rotation(own_diag, peer_diag, cross, parity)
        own_block = mix_blocks(own_block, incoming, keep_mat, take_mat)
    return own_block


def solution(mesh):
    return jax.shard_map(
        shards,
        mesh=mesh,
        in_specs=(P("space", None, None, "blk"),),
        out_specs=P("space", None, None, "blk"),
        check_vma=False,
    )
```

profile of v0, /device:TPU:0, one launch (start us, length us, event | category | flops | bytes accessed | tf_op | source)
XLA Modules:
  0.0 270.0 jit_solution(5520724226679208195)
XLA Ops:
  6.5 0.5 collective-permute-start.2
  7.0 1.0 fusion.37
  8.0 4.4 %collective-permute-start.1 = (f32[1,16,16,128]{3,2,1,0:T(8,128)S(1)}, f32[1,16,16,128]{3,2,1,0:T(8,128)S(1)}, u32[]{:S(2)}, u32[]{:S(2)}) collective-permute-start(f32[1,16,16,128]{3,2,1,0:T(8,128)S(1)} %get-tuple-element.14), channel_id=1, source_target_pairs={{0,4},{4,8},{8,12},{12,16},{16,20},{20,24},{24,28},{1,5},{5,9},{9,... | collective-permute-start | bytes 393224 | tf_op jit(solution)/shard_map/ppermute | solution.py:16
  12.4 1.3 collective-permute-start
  13.9 1.9 collective-permute-done.1
  15.8 4.1 %collective-permute-done = f32[1,16,16,128]{3,2,1,0:T(8,128)S(1)} collective-permute-done((f32[1,16,16,128]{3,2,1,0:T(8,128)S(1)}, f32[1,16,16,128]{3,2,1,0:T(8,128)S(1)}, u32[]{:S(2)}, u32[]{:S(2)}) %collective-permute-start) | collective-permute-done | bytes 131104 | tf_op jit(solution)/shard_map/ppermute | solution.py:17
  19.9 5.4 %fusion.7 = f32[8,16,16,128]{3,2,1,0:T(8,128)S(1)} fusion(f32[8,16,16,128]{3,2,1,0:T(8,128)} %param.4, f32[1,16,16,128]{3,2,1,0:T(8,128)S(1)} %collective-permute-done.1, f32[1,16,16,128]{3,2,1,0:T(8,128)S(1)} %collective-permute-done, f32[8,16,16]{2,1,0:T(8,128)S(1)} %broadcast_add_fusion), kind=kLoop, calls=%fused_computation.30 | loop fusion | flops 2621440 | bytes 2367488 | tf_op jit(solution)/shard_map/add | solution.py:49
  25.3 2.5 convolution_bitcast_fusion.1
  27.8 2.5 convolution_bitcast_fusion.2
  30.6 71.0 %all-reduce.9.cloned.1.call-done = (f32[128,128]{1,0:T(8,128)}, f32[128,128]{1,0:T(8,128)}) async-done(((f32[128,128]{1,0:T(8,128)}, f32[128,128]{1,0:T(8,128)}), (f32[128,128]{1,0:T(8,128)}, f32[128,128]{1,0:T(8,128)})) %all-reduce.9.cloned.1.call-update) | async-done | bytes 131088 | tf_op jit(solution)/shard_map/psum | solution.py:104
  101.6 2.0 gather_fusion
  103.5 1.2 gather_fusion.1
  104.8 0.3 convolution_add_fusion.3
  105.3 11.7 %cholesky.44 = f32[128,128]{1,0:T(8,128)S(1)} custom-call(f32[128,128]{1,0:T(8,128)S(1)} %fusion.33), custom_call_target="Cholesky" | custom-call | tf_op jit(solution)/shard_map/jit(cholesky)/cholesky | solution.py:70
  117.0 0.6 compare_reduce_fusion.1
  117.6 0.7 fusion.20
  118.3 9.8 %custom-call.18 = f32[1,128,128]{1,2,0:T(8,128)S(1)} custom-call(f32[1,128,128]{2,1,0:T(8,128)S(1)} %fusion.20), custom_call_target="InvertDiagBlocksLowerTriangular" | custom-call | tf_op jit(solution)/shard_map/jit(_cho_solve)/triangular_solve | solution.py:71
  128.1 0.3 fusion.18
  128.4 0.3 fusion.29
  128.7 0.3 fusion.1
  129.0 1.0 fusion.38
  130.3 1.1 convolution_add_fusion.1
  131.3 0.3 copy.16
  131.7 1.5 collective-permute-start.6
  133.2 0.8 copy.18
  134.0 2.7 collective-permute-start.5
  136.7 0.7 copy.17
  137.4 1.5 collective-permute-start.4
  138.9 1.2 collective-permute-done.5
  140.1 4.7 %collective-permute-done.4 = f32[1,16,16,128]{3,2,1,0:T(8,128)S(1)} collective-permute-done((f32[1,16,16,128]{3,2,1,0:T(8,128)}, f32[1,16,16,128]{3,2,1,0:T(8,128)S(1)}, u32[]{:S(2)}, u32[]{:S(2)}) %collective-permute-start.4) | collective-permute-done | bytes 131104 | tf_op jit(solution)/shard_map/ppermute | solution.py:17
  144.8 0.5 fusion.13
  145.3 2.5 fusion.39
  147.8 9.5 %collective-permute-done.6 = f32[8,16,16,128]{3,2,1,0:T(8,128)S(1)} collective-permute-done((f32[8,16,16,128]{3,2,1,0:T(8,128)S(1)}, f32[8,16,16,128]{3,2,1,0:T(8,128)S(1)}, u32[]{:S(2)}, u32[]{:S(2)}) %collective-permute-start.6) | collective-permute-done | bytes 1048608 | tf_op jit(solution)/shard_map/ppermute | solution.py:29
  157.3 2.5 convolution_bitcast_fusion
  159.8 69.3 %all-reduce.7.cloned.1.call-done = (f32[128,128]{1,0:T(8,128)}, f32[128,128]{1,0:T(8,128)}) async-done(((f32[128,128]{1,0:T(8,128)}, f32[128,128]{1,0:T(8,128)}), (f32[128,128]{1,0:T(8,128)}, f32[128,128]{1,0:T(8,128)})) %all-reduce.7.cloned.1.call-update) | async-done | bytes 131088 | tf_op jit(solution)/shard_map/psum | solution.py:104
  229.1 1.5 collective-permute-start.7
  230.6 2.0 gather_fusion.2
  232.6 1.0 collective-permute-done.7
  233.6 1.2 gather_fusion.3
  234.9 0.3 convolution_add_fusion.2
  235.3 11.7 %cholesky.55 = f32[128,128]{1,0:T(8,128)S(1)} custom-call(f32[128,128]{1,0:T(8,128)S(1)} %fusion.27), custom_call_target="Cholesky" | custom-call | tf_op jit(solution)/shard_map/jit(cholesky)/cholesky | solution.py:70
  247.1 0.6 compare_reduce_fusion
  247.7 0.7 fusion.21
  248.4 9.8 %custom-call.20 = f32[1,128,128]{1,2,0:T(8,128)S(1)} custom-call(f32[1,128,128]{2,1,0:T(8,128)S(1)} %fusion.21), custom_call_target="InvertDiagBlocksLowerTriangular" | custom-call | tf_op jit(solution)/shard_map/jit(_cho_solve)/triangular_solve | solution.py:71
  258.5 0.3 fusion.23
  258.8 0.3 fusion
  259.1 1.8 fusion.40
  261.2 2.0 convolution_add_fusion
  (28 shorter events, 1.4 us)
Async XLA Ops:
  6.5 95.0 %all-reduce.9.cloned.1.call-start = ((), (), s32[]{:S(2)}) async-start(), calls=%async_computation.1 | async-start | bytes 262144 | tf_op jit(solution)/shard_map/psum | solution.py:104
  6.5 21.2 %collective-permute-start.2 = (f32[8,16,16,128]{3,2,1,0:T(8,128)}, f32[8,16,16,128]{3,2,1,0:T(8,128)S(1)}, u32[]{:S(2)}, u32[]{:S(2)}) collective-permute-start(f32[8,16,16,128]{3,2,1,0:T(8,128)} %param.4), channel_id=1, source_target_pairs={{0,1},{1,0},{2,3},{3,2},{4,5},{5,4},{6,7},{7,6},{8,9},{9,8},{10,11... | collective-permute-start | bytes 3145736 | tf_op jit(solution)/shard_map/ppermute | solution.py:29
  8.0 7.8 %collective-permute-start.1 = (f32[1,16,16,128]{3,2,1,0:T(8,128)S(1)}, f32[1,16,16,128]{3,2,1,0:T(8,128)S(1)}, u32[]{:S(2)}, u32[]{:S(2)}) collective-permute-start(f32[1,16,16,128]{3,2,1,0:T(8,128)S(1)} %get-tuple-element.14), channel_id=1, source_target_pairs={{0,4},{4,8},{8,12},{12,16},{16,20},{20,24},{24,28},{1,5},{5,9},{9,... | collective-permute-start | bytes 393224 | tf_op jit(solution)/shard_map/ppermute | solution.py:16
  12.4 7.5 %collective-permute-start = (f32[1,16,16,128]{3,2,1,0:T(8,128)S(1)}, f32[1,16,16,128]{3,2,1,0:T(8,128)S(1)}, u32[]{:S(2)}, u32[]{:S(2)}) collective-permute-start(f32[1,16,16,128]{3,2,1,0:T(8,128)S(1)} %get-tuple-element.13), channel_id=1, source_target_pairs={{4,0},{8,4},{12,8},{16,12},{20,16},{24,20},{28,24},{5,1},{9,5},{13... | collective-permute-start | bytes 393224 | tf_op jit(solution)/shard_map/ppermute | solution.py:17
  13.9 11.4 %copy-start = (f32[8,16,16,128]{3,2,1,0:T(8,128)S(1)}, f32[8,16,16,128]{3,2,1,0:T(8,128)}, u32[]{:S(2)}) copy-start(f32[8,16,16,128]{3,2,1,0:T(8,128)} %param.4) | copy-start | bytes 3145732
  30.3 198.8 %all-reduce.7.cloned.1.call-start = ((), (), s32[]{:S(2)}) async-start(), calls=%async_computation | async-start | bytes 262144 | tf_op jit(solution)/shard_map/psum | solution.py:104
  101.5 3.2 %copy-start.1 = (f32[128,128]{1,0:T(8,128)S(1)}, f32[128,128]{1,0:T(8,128)}, u32[]{:S(2)}) copy-start(f32[128,128]{1,0:T(8,128)} %get-tuple-element.9) | copy-start | bytes 196612
  101.5 2.0 collective-permute-start.3
  131.7 25.6 %collective-permute-start.6 = (f32[8,16,16,128]{3,2,1,0:T(8,128)S(1)}, f32[8,16,16,128]{3,2,1,0:T(8,128)S(1)}, u32[]{:S(2)}, u32[]{:S(2)}) collective-permute-start(f32[8,16,16,128]{3,2,1,0:T(8,128)S(1)} %bitcast.80), channel_id=1, source_target_pairs={{0,2},{2,0},{1,3},{3,1},{4,6},{6,4},{5,7},{7,5},{8,10},{10,8},{9,1... | collective-permute-start | bytes 3145736 | tf_op jit(solution)/shard_map/ppermute | solution.py:29
  134.0 6.1 %collective-permute-start.5 = (f32[1,16,16,128]{3,2,1,0:T(8,128)}, f32[1,16,16,128]{3,2,1,0:T(8,128)S(1)}, u32[]{:S(2)}, u32[]{:S(2)}) collective-permute-start(f32[1,16,16,128]{3,2,1,0:T(8,128)} %bitcast.85), channel_id=1, source_target_pairs={{0,4},{4,8},{8,12},{12,16},{16,20},{20,24},{24,28},{1,5},{5,9},{9,... | collective-permute-start | bytes 393224 | tf_op jit(solution)/shard_map/ppermute | solution.py:16
  137.4 7.4 %collective-permute-start.4 = (f32[1,16,16,128]{3,2,1,0:T(8,128)}, f32[1,16,16,128]{3,2,1,0:T(8,128)S(1)}, u32[]{:S(2)}, u32[]{:S(2)}) collective-permute-start(f32[1,16,16,128]{3,2,1,0:T(8,128)} %bitcast.86), channel_id=1, source_target_pairs={{4,0},{8,4},{12,8},{16,12},{20,16},{24,20},{28,24},{5,1},{9,5},{13... | collective-permute-start | bytes 393224 | tf_op jit(solution)/shard_map/ppermute | solution.py:17
  229.1 5.7 %copy-start.2 = (f32[128,128]{1,0:T(8,128)S(1)}, f32[128,128]{1,0:T(8,128)}, u32[]{:S(2)}) copy-start(f32[128,128]{1,0:T(8,128)} %get-tuple-element.6) | copy-start | bytes 196612
  229.1 4.5 %collective-permute-start.7 = (f32[128,128]{1,0:T(8,128)}, f32[128,128]{1,0:T(8,128)S(1)}, u32[]{:S(2)}, u32[]{:S(2)}) collective-permute-start(f32[128,128]{1,0:T(8,128)} %get-tuple-element.8), channel_id=1, source_target_pairs={{0,2},{2,0},{1,3},{3,1},{4,6},{6,4},{5,7},{7,5},{8,10},{10,8},{9,1... | collective-permute-start | bytes 196616 | tf_op jit(solution)/shard_map/ppermute | solution.py:29
Sparse Core Ops, SparseCore 0:
  30.4 71.0 all-reduce.8
  159.9 69.1 all-reduce.6
where the time goes:
time: 270 us
  waiting for transfers between devices  163 us (60%)
  other arithmetic  51.7 us (19%)
  matrix products  18.7 us (7%)
  between operations  13.7 us (5%)
  starting transfers between devices  13.6 us (5%)
  local copies, waits for them, and re-layouts  9.46 us (4%)
    psum x2, waiting for transfers between devices, shards(): own_diag, cross = lax.psum((local_diag, local_cross), 'space')  140 us
    another operation x6, other arithmetic, rotation(): factor = jnp.linalg.cholesky(normal_mat)  24.8 us
    another operation x4, other arithmetic, rotation(): inverse = jax.scipy.linalg.cho_solve((factor, True), eye_mat)  20.9 us
    ppermute x4, waiting for transfers between devices, from_partner(): return lax.ppermute(block, axis, route)  10.5 us
    dot_general x4, matrix products, gram_of(): lax.dot_general(left.reshape(-1, width), right.reshape(-1, width), (((0,)...  10 us
    ppermute x2, waiting for transfers between devices, padded_2(): after = lax.ppermute(first, axis, down)  8.87 us
    ppermute x2, starting transfers between devices, padded_2(): before = lax.ppermute(last, axis, up)  7.07 us
    gather x4, local copies, waits for them, and re-layouts, rotation(): denom = jnp.diagonal(own_diag)[:, None] + jnp.diagonal(peer_diag)[None, :]  6.43 us
  transfers between devices with their start and end apart: 10, of which 8 were waited for; matrix products, arithmetic and copies ran while one was open for 6% of the time, Pallas kernels for 0%

commit v1 on v0

v1 whole, which is shorter than its diff:
```python
import functools

import jax
import jax.numpy as jnp
from jax import lax
from jax.experimental import pallas as pl
from jax.experimental.pallas import tpu as pltpu
from jax.sharding import PartitionSpec as P

F32 = jnp.float32
BF16 = jnp.bfloat16
VMEM = pl.BlockSpec(memory_space=pltpu.VMEM)
PARAMS = pltpu.CompilerParams(vmem_limit_bytes=40 * 2**20)
CLOSE = 5e-4
STEPS = 5
CHUNKS = 1


def place():
    space = lax.axis_index("space")
    size = lax.axis_size("space")
    blk = lax.axis_index("blk")
    odd = space % 2
    has_a = jnp.where(odd == 1, 1, jnp.where(space < size - 1, 1, 0))
    has_b = jnp.where(odd == 1, jnp.where(space < size - 1, 1, 0), jnp.where(space > 0, 1, 0))
    return blk % 2, odd, has_a, has_b, (blk // 2) % 2


def cost(micros):
    return pl.CostEstimate(flops=int(micros * 1e9), bytes_accessed=1, transcendentals=0)


def rows_of(chunks, start, count):
    for chunk in chunks:
        if start < chunk.shape[0]:
            return chunk[start:start + count, :]
        start -= chunk.shape[0]


def shape_of(rows, width):
    return jax.ShapeDtypeStruct((rows, width), F32)


def exchanged(value, axis, mask):
    count = lax.axis_size(axis)
    return lax.ppermute(value, axis, [(i, i ^ mask) for i in range(count)])


def halves(value):
    high = value.astype(BF16)
    return high, (value - high.astype(F32)).astype(BF16)


def gram(left, right):
    def one(a, b):
        return lax.dot_general(a, b, (((0,), (0,)), ((), ())), preferred_element_type=F32)

    left_high, left_low = halves(left)
    right_high, right_low = halves(right)
    return one(left_high, right_high) + (one(left_high, right_low) + one(left_low, right_high))


def thirds(value):
    high = value.astype(BF16)
    rest = value - high.astype(F32)
    middle = rest.astype(BF16)
    return high, middle, (rest - middle.astype(F32)).astype(BF16)


def product(left, right):
    a, b, c = thirds(left)
    x, y, z = thirds(right)

    def pair(one, two, three, four):
        return jnp.dot(
            jnp.concatenate([one, two], axis=1), jnp.concatenate([three, four], axis=0),
            preferred_element_type=F32,
        )

    return pair(a, a, x, y) + (pair(b, a, x, z) + pair(c, b, x, y))


def product_3(left, right):
    left_high, left_low = halves(left)
    right_high, right_low = halves(right)
    deep = jnp.dot(
        jnp.concatenate([left_high, left_low], axis=1),
        jnp.concatenate([right_high, right_high], axis=0),
        preferred_element_type=F32,
    )
    return deep + jnp.dot(left_high, right_low, preferred_element_type=F32)


def product_nt(left, right):
    def one(a, b):
        return lax.dot_general(a, b, (((1,), (1,)), ((), ())), preferred_element_type=F32)

    left_high, left_low = halves(left)
    right_high, right_low = halves(right)
    return one(left_high, right_high) + (one(left_high, right_low) + one(left_low, right_high))


def inner_image(at, i, layers, cells_z):
    v = at(i)
    layer, width = v.shape
    place = lax.broadcasted_iota(jnp.int32, (layer, width), 0) % cells_z
    near = at(min(i + 1, layers - 1)) + at(max(i - 1, 0))
    near = near + jnp.concatenate([v[cells_z:], v[-cells_z:]], axis=0)
    near = near + jnp.concatenate([v[:cells_z], v[:-cells_z]], axis=0)
    near = near + jnp.where(place == cells_z - 1, v, pltpu.roll(v, layer - 1, 0))
    near = near + jnp.where(place == 0, v, pltpu.roll(v, 1, 0))
    return 7.0 * v - near


def inner_kernel(cells_y, cells_z, *refs):
    layer = cells_y * cells_z
    chunks = refs[:CHUNKS]
    p_ref, w_ref, c_ref, d_ref = refs[CHUNKS:]
    layers = p_ref.shape[0] // layer
    width = p_ref.shape[1]
    high = place()[0] == 1
    cross = jnp.zeros((width, width), F32)
    diag = jnp.zeros((8, width), F32)

    def at(j):
        return rows_of(chunks, j * layer, layer)

    for i in range(layers):
        rows = slice(i * layer, (i + 1) * layer)
        v = at(i)
        image = inner_image(at, i, layers, cells_z)
        w_ref[rows, :] = image
        diag += jnp.sum((image * v).reshape(layer // 8, 8, width), axis=0)
        peer = p_ref[rows, :]
        cross += gram(jnp.where(high, peer, image), jnp.where(high, image, peer))
    c_ref[...] = cross
    d_ref[...] = diag


def edge_kernel(edge_a, edge_b, p_ref, c_ref, d_ref, near_a, near_b, step_ref, msg_ref):
    layer, width = edge_a.shape
    layers = p_ref.shape[0] // layer
    half = width // 2
    high = place()[0] == 1
    odd = place()[1]
    total = c_ref[...]
    diag = d_ref[...]
    for k, (spot, edge, halo, there) in enumerate((
        ((1 - odd) * (layers - 1), edge_a, near_a, place()[2]),
        (odd * (layers - 1), edge_b, near_b, place()[3]),
    )):
        rows = pl.ds(pl.multiple_of(spot * layer, layer), layer)
        v = edge[...]
        step = jnp.where(there == 1, v - halo[...], 0.0)
        step_ref[k * layer:(k + 1) * layer, :] = step
        diag = diag + jnp.sum((step * v).reshape(layer // 8, 8, width), axis=0)
        peer = p_ref[rows, :]
        total = total + gram(jnp.where(high, peer, step), jnp.where(high, step, peer))
    msg_ref[:half, :] = jnp.where(high, total[half:], total[:half])
    msg_ref[half:, :] = jnp.broadcast_to(jnp.sum(diag, axis=0, keepdims=True), (8, width))


def beside(value):
    return jnp.concatenate(halves(value), axis=1)


def down_product(high, low, right):
    width = right.shape[1]
    both = beside(right)
    total = jnp.dot(high, both, preferred_element_type=F32)
    return total[:, :width] + (
        total[:, width:] + jnp.dot(low, both[:, :width], preferred_element_type=F32)
    )


def near_kernel(layer, cells_z, wo, own_step, peer_step, *refs):
    chunks = refs[:CHUNKS]
    xp, out, high_t, low_t, wp = refs[CHUNKS:]
    width = xp.shape[1]
    layers = xp.shape[0] // layer
    odd = place()[1]

    def at(j):
        return xp[j * layer:(j + 1) * layer, :]

    for i in range(layers):
        wp[i * layer:(i + 1) * layer, :] = inner_image(at, i, layers, cells_z)
    for k, spot in enumerate(((1 - odd) * (layers - 1), odd * (layers - 1))):
        rows = pl.ds(pl.multiple_of(spot * layer, layer), layer)
        wp[rows, :] += peer_step[k * layer:(k + 1) * layer, :]
    for i in range(layers):
        rows = slice(i * layer, (i + 1) * layer)
        image = wo[rows, :]
        for k in range(2):
            if i in (0, layers - 1):
                here = ((1 - odd), odd)[k] * (layers - 1) == i
                image = image + jnp.where(here, own_step[k * layer:(k + 1) * layer, :], 0.0)
        left = jnp.concatenate([image.T, wp[rows, :].T], axis=0)
        high_t[:, rows], low_t[:, rows] = halves(left)
    own = jnp.concatenate([chunk[...] for chunk in chunks], axis=0)
    for k, value in enumerate((own, xp[...])):
        out[:, k * width:(k + 1) * width] = down_product(high_t[...], low_t[...], value)


def far_kernel(high_t, low_t, far_own, out):
    out[...] = down_product(high_t[...], low_t[...], far_own[...])


def edges_kernel(x_ref, edge_a, edge_b, sems):
    layer = edge_a.shape[0]
    last = x_ref.shape[0] - layer
    odd = place()[1]
    copies = [
        pltpu.make_async_copy(x_ref.at[pl.ds(pl.multiple_of(start, layer), layer)], out, sems.at[k])
        for k, (start, out) in enumerate((((1 - odd) * last, edge_a), (odd * last, edge_b)))
    ]
    for copy in copies:
        copy.start()
    for copy in copies:
        copy.wait()


def eye_of(width):
    row = lax.broadcasted_iota(jnp.int32, (width, width), 0)
    col = lax.broadcasted_iota(jnp.int32, (width, width), 1)
    return jnp.where(row == col, 1.0, 0.0).astype(F32)


def rotations(pairs, high, x_ref):
    width = pairs[0][0].shape[1]
    half = width // 2
    eye = eye_of(width)
    ratios, normals = [], []
    for own, other in pairs:
        cross = jnp.concatenate(
            [jnp.where(high, other[:half], own[:half]), jnp.where(high, own[:half], other[:half])], axis=0
        )
        cross = jnp.where(high, cross.T, cross)
        rows = jnp.broadcast_to(own[half:half + 1], (width, width)).T
        ratio = cross / (rows + other[half:half + 1])
        ratios.append(ratio)
        normals.append(eye + product(ratio, ratio.T))
    bound = jnp.max(jnp.sum(jnp.abs(normals[0]), axis=0, keepdims=True), axis=1, keepdims=True)
    for normal in normals[1:]:
        size = jnp.max(jnp.sum(jnp.abs(normal), axis=0, keepdims=True), axis=1, keepdims=True)
        bound = jnp.maximum(bound, size)
    scale = 2.0 / (bound + 1.0)
    err = (bound - 1.0) * (0.5 * scale)

    def next_of(err):
        fresh = 2.0 / (2.0 - err * err)
        return err * err * (0.5 * fresh), fresh

    err, fresh = next_of(err)
    boths = []
    for normal in normals:
        image = scale * normal
        turn = fresh * (2.0 * eye - image)
        boths.append(jnp.concatenate([scale * turn, product_3(turn, image)], axis=1))
    for _ in range(STEPS - 1):
        err, fresh = next_of(err)
        boths = [product_3(fresh * (2.0 * eye - both[:, width:]), both) for both in boths]
    for k, both in enumerate(boths):
        x_ref[k] = both

    def step(err):
        err, fresh = next_of(err)
        for k in range(len(pairs)):
            both = x_ref[k]
            x_ref[k] = product_3(fresh * (2.0 * eye - both[:, width:]), both)
        return err

    lax.while_loop(lambda err: err > CLOSE, step, jnp.max(err))

    def refine(_=None):
        size = 0.0
        for k, (ratio, normal) in enumerate(zip(ratios, normals)):
            inverse = x_ref[k, :, :width]
            left_over = eye - product(inverse, normal)
            both = jnp.concatenate([inverse, product(inverse, ratio)], axis=1)
            x_ref[k] = both + product_3(left_over, both)
            size = jnp.maximum(size, jnp.max(jnp.sum(jnp.abs(left_over), axis=0)))
        return size

    lax.while_loop(lambda size: size > CLOSE, refine, refine())
    sign = jnp.where(high, 2.0, -2.0)
    return [
        (2.0 * x_ref[k, :, :width] - eye, sign * x_ref[k, :, width:]) for k in range(len(pairs))
    ]


def first_kernel(own_msg, core_msg, y_msg, far_msg, own_t, far_t, x_ref):
    width = own_msg.shape[1]
    pairs = [(own_msg[...], core_msg[...]), (y_msg[...], far_msg[...])]
    for (keep, take), out in zip(rotations(pairs, place()[0] == 1, x_ref), (own_t, far_t)):
        out[:, :width] = keep
        out[:, width:] = take


def apply_kernel(near_ref, far_ref, far_peer_ref, own_t, far_t, msg_ref):
    width = far_ref.shape[1]
    half = width // 2
    y_high = place()[4] == 1
    turn, far_turn = own_t[...], far_t[...]
    far_peer = jnp.concatenate([far_peer_ref[width:, :], far_peer_ref[:width, :]], axis=0)
    part = product_3(turn, jnp.concatenate([near_ref[...], far_ref[...], far_peer], axis=1))
    inside = turn * part[:, :2 * width]
    inside_high, inside_low = halves(inside)
    ones = jnp.ones((16, 2 * width), BF16)

    def lanes(value):
        return lax.dot_general(ones, value, (((1,), (1,)), ((), ())), preferred_element_type=F32)

    diag = lanes(inside_high) + lanes(inside_low)
    part = part[:, 2 * width:]
    cross = product_nt(jnp.where(y_high, far_turn, part), jnp.where(y_high, part, far_turn))
    msg_ref[:half, :] = jnp.where(y_high, cross[half:], cross[:half])
    msg_ref[half:, :] = diag[:8]


def wide_product(high_part, low_part, m_ref):
    width = m_ref.shape[1] // 2
    both = jnp.dot(high_part, m_ref[...], preferred_element_type=F32)
    rest = jnp.dot(low_part, m_ref[:, :width], preferred_element_type=F32)
    return both[:, :width] + (both[:, width:] + rest)


def turn_kernel(*refs):
    chunks = refs[:CHUNKS]
    xp, far_own, far_peer, own_t, far_t, high_ref, low_ref, m_ref = refs[CHUNKS:]
    width = xp.shape[1]
    step = 256
    for k, turn in enumerate((own_t, far_t)):
        m_ref[k, :, :width], m_ref[k, :, width:] = halves(
            jnp.concatenate([turn[:, :width].T, turn[:, width:].T], axis=0)
        )

    for i in range(xp.shape[0] // step):
        rows = slice(i * step, (i + 1) * step)
        ones = (rows_of(chunks, i * step, step), far_own[rows, :])
        for k, (one, two) in enumerate(zip(ones, (xp, far_peer))):
            parts = halves(jnp.concatenate([one, two[rows, :]], axis=1))
            turned = wide_product(*parts, m_ref.at[k])
            columns = slice(k * width, (k + 1) * width)
            high_ref[rows, columns], low_ref[rows, columns] = halves(turned)


def last_kernel(own_msg, y_msg, high_ref, low_ref, out, x_ref, m_ref, o_ref, sems):
    width = own_msg.shape[1]
    ((keep, take),) = rotations([(own_msg[...], y_msg[...])], place()[4] == 1, x_ref)
    m_ref[:, :width], m_ref[:, width:] = halves(jnp.concatenate([keep, take.T], axis=0))
    step = o_ref.shape[1]
    copies = []
    for k in range(o_ref.shape[0]):
        rows = slice(k * step, (k + 1) * step)
        o_ref[k] = wide_product(high_ref[rows, :], low_ref[rows, :], m_ref)
        copies.append(pltpu.make_async_copy(o_ref.at[k], out.at[pl.ds(k * step, step)], sems.at[k]))
        copies[-1].start()
    for copy in copies:
        copy.wait()


def power_of_two(count):
    return count & (count - 1) == 0


def summed_over_space(value, beside_it):
    count = lax.axis_size("space")
    blocks = lax.axis_size("blk")
    if not power_of_two(count):
        value = lax.psum(value, "space")
        beside_it([value])
        return value
    bits = [1 << bit for bit in range(count.bit_length() - 1)]
    orders = (bits, bits[-1:] + bits[:-1])
    sums = []
    for step in range(len(bits)):
        route = [
            (i * blocks + j, (i ^ orders[j & 1][step]) * blocks + j) for i in range(count) for j in range(blocks)
        ]
        there = lax.ppermute(value, ("space", "blk"), route)
        if step == len(bits) - 1:
            value = lax.optimization_barrier((value, beside_it(sums)))[0]
        value = value + there
        sums.append(value)
    return value


def shards(snapshots):
    layers, cells_y, cells_z, width = snapshots.shape
    layer = cells_y * cells_z
    cells = layers * layer
    own = snapshots.reshape(cells, width)
    size = lax.axis_size("space")
    route_a = [(i, i ^ 1) for i in range(size) if i ^ 1 < size]
    route_b = [(i, j) for i in range(1, size - 1, 2) for j in (i + 1,)]
    route_b = route_b + [(j, i) for i, j in route_b]
    half_rows = width // 2 + 8

    def call(body, inputs, outputs, scratch, micros, name, **more):
        return pl.pallas_call(
            body,
            in_specs=[VMEM] * len(inputs),
            out_specs=[VMEM] * len(outputs),
            out_shape=outputs,
            scratch_shapes=scratch,
            compiler_params=PARAMS,
            cost_estimate=cost(micros),
            name=name,
            **more,
        )(*inputs)

    chunks = [own]
    peer = exchanged(own, "blk", 1)
    edge_a, edge_b = pl.pallas_call(
        edges_kernel,
        in_specs=[pl.BlockSpec(memory_space=pl.ANY)],
        out_specs=[VMEM] * 2,
        out_shape=[shape_of(layer, width)] * 2,
        scratch_shapes=[pltpu.SemaphoreType.DMA((2,))],
        compiler_params=pltpu.CompilerParams(vmem_limit_bytes=53 * 2**20),
        cost_estimate=cost(0.1),
        name="edges",
    )(own)
    near_a = lax.ppermute(edge_a, "space", route_a)
    near_b = lax.ppermute(edge_b, "space", route_b)
    far_own = exchanged(own, "blk", 2)

    image, cross, diag = call(
        lambda *refs: inner_kernel(cells_y, cells_z, *refs), [*chunks, peer],
        [shape_of(cells, width), shape_of(width, width), shape_of(8, width)], [], 0.1, "inner_grams",
    )
    steps, msg = call(
        edge_kernel, [edge_a, edge_b, peer, cross, diag, near_a, near_b],
        [shape_of(2 * layer, width), shape_of(half_rows, width)], [], 0.1, "edge_grams",
    )
    turned_down = jax.ShapeDtypeStruct((2 * width, cells), BF16)
    near = []

    def near_products(sums):
        peer_steps = exchanged(lax.optimization_barrier((steps, sums[0]))[0], "blk", 1)
        near[:] = call(
            functools.partial(near_kernel, layer, cells_z), [image, steps, peer_steps, *chunks, peer],
            [shape_of(2 * width, 2 * width), turned_down, turned_down], [pltpu.VMEM((cells, width), F32)],
            2.5, "near_grams",
        )
        return near[0]

    msg = summed_over_space(msg, near_products)
    near_grams, high_t, low_t = near
    core_msg, y_msg, far_msg = (exchanged(msg, "blk", mask) for mask in (1, 2, 3))
    (far_grams,) = call(
        far_kernel, [high_t, low_t, far_own], [shape_of(2 * width, width)], [], 0.7, "far_grams"
    )
    far_peer_grams = exchanged(far_grams, "blk", 1)
    msg, far_grams = lax.optimization_barrier((msg, far_grams))
    own_t, far_t = call(
        first_kernel, [msg, core_msg, y_msg, far_msg], [shape_of(width, 2 * width)] * 2,
        [pltpu.VMEM((2, width, 2 * width), F32)], 4, "first_rotation",
    )
    (msg,) = call(
        apply_kernel, [near_grams, far_grams, far_peer_grams, own_t, far_t],
        [shape_of(half_rows, width)], [], 1.2, "rotated_grams",
    )
    bits = jax.ShapeDtypeStruct((cells, 2 * width), BF16)
    turned = []

    def turn_blocks(sums):
        ready = lax.optimization_barrier((far_own, sums[0]))[0]
        far_peer = exchanged(ready, "blk", 1)
        turned[:] = call(
            turn_kernel, [*chunks, peer, ready, far_peer, own_t, far_t], [bits, bits],
            [pltpu.VMEM((2, 2 * width, 2 * width), BF16)], 1.4, "turned_blocks",
        )
        return turned[0]

    own_msg = summed_over_space(msg, turn_blocks)
    highs, lows = turned
    y_msg = exchanged(own_msg, "blk", 2)

    step = 512
    mixed = pl.pallas_call(
        last_kernel,
        in_specs=[VMEM] * 4,
        out_specs=pl.BlockSpec(memory_space=pl.ANY),
        out_shape=shape_of(cells, width),
        scratch_shapes=[
            pltpu.VMEM((1, width, 2 * width), F32),
            pltpu.VMEM((2 * width, 2 * width), BF16),
            pltpu.VMEM((cells // step, step, width), F32),
            pltpu.SemaphoreType.DMA((cells // step,)),
        ],
        compiler_params=PARAMS,
        cost_estimate=cost(4),
        name="last_rotation",
    )(own_msg, y_msg, highs, lows)
    return mixed.reshape(snapshots.shape)


def solution(mesh):
    return jax.shard_map(
        shards,
        mesh=mesh,
        in_specs=(P("space", None, None, "blk"),),
        out_specs=P("space", None, None, "blk"),
        check_vma=False,
    )
```

time: 270 us -> 54.5 us (0.20)
  waiting for transfers between devices: 163 us -> 16.7 us
  other arithmetic: 51.7 us -> 0.04 us
  matrix products: 18.7 us -> 0 us
  between operations: 13.7 us -> 0.11 us
  Pallas kernels: 0 us -> 12.7 us
  starting transfers between devices: 13.6 us -> 24.8 us
  local copies, waits for them, and re-layouts: 9.46 us -> 0.01 us
    psum x2 -> x0, waiting for transfers between devices: 140 us -> none  [shards(): own_diag, cross = lax.psum((local_diag, local_cross), 'space')]
    another operation x10 -> x0, other arithmetic: 45.7 us -> none  [the longest x6 24.8 us: rotation(): factor = jnp.linalg.cholesky(normal_mat)]
    dot_general x10 -> x0, matrix products: 16.6 us -> none  [the longest x4 10 us: gram_of(): lax.dot_general(left.reshape(-1, width), right.reshape(-1, width), (((0,)...]
    pallas_call x0 -> x9, Pallas kernels: none -> 12.7 us  [the longest x7 8.23 us: call(): pl.pallas_call(body, in_specs=[VMEM] * len(inputs), out_specs=[VMEM] * le...]
    ppermute x8 -> x17, starting transfers between devices: 13.3 us -> 24.8 us  [the longest x6 15.9 us: summed_over_space(): there = lax.ppermute(value, ('space', 'blk'), route)]
    gather x4 -> x0, local copies, waits for them, and re-layouts: 6.43 us -> none  [rotation(): denom = jnp.diagonal(own_diag)[:, None] + jnp.diagonal(peer_diag)[None, :]]
    add x6, other arithmetic: 5.97 us -> 0.04 us  [summed_over_space(): value = value + there]
    ppermute x8 -> x17, waiting for transfers between devices: 22.5 us -> 16.7 us  [the longest x6 10.1 us: summed_over_space(): there = lax.ppermute(value, ('space', 'blk'), route)]
  transfers between devices with their start and end apart: 10 -> 17, of which waited for: 8 -> 9; matrix products, arithmetic and copies ran while one was open for 6% -> 0% of each run, Pallas kernels for 0% -> 16%
where the time goes in v1:
time: 54.5 us; the launch traced here: 54.3 us
  starting transfers between devices  24.8 us (46%)
  waiting for transfers between devices  16.7 us (31%)
  Pallas kernels  12.7 us (23%)
    ppermute x6, starting transfers between devices, summed_over_space(): there = lax.ppermute(value, ('space', 'blk'), route)  15.9 us
    ppermute x6, waiting for transfers between devices, summed_over_space(): there = lax.ppermute(value, ('space', 'blk'), route)  10.1 us
    pallas_call x7, Pallas kernels, call(): pl.pallas_call(body, in_specs=[VMEM] * len(inputs), out_specs=[VMEM] * le...  8.23 us
    ppermute x9, starting transfers between devices, exchanged(): return lax.ppermute(value, axis, [(i, i ^ mask) for i in range(count)])  6.67 us
    ppermute x9, waiting for transfers between devices, exchanged(): return lax.ppermute(value, axis, [(i, i ^ mask) for i in range(count)])  4.37 us
    pallas_call x1, Pallas kernels, shards(): pl.pallas_call(last_kernel, in_specs=[VMEM] * 4, out_specs=pl.BlockSpec(m...  3.46 us
    ppermute x1, waiting for transfers between devices, shards(): near_a = lax.ppermute(edge_a, 'space', route_a)  2.23 us
    ppermute x1, starting transfers between devices, shards(): near_a = lax.ppermute(edge_a, 'space', route_a)  1.56 us
  transfers between devices with their start and end apart: 17, of which 9 were waited for; matrix products, arithmetic and copies ran while one was open for 0% of the time, Pallas kernels for 16%

profile of v1, /device:TPU:0, one launch (start us, length us, event | category | flops | bytes accessed | tf_op | source)
XLA Modules:
  0.0 54.3 jit_solution(8537587180339473646)
XLA Ops:
  0.0 0.0 copy-start
  0.0 0.5 collective-permute-start
  0.5 2.6 %collective-permute-start.7 = (f32[2048,128]{1,0:T(8,128)}, f32[2048,128]{1,0:T(8,128)S(1)}, u32[]{:S(2)}, u32[]{:S(2)}) collective-permute-start(f32[2048,128]{1,0:T(8,128)} %bitcast.3), channel_id=1, source_target_pairs={{0,2},{1,3},{2,0},{3,1},{4,6},{5,7},{6,4},{7,5},{8,10},{9,11},{10,... | collective-permute-start | bytes 3145736 | tf_op jit(solution)/shard_map/ppermute | solution.py:46
  3.0 1.0 %edges.1 = (f32[256,128]{1,0:T(8,128)S(1)}, f32[256,128]{1,0:T(8,128)S(1)}) custom-call(f32[2048,128]{1,0:T(8,128)} %bitcast.4), custom_call_target="tpu_custom_call" | custom-call | flops 100000000 | bytes 1 | tf_op jit(solution)/shard_map/edges/pallas_call | solution.py:415
  4.0 1.6 %collective-permute-start.1 = (f32[256,128]{1,0:T(8,128)S(1)}, f32[256,128]{1,0:T(8,128)S(1)}, u32[]{:S(2)}, u32[]{:S(2)}) collective-permute-start(f32[256,128]{1,0:T(8,128)S(1)} %get-tuple-element.26.edge_a), channel_id=1, source_target_pairs={{0,4},{4,0},{8,12},{12,8},{16,20},{20,16},{24,28},{28,24},{1,5},{5... | collective-permute-start | bytes 393224 | tf_op jit(solution)/shard_map/ppermute | solution.py:425
  5.6 0.7 %collective-permute-start.2 = (f32[256,128]{1,0:T(8,128)S(1)}, f32[256,128]{1,0:T(8,128)S(1)}, u32[]{:S(2)}, u32[]{:S(2)}) collective-permute-start(f32[256,128]{1,0:T(8,128)S(1)} %get-tuple-element.27.edge_b), channel_id=1, source_target_pairs={{4,8},{12,16},{20,24},{8,4},{16,12},{24,20},{5,9},{13,17},{21,25},... | collective-permute-start | bytes 393224 | tf_op jit(solution)/shard_map/ppermute | solution.py:426
  6.3 0.0 collective-permute-done.refs_1_.p_ref
  6.3 0.0 copy-done
  6.3 1.2 %inner_grams.1 = (f32[2048,128]{1,0:T(8,128)S(1)}, f32[128,128]{1,0:T(8,128)S(1)}, f32[8,128]{1,0:T(8,128)S(1)}) custom-call(f32[2048,128]{1,0:T(8,128)S(1)} %bitcast.5, f32[2048,128]{1,0:T(8,128)S(1)} %collective-permute-done.refs_1_.p_ref), custom_call_target="tpu_custom_call" | custom-call | flops 100000000 | bytes 1 | tf_op jit(solution)/shard_map/inner_grams/pallas_call | solution.py:401
  7.4 2.2 %collective-permute-done.1.near_a = f32[256,128]{1,0:T(8,128)S(1)} collective-permute-done((f32[256,128]{1,0:T(8,128)S(1)}, f32[256,128]{1,0:T(8,128)S(1)}, u32[]{:S(2)}, u32[]{:S(2)}) %collective-permute-start.1) | collective-permute-done | bytes 131104 | tf_op jit(solution)/shard_map/ppermute | solution.py:425
  9.7 0.0 collective-permute-done.2.near_b
  9.7 0.3 edge_grams.1
  10.0 4.6 %collective-permute-start.3 = (f32[72,128]{1,0:T(8,128)S(1)}, f32[72,128]{1,0:T(8,128)S(1)}, u32[]{:S(2)}, u32[]{:S(2)}) collective-permute-start(f32[72,128]{1,0:T(8,128)S(1)} %get-tuple-element.31), channel_id=1, source_target_pairs={{0,4},{1,17},{2,6},{3,19},{4,0},{5,21},{6,2},{7,23},{8,12},{9,25},... | collective-permute-start | bytes 110600 | tf_op jit(solution)/shard_map/ppermute | solution.py:381
  14.6 1.9 %collective-permute-done.3 = f32[72,128]{1,0:T(8,128)S(1)} collective-permute-done((f32[72,128]{1,0:T(8,128)S(1)}, f32[72,128]{1,0:T(8,128)S(1)}, u32[]{:S(2)}, u32[]{:S(2)}) %collective-permute-start.3) | collective-permute-done | bytes 36896 | tf_op jit(solution)/shard_map/ppermute | solution.py:381
  16.6 0.2 collective-permute-start.4
  16.8 2.9 %collective-permute-start.5 = (f32[72,128]{1,0:T(8,128)S(1)}, f32[72,128]{1,0:T(8,128)S(1)}, u32[]{:S(2)}, u32[]{:S(2)}) collective-permute-start(f32[72,128]{1,0:T(8,128)S(1)} %add.18), channel_id=1, source_target_pairs={{0,8},{1,5},{2,10},{3,7},{4,12},{5,1},{6,14},{7,3},{8,0},{9,13},{1... | collective-permute-start | bytes 110600 | tf_op jit(solution)/shard_map/ppermute | solution.py:381
  19.7 1.9 %collective-permute-done.5 = f32[72,128]{1,0:T(8,128)S(1)} collective-permute-done((f32[72,128]{1,0:T(8,128)S(1)}, f32[72,128]{1,0:T(8,128)S(1)}, u32[]{:S(2)}, u32[]{:S(2)}) %collective-permute-start.5) | collective-permute-done | bytes 36896 | tf_op jit(solution)/shard_map/ppermute | solution.py:381
  21.6 3.0 %collective-permute-start.6 = (f32[72,128]{1,0:T(8,128)S(1)}, f32[72,128]{1,0:T(8,128)S(1)}, u32[]{:S(2)}, u32[]{:S(2)}) collective-permute-start(f32[72,128]{1,0:T(8,128)S(1)} %add.19), channel_id=1, source_target_pairs={{0,16},{1,9},{2,18},{3,11},{4,20},{5,13},{6,22},{7,15},{8,24},{9,1... | collective-permute-start | bytes 110600 | tf_op jit(solution)/shard_map/ppermute | solution.py:381
  24.7 0.0 collective-permute-done.4.peer_step
  24.7 1.8 %near_grams.1 = (f32[256,256]{1,0:T(8,128)S(1)}, bf16[256,2048]{1,0:T(8,128)(2,1)S(1)}, bf16[256,2048]{1,0:T(8,128)(2,1)S(1)}) custom-call(f32[2048,128]{1,0:T(8,128)S(1)} %get-tuple-element.25.wo, f32[512,128]{1,0:T(8,128)S(1)} %get-tuple-element.32.own_step, f32[512,128]{1,0:T(8,128)S(1)} %collective-permute-done.4.peer_step, f32[2048,128]{1,0:T(8,128)S(1)} %bitcast.6, ...), custom_call_target="tpu_custom_call" | custom-call | flops 2500000000 | bytes 1 | tf_op jit(solution)/shard_map/near_grams/pallas_call | solution.py:401
  26.5 0.1 collective-permute-done.6
  26.6 0.5 collective-permute-start.10
  27.1 0.0 collective-permute-start.11
  27.1 1.6 %collective-permute-start.9 = (f32[72,128]{1,0:T(8,128)S(1)}, f32[72,128]{1,0:T(8,128)S(1)}, u32[]{:S(2)}, u32[]{:S(2)}) collective-permute-start(f32[72,128]{1,0:T(8,128)S(1)} %add.20.own_msg), channel_id=1, source_target_pairs={{0,1},{1,0},{2,3},{3,2},{4,5},{5,4},{6,7},{7,6},{8,9},{9,8},{10,11... | collective-permute-start | bytes 110600 | tf_op jit(solution)/shard_map/ppermute | solution.py:46
  28.8 0.0 collective-permute-done.7.far_own.refs_2_
  28.8 0.7 %far_grams.1.far_ref = f32[256,128]{1,0:T(8,128)S(1)} custom-call(bf16[256,2048]{1,0:T(8,128)(2,1)S(1)} %get-tuple-element.35.high_t, bf16[256,2048]{1,0:T(8,128)(2,1)S(1)} %get-tuple-element.36.low_t, f32[2048,128]{1,0:T(8,128)S(1)} %collective-permute-done.7.far_own.refs_2_), custom_call_target="tpu_custom_call" | custom-call | flops 700000000 | bytes 1 | tf_op jit(solution)/shard_map/far_grams/pallas_call | solution.py:401
  29.5 0.1 collective-permute-start.8
  29.6 1.3 %collective-permute-done.10.y_msg = f32[72,128]{1,0:T(8,128)S(1)} collective-permute-done((f32[72,128]{1,0:T(8,128)S(1)}, f32[72,128]{1,0:T(8,128)S(1)}, u32[]{:S(2)}, u32[]{:S(2)}) %collective-permute-start.10) | collective-permute-done | bytes 36896 | tf_op jit(solution)/shard_map/ppermute | solution.py:46
  30.9 0.0 collective-permute-done.11.far_msg
  30.9 0.0 collective-permute-done.9.core_msg
  30.9 2.4 %first_rotation.1 = (f32[128,256]{1,0:T(8,128)S(1)}, f32[128,256]{1,0:T(8,128)S(1)}) custom-call(f32[72,128]{1,0:T(8,128)S(1)} %add.20.own_msg, f32[72,128]{1,0:T(8,128)S(1)} %collective-permute-done.9.core_msg, f32[72,128]{1,0:T(8,128)S(1)} %collective-permute-done.10.y_msg, f32[72,128]{1,0:T(8,128)S(1)} %collective-permute-done.11.far_msg), custom_call_target="tpu_custom_call" | custom-call | flops 4000000000 | bytes 1 | tf_op jit(solution)/shard_map/first_rotation/pallas_call | solution.py:401
  33.3 0.0 collective-permute-done.8.far_peer_ref
  33.3 0.5 rotated_grams.1
  33.8 0.8 %collective-permute-start.12 = (f32[72,128]{1,0:T(8,128)S(1)}, f32[72,128]{1,0:T(8,128)S(1)}, u32[]{:S(2)}, u32[]{:S(2)}) collective-permute-start(f32[72,128]{1,0:T(8,128)S(1)} %rotated_grams.1), channel_id=1, source_target_pairs={{0,4},{1,17},{2,6},{3,19},{4,0},{5,21},{6,2},{7,23},{8,12},{9,25},... | collective-permute-start | bytes 110600 | tf_op jit(solution)/shard_map/ppermute | solution.py:381
  34.6 3.2 %collective-permute-done.12 = f32[72,128]{1,0:T(8,128)S(1)} collective-permute-done((f32[72,128]{1,0:T(8,128)S(1)}, f32[72,128]{1,0:T(8,128)S(1)}, u32[]{:S(2)}, u32[]{:S(2)}) %collective-permute-start.12) | collective-permute-done | bytes 36896 | tf_op jit(solution)/shard_map/ppermute | solution.py:381
  37.8 0.3 collective-permute-start.14
  38.1 1.8 %collective-permute-start.13 = (f32[72,128]{1,0:T(8,128)S(1)}, f32[72,128]{1,0:T(8,128)S(1)}, u32[]{:S(2)}, u32[]{:S(2)}) collective-permute-start(f32[72,128]{1,0:T(8,128)S(1)} %add.21), channel_id=1, source_target_pairs={{0,8},{1,5},{2,10},{3,7},{4,12},{5,1},{6,14},{7,3},{8,0},{9,13},{1... | collective-permute-start | bytes 110600 | tf_op jit(solution)/shard_map/ppermute | solution.py:381
  39.9 2.1 %collective-permute-done.13 = f32[72,128]{1,0:T(8,128)S(1)} collective-permute-done((f32[72,128]{1,0:T(8,128)S(1)}, f32[72,128]{1,0:T(8,128)S(1)}, u32[]{:S(2)}, u32[]{:S(2)}) %collective-permute-start.13) | collective-permute-done | bytes 36896 | tf_op jit(solution)/shard_map/ppermute | solution.py:381
  42.0 2.7 %collective-permute-start.15 = (f32[72,128]{1,0:T(8,128)S(1)}, f32[72,128]{1,0:T(8,128)S(1)}, u32[]{:S(2)}, u32[]{:S(2)}) collective-permute-start(f32[72,128]{1,0:T(8,128)S(1)} %add.22), channel_id=1, source_target_pairs={{0,16},{1,9},{2,18},{3,11},{4,20},{5,13},{6,22},{7,15},{8,24},{9,1... | collective-permute-start | bytes 110600 | tf_op jit(solution)/shard_map/ppermute | solution.py:381
  44.8 0.0 collective-permute-done.14.refs_3_
  44.8 1.4 %turned_blocks.1 = (bf16[2048,256]{1,0:T(8,128)(2,1)S(1)}, bf16[2048,256]{1,0:T(8,128)(2,1)S(1)}) custom-call(f32[2048,128]{1,0:T(8,128)S(1)} %bitcast.7, f32[2048,128]{1,0:T(8,128)S(1)} %collective-permute-done.refs_1_.p_ref, f32[2048,128]{1,0:T(8,128)S(1)} %collective-permute-done.7.far_own.refs_2_, f32[2048,128]{1,0:T(8,128)S(1)} %collective-permute-done.14.refs_3_, ...), custom_call_target="tpu_custom_call" | custom-call | flops 1400000000 | bytes 1 | tf_op jit(solution)/shard_map/turned_blocks/pallas_call | solution.py:401
  46.2 0.7 %collective-permute-done.15 = f32[72,128]{1,0:T(8,128)S(1)} collective-permute-done((f32[72,128]{1,0:T(8,128)S(1)}, f32[72,128]{1,0:T(8,128)S(1)}, u32[]{:S(2)}, u32[]{:S(2)}) %collective-permute-start.15) | collective-permute-done | bytes 36896 | tf_op jit(solution)/shard_map/ppermute | solution.py:381
  46.9 0.9 %collective-permute-start.16 = (f32[72,128]{1,0:T(8,128)S(1)}, f32[72,128]{1,0:T(8,128)S(1)}, u32[]{:S(2)}, u32[]{:S(2)}) collective-permute-start(f32[72,128]{1,0:T(8,128)S(1)} %add.23.own_msg), channel_id=1, source_target_pairs={{0,2},{1,3},{2,0},{3,1},{4,6},{5,7},{6,4},{7,5},{8,10},{9,11},{10,... | collective-permute-start | bytes 110600 | tf_op jit(solution)/shard_map/ppermute | solution.py:46
  47.9 3.0 %collective-permute-done.16.y_msg = f32[72,128]{1,0:T(8,128)S(1)} collective-permute-done((f32[72,128]{1,0:T(8,128)S(1)}, f32[72,128]{1,0:T(8,128)S(1)}, u32[]{:S(2)}, u32[]{:S(2)}) %collective-permute-start.16) | collective-permute-done | bytes 36896 | tf_op jit(solution)/shard_map/ppermute | solution.py:46
  50.9 3.5 %last_rotation.1 = f32[2048,128]{1,0:T(8,128)} custom-call(f32[72,128]{1,0:T(8,128)S(1)} %add.23.own_msg, f32[72,128]{1,0:T(8,128)S(1)} %collective-permute-done.16.y_msg, bf16[2048,256]{1,0:T(8,128)(2,1)S(1)} %get-tuple-element.42.high_ref, bf16[2048,256]{1,0:T(8,128)(2,1)S(1)} %get-tuple-element.44.low_ref), custom_call_target="tpu_custom_call" | custom-call | flops 4000000000 | bytes 1 | tf_op jit(solution)/shard_map/last_rotation/pallas_call | solution.py:482
  (6 shorter events, 0.0 us)
Async XLA Ops:
  0.0 6.3 %copy-start = (f32[8,16,16,128]{3,2,1,0:T(8,128)S(1)}, f32[8,16,16,128]{3,2,1,0:T(8,128)}, u32[]{:S(2)}) copy-start(f32[8,16,16,128]{3,2,1,0:T(8,128)} %param.1) | copy-start | bytes 3145732
  0.0 6.3 %collective-permute-start = (f32[2048,128]{1,0:T(8,128)}, f32[2048,128]{1,0:T(8,128)S(1)}, u32[]{:S(2)}, u32[]{:S(2)}) collective-permute-start(f32[2048,128]{1,0:T(8,128)} %bitcast.2), channel_id=1, source_target_pairs={{0,1},{1,0},{2,3},{3,2},{4,5},{5,4},{6,7},{7,6},{8,9},{9,8},{10,11... | collective-permute-start | bytes 3145736 | tf_op jit(solution)/shard_map/ppermute | solution.py:46
  0.5 28.3 %collective-permute-start.7 = (f32[2048,128]{1,0:T(8,128)}, f32[2048,128]{1,0:T(8,128)S(1)}, u32[]{:S(2)}, u32[]{:S(2)}) collective-permute-start(f32[2048,128]{1,0:T(8,128)} %bitcast.3), channel_id=1, source_target_pairs={{0,2},{1,3},{2,0},{3,1},{4,6},{5,7},{6,4},{7,5},{8,10},{9,11},{10,... | collective-permute-start | bytes 3145736 | tf_op jit(solution)/shard_map/ppermute | solution.py:46
  4.0 5.6 %collective-permute-start.1 = (f32[256,128]{1,0:T(8,128)S(1)}, f32[256,128]{1,0:T(8,128)S(1)}, u32[]{:S(2)}, u32[]{:S(2)}) collective-permute-start(f32[256,128]{1,0:T(8,128)S(1)} %get-tuple-element.26.edge_a), channel_id=1, source_target_pairs={{0,4},{4,0},{8,12},{12,8},{16,20},{20,16},{24,28},{28,24},{1,5},{5... | collective-permute-start | bytes 393224 | tf_op jit(solution)/shard_map/ppermute | solution.py:425
  5.6 4.1 %collective-permute-start.2 = (f32[256,128]{1,0:T(8,128)S(1)}, f32[256,128]{1,0:T(8,128)S(1)}, u32[]{:S(2)}, u32[]{:S(2)}) collective-permute-start(f32[256,128]{1,0:T(8,128)S(1)} %get-tuple-element.27.edge_b), channel_id=1, source_target_pairs={{4,8},{12,16},{20,24},{8,4},{16,12},{24,20},{5,9},{13,17},{21,25},... | collective-permute-start | bytes 393224 | tf_op jit(solution)/shard_map/ppermute | solution.py:426
  10.0 6.5 %collective-permute-start.3 = (f32[72,128]{1,0:T(8,128)S(1)}, f32[72,128]{1,0:T(8,128)S(1)}, u32[]{:S(2)}, u32[]{:S(2)}) collective-permute-start(f32[72,128]{1,0:T(8,128)S(1)} %get-tuple-element.31), channel_id=1, source_target_pairs={{0,4},{1,17},{2,6},{3,19},{4,0},{5,21},{6,2},{7,23},{8,12},{9,25},... | collective-permute-start | bytes 110600 | tf_op jit(solution)/shard_map/ppermute | solution.py:381
  16.6 8.1 %collective-permute-start.4 = (f32[512,128]{1,0:T(8,128)S(1)}, f32[512,128]{1,0:T(8,128)S(1)}, u32[]{:S(2)}, u32[]{:S(2)}) collective-permute-start(f32[512,128]{1,0:T(8,128)S(1)} %get-tuple-element.32.own_step), channel_id=1, source_target_pairs={{0,1},{1,0},{2,3},{3,2},{4,5},{5,4},{6,7},{7,6},{8,9},{9,8},{10,11... | collective-permute-start | bytes 786440 | tf_op jit(solution)/shard_map/ppermute | solution.py:46
  16.8 4.9 %collective-permute-start.5 = (f32[72,128]{1,0:T(8,128)S(1)}, f32[72,128]{1,0:T(8,128)S(1)}, u32[]{:S(2)}, u32[]{:S(2)}) collective-permute-start(f32[72,128]{1,0:T(8,128)S(1)} %add.18), channel_id=1, source_target_pairs={{0,8},{1,5},{2,10},{3,7},{4,12},{5,1},{6,14},{7,3},{8,0},{9,13},{1... | collective-permute-start | bytes 110600 | tf_op jit(solution)/shard_map/ppermute | solution.py:381
  21.6 5.0 %collective-permute-start.6 = (f32[72,128]{1,0:T(8,128)S(1)}, f32[72,128]{1,0:T(8,128)S(1)}, u32[]{:S(2)}, u32[]{:S(2)}) collective-permute-start(f32[72,128]{1,0:T(8,128)S(1)} %add.19), channel_id=1, source_target_pairs={{0,16},{1,9},{2,18},{3,11},{4,20},{5,13},{6,22},{7,15},{8,24},{9,1... | collective-permute-start | bytes 110600 | tf_op jit(solution)/shard_map/ppermute | solution.py:381
  26.6 4.3 %collective-permute-start.10 = (f32[72,128]{1,0:T(8,128)S(1)}, f32[72,128]{1,0:T(8,128)S(1)}, u32[]{:S(2)}, u32[]{:S(2)}) collective-permute-start(f32[72,128]{1,0:T(8,128)S(1)} %add.20.own_msg), channel_id=1, source_target_pairs={{0,2},{1,3},{2,0},{3,1},{4,6},{5,7},{6,4},{7,5},{8,10},{9,11},{10,... | collective-permute-start | bytes 110600 | tf_op jit(solution)/shard_map/ppermute | solution.py:46
  27.1 3.8 %collective-permute-start.11 = (f32[72,128]{1,0:T(8,128)S(1)}, f32[72,128]{1,0:T(8,128)S(1)}, u32[]{:S(2)}, u32[]{:S(2)}) collective-permute-start(f32[72,128]{1,0:T(8,128)S(1)} %add.20.own_msg), channel_id=1, source_target_pairs={{0,3},{1,2},{2,1},{3,0},{4,7},{5,6},{6,5},{7,4},{8,11},{9,10},{10,... | collective-permute-start | bytes 110600 | tf_op jit(solution)/shard_map/ppermute | solution.py:46
  27.1 3.8 %collective-permute-start.9 = (f32[72,128]{1,0:T(8,128)S(1)}, f32[72,128]{1,0:T(8,128)S(1)}, u32[]{:S(2)}, u32[]{:S(2)}) collective-permute-start(f32[72,128]{1,0:T(8,128)S(1)} %add.20.own_msg), channel_id=1, source_target_pairs={{0,1},{1,0},{2,3},{3,2},{4,5},{5,4},{6,7},{7,6},{8,9},{9,8},{10,11... | collective-permute-start | bytes 110600 | tf_op jit(solution)/shard_map/ppermute | solution.py:46
  29.5 3.8 %collective-permute-start.8 = (f32[256,128]{1,0:T(8,128)S(1)}, f32[256,128]{1,0:T(8,128)S(1)}, u32[]{:S(2)}, u32[]{:S(2)}) collective-permute-start(f32[256,128]{1,0:T(8,128)S(1)} %far_grams.1.far_ref), channel_id=1, source_target_pairs={{0,1},{1,0},{2,3},{3,2},{4,5},{5,4},{6,7},{7,6},{8,9},{9,8},{10,11... | collective-permute-start | bytes 393224 | tf_op jit(solution)/shard_map/ppermute | solution.py:46
  33.8 4.0 %collective-permute-start.12 = (f32[72,128]{1,0:T(8,128)S(1)}, f32[72,128]{1,0:T(8,128)S(1)}, u32[]{:S(2)}, u32[]{:S(2)}) collective-permute-start(f32[72,128]{1,0:T(8,128)S(1)} %rotated_grams.1), channel_id=1, source_target_pairs={{0,4},{1,17},{2,6},{3,19},{4,0},{5,21},{6,2},{7,23},{8,12},{9,25},... | collective-permute-start | bytes 110600 | tf_op jit(solution)/shard_map/ppermute | solution.py:381
  37.8 7.0 %collective-permute-start.14 = (f32[2048,128]{1,0:T(8,128)S(1)}, f32[2048,128]{1,0:T(8,128)S(1)}, u32[]{:S(2)}, u32[]{:S(2)}) collective-permute-start(f32[2048,128]{1,0:T(8,128)S(1)} %collective-permute-done.7.far_own.refs_2_), channel_id=1, source_target_pairs={{0,1},{1,0},{2,3},{3,2},{4,5},{5,4},{6,7},{7,6},{8,9},{9,8},{10,11... | collective-permute-start | bytes 3145736 | tf_op jit(solution)/shard_map/ppermute | solution.py:46
  38.1 4.0 %collective-permute-start.13 = (f32[72,128]{1,0:T(8,128)S(1)}, f32[72,128]{1,0:T(8,128)S(1)}, u32[]{:S(2)}, u32[]{:S(2)}) collective-permute-start(f32[72,128]{1,0:T(8,128)S(1)} %add.21), channel_id=1, source_target_pairs={{0,8},{1,5},{2,10},{3,7},{4,12},{5,1},{6,14},{7,3},{8,0},{9,13},{1... | collective-permute-start | bytes 110600 | tf_op jit(solution)/shard_map/ppermute | solution.py:381
  42.0 4.9 %collective-permute-start.15 = (f32[72,128]{1,0:T(8,128)S(1)}, f32[72,128]{1,0:T(8,128)S(1)}, u32[]{:S(2)}, u32[]{:S(2)}) collective-permute-start(f32[72,128]{1,0:T(8,128)S(1)} %add.22), channel_id=1, source_target_pairs={{0,16},{1,9},{2,18},{3,11},{4,20},{5,13},{6,22},{7,15},{8,24},{9,1... | collective-permute-start | bytes 110600 | tf_op jit(solution)/shard_map/ppermute | solution.py:381
  46.9 4.0 %collective-permute-start.16 = (f32[72,128]{1,0:T(8,128)S(1)}, f32[72,128]{1,0:T(8,128)S(1)}, u32[]{:S(2)}, u32[]{:S(2)}) collective-permute-start(f32[72,128]{1,0:T(8,128)S(1)} %add.23.own_msg), channel_id=1, source_target_pairs={{0,2},{1,3},{2,0},{3,1},{4,6},{5,7},{6,4},{7,5},{8,10},{9,11},{10,... | collective-permute-start | bytes 110600 | tf_op jit(solution)/shard_map/ppermute | solution.py:46

commit v2 on v1

--- a/solution.py
+++ b/solution.py
@@ -364,26 +364,48 @@
     return count & (count - 1) == 0
 
 
+def summed_over(value, bits):
+    if len(bits) == 1:
+        return value + exchanged(value, "space", bits[0])
+    one, two = bits
+    near, far, both = (exchanged(value, "space", mask) for mask in (one, two, one | two))
+    return (value + near) + (far + both)
+
+
+def bits_of(count):
+    return [1 << bit for bit in range(count.bit_length() - 1)]
+
+
+def summed_but_one(value):
+    count = lax.axis_size("space")
+    if not power_of_two(count):
+        return lax.psum(value, "space"), 0
+    bits = bits_of(count)
+    if len(bits) % 2 == 0:
+        value = summed_over(value, bits[:1])
+    for k in range(1 - len(bits) % 2, len(bits) - 1, 2):
+        value = summed_over(value, bits[k:k + 2])
+    return value, bits[-1]
+
+
 def summed_over_space(value, beside_it):
-    count = lax.axis_size("space")
-    blocks = lax.axis_size("blk")
-    if not power_of_two(count):
-        value = lax.psum(value, "space")
-        beside_it([value])
+    value, bit = summed_but_one(value)
+    if bit == 0:
         return value
-    bits = [1 << bit for bit in range(count.bit_length() - 1)]
-    orders = (bits, bits[-1:] + bits[:-1])
-    sums = []
-    for step in range(len(bits)):
-        route = [
-            (i * blocks + j, (i ^ orders[j & 1][step]) * blocks + j) for i in range(count) for j in range(blocks)
-        ]
-        there = lax.ppermute(value, ("space", "blk"), route)
-        if step == len(bits) - 1:
-            value = lax.optimization_barrier((value, beside_it(sums)))[0]
-        value = value + there
-        sums.append(value)
-    return value
+    there = exchanged(value, "space", bit)
+    return lax.optimization_barrier((value, beside_it))[0] + there
+
+
+def summed_with_y(value, bit, beside_it):
+    if bit == 0:
+        return value, exchanged(value, "blk", 2)
+    count, blocks = lax.axis_size("space"), lax.axis_size("blk")
+    there = exchanged(value, "space", bit)
+    other = exchanged(value, "blk", 2)
+    route = [(i * blocks + j, (i ^ bit) * blocks + (j ^ 2)) for i in range(count) for j in range(blocks)]
+    other_there = lax.ppermute(value, ("space", "blk"), route)
+    value, other = lax.optimization_barrier((value, other, beside_it))[:2]
+    return value + there, other + other_there
 
 
 def shards(snapshots):
@@ -434,20 +456,14 @@
         edge_kernel, [edge_a, edge_b, peer, cross, diag, near_a, near_b],
         [shape_of(2 * layer, width), shape_of(half_rows, width)], [], 0.1, "edge_grams",
     )
+    peer_steps = exchanged(steps, "blk", 1)
     turned_down = jax.ShapeDtypeStruct((2 * width, cells), BF16)
-    near = []
-
-    def near_products(sums):
-        peer_steps = exchanged(lax.optimization_barrier((steps, sums[0]))[0], "blk", 1)
-        near[:] = call(
-            functools.partial(near_kernel, layer, cells_z), [image, steps, peer_steps, *chunks, peer],
-            [shape_of(2 * width, 2 * width), turned_down, turned_down], [pltpu.VMEM((cells, width), F32)],
-            2.5, "near_grams",
-        )
-        return near[0]
-
-    msg = summed_over_space(msg, near_products)
-    near_grams, high_t, low_t = near
+    near_grams, high_t, low_t = call(
+        functools.partial(near_kernel, layer, cells_z), [image, steps, peer_steps, *chunks, peer],
+        [shape_of(2 * width, 2 * width), turned_down, turned_down], [pltpu.VMEM((cells, width), F32)],
+        2.5, "near_grams",
+    )
+    msg = summed_over_space(msg, near_grams)
     core_msg, y_msg, far_msg = (exchanged(msg, "blk", mask) for mask in (1, 2, 3))
     (far_grams,) = call(
         far_kernel, [high_t, low_t, far_own], [shape_of(2 * width, width)], [], 0.7, "far_grams"
@@ -462,21 +478,15 @@
         apply_kernel, [near_grams, far_grams, far_peer_grams, own_t, far_t],
         [shape_of(half_rows, width)], [], 1.2, "rotated_grams",
     )
+    msg, last = summed_but_one(msg)
+    far_own = lax.optimization_barrier((far_own, msg))[0]
+    far_peer = exchanged(far_own, "blk", 1)
     bits = jax.ShapeDtypeStruct((cells, 2 * width), BF16)
-    turned = []
-
-    def turn_blocks(sums):
-        ready = lax.optimization_barrier((far_own, sums[0]))[0]
-        far_peer = exchanged(ready, "blk", 1)
-        turned[:] = call(
-            turn_kernel, [*chunks, peer, ready, far_peer, own_t, far_t], [bits, bits],
-            [pltpu.VMEM((2, 2 * width, 2 * width), BF16)], 1.4, "turned_blocks",
-        )
-        return turned[0]
-
-    own_msg = summed_over_space(msg, turn_blocks)
-    highs, lows = turned
-    y_msg = exchanged(own_msg, "blk", 2)
+    highs, lows = call(
+        turn_kernel, [*chunks, peer, far_own, far_peer, own_t, far_t], [bits, bits],
+        [pltpu.VMEM((2, 2 * width, 2 * width), BF16)], 1.4, "turned_blocks",
+    )
+    own_msg, y_msg = summed_with_y(msg, last, highs)
 
     step = 512
     mixed = pl.pallas_call(

time: 54.5 us -> 52.8 us (0.969)
  waiting for transfers between devices: 16.7 us -> 14.9 us
    ppermute x9 -> x17, starting transfers between devices: 6.67 us -> 19.5 us  [exchanged(): return lax.ppermute(value, axis, [(i, i ^ mask) for i in range(count)])]
    ppermute x6 -> x1, starting transfers between devices: 15.9 us -> 3.18 us  [summed_with_y(): other_there = lax.ppermute(value, ('space', 'blk'), route)]
    ppermute x6 -> x1, waiting for transfers between devices: 10.1 us -> 1.18 us  [summed_with_y(): other_there = lax.ppermute(value, ('space', 'blk'), route)]
    ppermute x9 -> x17, waiting for transfers between devices: 4.37 us -> 11.5 us  [exchanged(): return lax.ppermute(value, axis, [(i, i ^ mask) for i in range(count)])]
  transfers between devices with their start and end apart: 17 -> 20, of which waited for: 9 -> 10; matrix products, arithmetic and copies ran while one was open for 0% -> 0% of each run, Pallas kernels for 16% -> 17%
where the time goes in v2:
time: 52.8 us; the launch traced here: 52.6 us
  starting transfers between devices  24.9 us (47%)
  waiting for transfers between devices  14.9 us (28%)
  Pallas kernels  12.7 us (24%)
    ppermute x17, starting transfers between devices, exchanged(): return lax.ppermute(value, axis, [(i, i ^ mask) for i in range(count)])  19.5 us
    ppermute x17, waiting for transfers between devices, exchanged(): return lax.ppermute(value, axis, [(i, i ^ mask) for i in range(count)])  11.5 us
    pallas_call x7, Pallas kernels, call(): pl.pallas_call(body, in_specs=[VMEM] * len(inputs), out_specs=[VMEM] * le...  8.23 us
    pallas_call x1, Pallas kernels, shards(): pl.pallas_call(last_kernel, in_specs=[VMEM] * 4, out_specs=pl.BlockSpec(m...  3.45 us
    ppermute x1, starting transfers between devices, summed_with_y(): other_there = lax.ppermute(value, ('space', 'blk'), route)  3.18 us
    ppermute x1, waiting for transfers between devices, shards(): near_a = lax.ppermute(edge_a, 'space', route_a)  2.23 us
    ppermute x1, starting transfers between devices, shards(): near_a = lax.ppermute(edge_a, 'space', route_a)  1.56 us
    ppermute x1, waiting for transfers between devices, summed_with_y(): other_there = lax.ppermute(value, ('space', 'blk'), route)  1.18 us
  transfers between devices with their start and end apart: 20, of which 10 were waited for; matrix products, arithmetic and copies ran while one was open for 0% of the time, Pallas kernels for 17%

profile of v2, /device:TPU:0, one launch (start us, length us, event | category | flops | bytes accessed | tf_op | source)
XLA Modules:
  0.0 52.6 jit_solution(4190330588232482077)
XLA Ops:
  0.0 0.5 collective-permute-start
  0.5 2.6 %collective-permute-start.8 = (f32[2048,128]{1,0:T(8,128)}, f32[2048,128]{1,0:T(8,128)S(1)}, u32[]{:S(2)}, u32[]{:S(2)}) collective-permute-start(f32[2048,128]{1,0:T(8,128)} %bitcast.3), channel_id=1, source_target_pairs={{0,2},{1,3},{2,0},{3,1},{4,6},{5,7},{6,4},{7,5},{8,10},{9,11},{10,... | collective-permute-start | bytes 3145736 | tf_op jit(solution)/shard_map/ppermute | solution.py:46
  3.0 1.0 %edges.1 = (f32[256,128]{1,0:T(8,128)S(1)}, f32[256,128]{1,0:T(8,128)S(1)}) custom-call(f32[2048,128]{1,0:T(8,128)} %bitcast.4), custom_call_target="tpu_custom_call" | custom-call | flops 100000000 | bytes 1 | tf_op jit(solution)/shard_map/edges/pallas_call | solution.py:437
  4.0 1.6 %collective-permute-start.1 = (f32[256,128]{1,0:T(8,128)S(1)}, f32[256,128]{1,0:T(8,128)S(1)}, u32[]{:S(2)}, u32[]{:S(2)}) collective-permute-start(f32[256,128]{1,0:T(8,128)S(1)} %get-tuple-element.26.edge_a), channel_id=1, source_target_pairs={{0,4},{4,0},{8,12},{12,8},{16,20},{20,16},{24,28},{28,24},{1,5},{5... | collective-permute-start | bytes 393224 | tf_op jit(solution)/shard_map/ppermute | solution.py:447
  5.6 0.7 %collective-permute-start.2 = (f32[256,128]{1,0:T(8,128)S(1)}, f32[256,128]{1,0:T(8,128)S(1)}, u32[]{:S(2)}, u32[]{:S(2)}) collective-permute-start(f32[256,128]{1,0:T(8,128)S(1)} %get-tuple-element.27.edge_b), channel_id=1, source_target_pairs={{4,8},{12,16},{20,24},{8,4},{16,12},{24,20},{5,9},{13,17},{21,25},... | collective-permute-start | bytes 393224 | tf_op jit(solution)/shard_map/ppermute | solution.py:448
  6.3 0.0 collective-permute-done.refs_1_.p_ref
  6.3 1.2 %inner_grams.1 = (f32[2048,128]{1,0:T(8,128)S(1)}, f32[128,128]{1,0:T(8,128)S(1)}, f32[8,128]{1,0:T(8,128)S(1)}) custom-call(f32[2048,128]{1,0:T(8,128)S(1)} %bitcast.5, f32[2048,128]{1,0:T(8,128)S(1)} %collective-permute-done.refs_1_.p_ref), custom_call_target="tpu_custom_call" | custom-call | flops 100000000 | bytes 1 | tf_op jit(solution)/shard_map/inner_grams/pallas_call | solution.py:423
  7.4 2.2 %collective-permute-done.1.near_a = f32[256,128]{1,0:T(8,128)S(1)} collective-permute-done((f32[256,128]{1,0:T(8,128)S(1)}, f32[256,128]{1,0:T(8,128)S(1)}, u32[]{:S(2)}, u32[]{:S(2)}) %collective-permute-start.1) | collective-permute-done | bytes 131104 | tf_op jit(solution)/shard_map/ppermute | solution.py:447
  9.7 0.0 collective-permute-done.2.near_b
  9.7 0.3 edge_grams.1
  10.0 4.6 %collective-permute-start.4 = (f32[72,128]{1,0:T(8,128)S(1)}, f32[72,128]{1,0:T(8,128)S(1)}, u32[]{:S(2)}, u32[]{:S(2)}) collective-permute-start(f32[72,128]{1,0:T(8,128)S(1)} %get-tuple-element.32), channel_id=1, source_target_pairs={{0,4},{4,0},{8,12},{12,8},{16,20},{20,16},{24,28},{28,24},{1,5},{5... | collective-permute-start | bytes 110600 | tf_op jit(solution)/shard_map/ppermute | solution.py:46
  14.6 1.6 %collective-permute-start.5 = (f32[72,128]{1,0:T(8,128)S(1)}, f32[72,128]{1,0:T(8,128)S(1)}, u32[]{:S(2)}, u32[]{:S(2)}) collective-permute-start(f32[72,128]{1,0:T(8,128)S(1)} %get-tuple-element.32), channel_id=1, source_target_pairs={{0,8},{4,12},{8,0},{12,4},{16,24},{20,28},{24,16},{28,20},{1,9},{5... | collective-permute-start | bytes 110600 | tf_op jit(solution)/shard_map/ppermute | solution.py:46
  16.2 0.9 %collective-permute-start.6 = (f32[72,128]{1,0:T(8,128)S(1)}, f32[72,128]{1,0:T(8,128)S(1)}, u32[]{:S(2)}, u32[]{:S(2)}) collective-permute-start(f32[72,128]{1,0:T(8,128)S(1)} %get-tuple-element.32), channel_id=1, source_target_pairs={{0,12},{4,8},{8,4},{12,0},{16,28},{20,24},{24,20},{28,16},{1,13},{... | collective-permute-start | bytes 110600 | tf_op jit(solution)/shard_map/ppermute | solution.py:46
  17.1 0.0 collective-permute-start.3
  17.1 0.0 collective-permute-done.4
  17.1 1.8 %collective-permute-done.5 = f32[72,128]{1,0:T(8,128)S(1)} collective-permute-done((f32[72,128]{1,0:T(8,128)S(1)}, f32[72,128]{1,0:T(8,128)S(1)}, u32[]{:S(2)}, u32[]{:S(2)}) %collective-permute-start.5) | collective-permute-done | bytes 36896 | tf_op jit(solution)/shard_map/ppermute | solution.py:46
  19.0 2.1 %collective-permute-done.6 = f32[72,128]{1,0:T(8,128)S(1)} collective-permute-done((f32[72,128]{1,0:T(8,128)S(1)}, f32[72,128]{1,0:T(8,128)S(1)}, u32[]{:S(2)}, u32[]{:S(2)}) %collective-permute-start.6) | collective-permute-done | bytes 36896 | tf_op jit(solution)/shard_map/ppermute | solution.py:46
  21.1 2.2 %collective-permute-start.7 = (f32[72,128]{1,0:T(8,128)S(1)}, f32[72,128]{1,0:T(8,128)S(1)}, u32[]{:S(2)}, u32[]{:S(2)}) collective-permute-start(f32[72,128]{1,0:T(8,128)S(1)} %add_add_fusion.1), channel_id=1, source_target_pairs={{0,16},{4,20},{8,24},{12,28},{16,0},{20,4},{24,8},{28,12},{1,17},{... | collective-permute-start | bytes 110600 | tf_op jit(solution)/shard_map/ppermute | solution.py:46
  23.3 0.0 collective-permute-done.3.peer_step
  23.3 1.8 %near_grams.1 = (f32[256,256]{1,0:T(8,128)S(1)}, bf16[256,2048]{1,0:T(8,128)(2,1)S(1)}, bf16[256,2048]{1,0:T(8,128)(2,1)S(1)}) custom-call(f32[2048,128]{1,0:T(8,128)S(1)} %get-tuple-element.25.wo, f32[512,128]{1,0:T(8,128)S(1)} %get-tuple-element.30.own_step, f32[512,128]{1,0:T(8,128)S(1)} %collective-permute-done.3.peer_step, f32[2048,128]{1,0:T(8,128)S(1)} %bitcast.6, ...), custom_call_target="tpu_custom_call" | custom-call | flops 2500000000 | bytes 1 | tf_op jit(solution)/shard_map/near_grams/pallas_call | solution.py:423
  25.1 1.2 %collective-permute-done.7 = f32[72,128]{1,0:T(8,128)S(1)} collective-permute-done((f32[72,128]{1,0:T(8,128)S(1)}, f32[72,128]{1,0:T(8,128)S(1)}, u32[]{:S(2)}, u32[]{:S(2)}) %collective-permute-start.7) | collective-permute-done | bytes 36896 | tf_op jit(solution)/shard_map/ppermute | solution.py:46
  26.3 0.0 collective-permute-start.10
  26.3 0.5 %collective-permute-start.11 = (f32[72,128]{1,0:T(8,128)S(1)}, f32[72,128]{1,0:T(8,128)S(1)}, u32[]{:S(2)}, u32[]{:S(2)}) collective-permute-start(f32[72,128]{1,0:T(8,128)S(1)} %add.30.own_msg), channel_id=1, source_target_pairs={{0,2},{1,3},{2,0},{3,1},{4,6},{5,7},{6,4},{7,5},{8,10},{9,11},{10,... | collective-permute-start | bytes 110600 | tf_op jit(solution)/shard_map/ppermute | solution.py:46
  26.8 1.3 %collective-permute-start.12 = (f32[72,128]{1,0:T(8,128)S(1)}, f32[72,128]{1,0:T(8,128)S(1)}, u32[]{:S(2)}, u32[]{:S(2)}) collective-permute-start(f32[72,128]{1,0:T(8,128)S(1)} %add.30.own_msg), channel_id=1, source_target_pairs={{0,3},{1,2},{2,1},{3,0},{4,7},{5,6},{6,5},{7,4},{8,11},{9,10},{10,... | collective-permute-start | bytes 110600 | tf_op jit(solution)/shard_map/ppermute | solution.py:46
  28.1 0.0 collective-permute-done.8.far_own.refs_2_
  28.1 0.7 %far_grams.1.far_ref = f32[256,128]{1,0:T(8,128)S(1)} custom-call(bf16[256,2048]{1,0:T(8,128)(2,1)S(1)} %get-tuple-element.34.high_t, bf16[256,2048]{1,0:T(8,128)(2,1)S(1)} %get-tuple-element.35.low_t, f32[2048,128]{1,0:T(8,128)S(1)} %collective-permute-done.8.far_own.refs_2_), custom_call_target="tpu_custom_call" | custom-call | flops 700000000 | bytes 1 | tf_op jit(solution)/shard_map/far_grams/pallas_call | solution.py:423
  28.9 0.4 collective-permute-start.9
  29.3 0.0 collective-permute-done.10.core_msg
  29.3 1.3 %collective-permute-done.11.y_msg = f32[72,128]{1,0:T(8,128)S(1)} collective-permute-done((f32[72,128]{1,0:T(8,128)S(1)}, f32[72,128]{1,0:T(8,128)S(1)}, u32[]{:S(2)}, u32[]{:S(2)}) %collective-permute-start.11) | collective-permute-done | bytes 36896 | tf_op jit(solution)/shard_map/ppermute | solution.py:46
  30.6 2.4 %first_rotation.1 = (f32[128,256]{1,0:T(8,128)S(1)}, f32[128,256]{1,0:T(8,128)S(1)}) custom-call(f32[72,128]{1,0:T(8,128)S(1)} %add.30.own_msg, f32[72,128]{1,0:T(8,128)S(1)} %collective-permute-done.10.core_msg, f32[72,128]{1,0:T(8,128)S(1)} %collective-permute-done.11.y_msg, f32[72,128]{1,0:T(8,128)S(1)} %collective-permute-done.12.far_msg), custom_call_target="tpu_custom_call" | custom-call | flops 4000000000 | bytes 1 | tf_op jit(solution)/shard_map/first_rotation/pallas_call | solution.py:423
  33.0 0.0 collective-permute-done.9.far_peer_ref
  33.0 0.5 rotated_grams.1
  33.5 1.4 %collective-permute-start.13 = (f32[72,128]{1,0:T(8,128)S(1)}, f32[72,128]{1,0:T(8,128)S(1)}, u32[]{:S(2)}, u32[]{:S(2)}) collective-permute-start(f32[72,128]{1,0:T(8,128)S(1)} %rotated_grams.1), channel_id=1, source_target_pairs={{0,4},{4,0},{8,12},{12,8},{16,20},{20,16},{24,28},{28,24},{1,5},{5... | collective-permute-start | bytes 110600 | tf_op jit(solution)/shard_map/ppermute | solution.py:46
  34.8 0.1 collective-permute-start.14
  34.9 2.1 %collective-permute-start.15 = (f32[72,128]{1,0:T(8,128)S(1)}, f32[72,128]{1,0:T(8,128)S(1)}, u32[]{:S(2)}, u32[]{:S(2)}) collective-permute-start(f32[72,128]{1,0:T(8,128)S(1)} %rotated_grams.1), channel_id=1, source_target_pairs={{0,12},{4,8},{8,4},{12,0},{16,28},{20,24},{24,20},{28,16},{1,13},{... | collective-permute-start | bytes 110600 | tf_op jit(solution)/shard_map/ppermute | solution.py:46
  37.0 0.5 collective-permute-done.13
  37.5 1.3 %collective-permute-done.14 = f32[72,128]{1,0:T(8,128)S(1)} collective-permute-done((f32[72,128]{1,0:T(8,128)S(1)}, f32[72,128]{1,0:T(8,128)S(1)}, u32[]{:S(2)}, u32[]{:S(2)}) %collective-permute-start.14) | collective-permute-done | bytes 36896 | tf_op jit(solution)/shard_map/ppermute | solution.py:46
  38.8 1.0 %collective-permute-done.15 = f32[72,128]{1,0:T(8,128)S(1)} collective-permute-done((f32[72,128]{1,0:T(8,128)S(1)}, f32[72,128]{1,0:T(8,128)S(1)}, u32[]{:S(2)}, u32[]{:S(2)}) %collective-permute-start.15) | collective-permute-done | bytes 36896 | tf_op jit(solution)/shard_map/ppermute | solution.py:46
  39.8 0.1 collective-permute-start.17
  39.9 1.3 %collective-permute-start.16 = (f32[72,128]{1,0:T(8,128)S(1)}, f32[72,128]{1,0:T(8,128)S(1)}, u32[]{:S(2)}, u32[]{:S(2)}) collective-permute-start(f32[72,128]{1,0:T(8,128)S(1)} %add_add_fusion), channel_id=1, source_target_pairs={{0,2},{1,3},{2,0},{3,1},{4,6},{5,7},{6,4},{7,5},{8,10},{9,11},{10,... | collective-permute-start | bytes 110600 | tf_op jit(solution)/shard_map/ppermute | solution.py:46
  41.1 3.2 %collective-permute-start.19 = (f32[72,128]{1,0:T(8,128)S(1)}, f32[72,128]{1,0:T(8,128)S(1)}, u32[]{:S(2)}, u32[]{:S(2)}) collective-permute-start(f32[72,128]{1,0:T(8,128)S(1)} %add_add_fusion), channel_id=1, source_target_pairs={{0,18},{1,19},{2,16},{3,17},{4,22},{5,23},{6,20},{7,21},{8,26},{9,... | collective-permute-start | bytes 110600 | tf_op jit(solution)/shard_map/ppermute | solution.py:406
  44.3 0.0 collective-permute-start.18
  44.3 0.0 collective-permute-done.17.refs_3_
  44.3 1.4 %turned_blocks.1 = (bf16[2048,256]{1,0:T(8,128)(2,1)S(1)}, bf16[2048,256]{1,0:T(8,128)(2,1)S(1)}) custom-call(f32[2048,128]{1,0:T(8,128)S(1)} %bitcast.7, f32[2048,128]{1,0:T(8,128)S(1)} %collective-permute-done.refs_1_.p_ref, f32[2048,128]{1,0:T(8,128)S(1)} %collective-permute-done.8.far_own.refs_2_, f32[2048,128]{1,0:T(8,128)S(1)} %collective-permute-done.17.refs_3_, ...), custom_call_target="tpu_custom_call" | custom-call | flops 1400000000 | bytes 1 | tf_op jit(solution)/shard_map/turned_blocks/pallas_call | solution.py:423
  45.7 0.0 collective-permute-done.16
  45.7 1.2 %collective-permute-done.19 = f32[72,128]{1,0:T(8,128)S(1)} collective-permute-done((f32[72,128]{1,0:T(8,128)S(1)}, f32[72,128]{1,0:T(8,128)S(1)}, u32[]{:S(2)}, u32[]{:S(2)}) %collective-permute-start.19) | collective-permute-done | bytes 36896 | tf_op jit(solution)/shard_map/ppermute | solution.py:406
  46.9 2.3 %collective-permute-done.18 = f32[72,128]{1,0:T(8,128)S(1)} collective-permute-done((f32[72,128]{1,0:T(8,128)S(1)}, f32[72,128]{1,0:T(8,128)S(1)}, u32[]{:S(2)}, u32[]{:S(2)}) %collective-permute-start.18) | collective-permute-done | bytes 36896 | tf_op jit(solution)/shard_map/ppermute | solution.py:46
  49.2 3.5 %last_rotation.1 = f32[2048,128]{1,0:T(8,128)} custom-call(f32[72,128]{1,0:T(8,128)S(1)} %add.34.own_msg, f32[72,128]{1,0:T(8,128)S(1)} %add.35.y_msg, bf16[2048,256]{1,0:T(8,128)(2,1)S(1)} %get-tuple-element.41.high_ref, bf16[2048,256]{1,0:T(8,128)(2,1)S(1)} %get-tuple-element.44.low_ref), custom_call_target="tpu_custom_call" | custom-call | flops 4000000000 | bytes 1 | tf_op jit(solution)/shard_map/last_rotation/pallas_call | solution.py:492
  (8 shorter events, 0.0 us)
Async XLA Ops:
  0.0 6.3 %copy-start = (f32[8,16,16,128]{3,2,1,0:T(8,128)S(1)}, f32[8,16,16,128]{3,2,1,0:T(8,128)}, u32[]{:S(2)}) copy-start(f32[8,16,16,128]{3,2,1,0:T(8,128)} %param.1) | copy-start | bytes 3145732
  0.0 6.3 %collective-permute-start = (f32[2048,128]{1,0:T(8,128)}, f32[2048,128]{1,0:T(8,128)S(1)}, u32[]{:S(2)}, u32[]{:S(2)}) collective-permute-start(f32[2048,128]{1,0:T(8,128)} %bitcast.2), channel_id=1, source_target_pairs={{0,1},{1,0},{2,3},{3,2},{4,5},{5,4},{6,7},{7,6},{8,9},{9,8},{10,11... | collective-permute-start | bytes 3145736 | tf_op jit(solution)/shard_map/ppermute | solution.py:46
  0.5 27.7 %collective-permute-start.8 = (f32[2048,128]{1,0:T(8,128)}, f32[2048,128]{1,0:T(8,128)S(1)}, u32[]{:S(2)}, u32[]{:S(2)}) collective-permute-start(f32[2048,128]{1,0:T(8,128)} %bitcast.3), channel_id=1, source_target_pairs={{0,2},{1,3},{2,0},{3,1},{4,6},{5,7},{6,4},{7,5},{8,10},{9,11},{10,... | collective-permute-start | bytes 3145736 | tf_op jit(solution)/shard_map/ppermute | solution.py:46
  4.0 5.6 %collective-permute-start.1 = (f32[256,128]{1,0:T(8,128)S(1)}, f32[256,128]{1,0:T(8,128)S(1)}, u32[]{:S(2)}, u32[]{:S(2)}) collective-permute-start(f32[256,128]{1,0:T(8,128)S(1)} %get-tuple-element.26.edge_a), channel_id=1, source_target_pairs={{0,4},{4,0},{8,12},{12,8},{16,20},{20,16},{24,28},{28,24},{1,5},{5... | collective-permute-start | bytes 393224 | tf_op jit(solution)/shard_map/ppermute | solution.py:447
  5.6 4.1 %collective-permute-start.2 = (f32[256,128]{1,0:T(8,128)S(1)}, f32[256,128]{1,0:T(8,128)S(1)}, u32[]{:S(2)}, u32[]{:S(2)}) collective-permute-start(f32[256,128]{1,0:T(8,128)S(1)} %get-tuple-element.27.edge_b), channel_id=1, source_target_pairs={{4,8},{12,16},{20,24},{8,4},{16,12},{24,20},{5,9},{13,17},{21,25},... | collective-permute-start | bytes 393224 | tf_op jit(solution)/shard_map/ppermute | solution.py:448
  10.0 7.1 %collective-permute-start.4 = (f32[72,128]{1,0:T(8,128)S(1)}, f32[72,128]{1,0:T(8,128)S(1)}, u32[]{:S(2)}, u32[]{:S(2)}) collective-permute-start(f32[72,128]{1,0:T(8,128)S(1)} %get-tuple-element.32), channel_id=1, source_target_pairs={{0,4},{4,0},{8,12},{12,8},{16,20},{20,16},{24,28},{28,24},{1,5},{5... | collective-permute-start | bytes 110600 | tf_op jit(solution)/shard_map/ppermute | solution.py:46
  14.6 4.3 %collective-permute-start.5 = (f32[72,128]{1,0:T(8,128)S(1)}, f32[72,128]{1,0:T(8,128)S(1)}, u32[]{:S(2)}, u32[]{:S(2)}) collective-permute-start(f32[72,128]{1,0:T(8,128)S(1)} %get-tuple-element.32), channel_id=1, source_target_pairs={{0,8},{4,12},{8,0},{12,4},{16,24},{20,28},{24,16},{28,20},{1,9},{5... | collective-permute-start | bytes 110600 | tf_op jit(solution)/shard_map/ppermute | solution.py:46
  16.2 4.9 %collective-permute-start.6 = (f32[72,128]{1,0:T(8,128)S(1)}, f32[72,128]{1,0:T(8,128)S(1)}, u32[]{:S(2)}, u32[]{:S(2)}) collective-permute-start(f32[72,128]{1,0:T(8,128)S(1)} %get-tuple-element.32), channel_id=1, source_target_pairs={{0,12},{4,8},{8,4},{12,0},{16,28},{20,24},{24,20},{28,16},{1,13},{... | collective-permute-start | bytes 110600 | tf_op jit(solution)/shard_map/ppermute | solution.py:46
  17.1 6.1 %collective-permute-start.3 = (f32[512,128]{1,0:T(8,128)S(1)}, f32[512,128]{1,0:T(8,128)S(1)}, u32[]{:S(2)}, u32[]{:S(2)}) collective-permute-start(f32[512,128]{1,0:T(8,128)S(1)} %get-tuple-element.30.own_step), channel_id=1, source_target_pairs={{0,1},{1,0},{2,3},{3,2},{4,5},{5,4},{6,7},{7,6},{8,9},{9,8},{10,11... | collective-permute-start | bytes 786440 | tf_op jit(solution)/shard_map/ppermute | solution.py:46
  21.1 5.2 %collective-permute-start.7 = (f32[72,128]{1,0:T(8,128)S(1)}, f32[72,128]{1,0:T(8,128)S(1)}, u32[]{:S(2)}, u32[]{:S(2)}) collective-permute-start(f32[72,128]{1,0:T(8,128)S(1)} %add_add_fusion.1), channel_id=1, source_target_pairs={{0,16},{4,20},{8,24},{12,28},{16,0},{20,4},{24,8},{28,12},{1,17},{... | collective-permute-start | bytes 110600 | tf_op jit(solution)/shard_map/ppermute | solution.py:46
  26.3 3.0 %collective-permute-start.10 = (f32[72,128]{1,0:T(8,128)S(1)}, f32[72,128]{1,0:T(8,128)S(1)}, u32[]{:S(2)}, u32[]{:S(2)}) collective-permute-start(f32[72,128]{1,0:T(8,128)S(1)} %add.30.own_msg), channel_id=1, source_target_pairs={{0,1},{1,0},{2,3},{3,2},{4,5},{5,4},{6,7},{7,6},{8,9},{9,8},{10,11... | collective-permute-start | bytes 110600 | tf_op jit(solution)/shard_map/ppermute | solution.py:46
  26.3 4.3 %collective-permute-start.11 = (f32[72,128]{1,0:T(8,128)S(1)}, f32[72,128]{1,0:T(8,128)S(1)}, u32[]{:S(2)}, u32[]{:S(2)}) collective-permute-start(f32[72,128]{1,0:T(8,128)S(1)} %add.30.own_msg), channel_id=1, source_target_pairs={{0,2},{1,3},{2,0},{3,1},{4,6},{5,7},{6,4},{7,5},{8,10},{9,11},{10,... | collective-permute-start | bytes 110600 | tf_op jit(solution)/shard_map/ppermute | solution.py:46
  26.8 3.8 %collective-permute-start.12 = (f32[72,128]{1,0:T(8,128)S(1)}, f32[72,128]{1,0:T(8,128)S(1)}, u32[]{:S(2)}, u32[]{:S(2)}) collective-permute-start(f32[72,128]{1,0:T(8,128)S(1)} %add.30.own_msg), channel_id=1, source_target_pairs={{0,3},{1,2},{2,1},{3,0},{4,7},{5,6},{6,5},{7,4},{8,11},{9,10},{10,... | collective-permute-start | bytes 110600 | tf_op jit(solution)/shard_map/ppermute | solution.py:46
  28.9 4.1 %collective-permute-start.9 = (f32[256,128]{1,0:T(8,128)S(1)}, f32[256,128]{1,0:T(8,128)S(1)}, u32[]{:S(2)}, u32[]{:S(2)}) collective-permute-start(f32[256,128]{1,0:T(8,128)S(1)} %far_grams.1.far_ref), channel_id=1, source_target_pairs={{0,1},{1,0},{2,3},{3,2},{4,5},{5,4},{6,7},{7,6},{8,9},{9,8},{10,11... | collective-permute-start | bytes 393224 | tf_op jit(solution)/shard_map/ppermute | solution.py:46
  33.5 4.0 %collective-permute-start.13 = (f32[72,128]{1,0:T(8,128)S(1)}, f32[72,128]{1,0:T(8,128)S(1)}, u32[]{:S(2)}, u32[]{:S(2)}) collective-permute-start(f32[72,128]{1,0:T(8,128)S(1)} %rotated_grams.1), channel_id=1, source_target_pairs={{0,4},{4,0},{8,12},{12,8},{16,20},{20,16},{24,28},{28,24},{1,5},{5... | collective-permute-start | bytes 110600 | tf_op jit(solution)/shard_map/ppermute | solution.py:46
  34.8 4.0 %collective-permute-start.14 = (f32[72,128]{1,0:T(8,128)S(1)}, f32[72,128]{1,0:T(8,128)S(1)}, u32[]{:S(2)}, u32[]{:S(2)}) collective-permute-start(f32[72,128]{1,0:T(8,128)S(1)} %rotated_grams.1), channel_id=1, source_target_pairs={{0,8},{4,12},{8,0},{12,4},{16,24},{20,28},{24,16},{28,20},{1,9},{5... | collective-permute-start | bytes 110600 | tf_op jit(solution)/shard_map/ppermute | solution.py:46
  34.9 4.9 %collective-permute-start.15 = (f32[72,128]{1,0:T(8,128)S(1)}, f32[72,128]{1,0:T(8,128)S(1)}, u32[]{:S(2)}, u32[]{:S(2)}) collective-permute-start(f32[72,128]{1,0:T(8,128)S(1)} %rotated_grams.1), channel_id=1, source_target_pairs={{0,12},{4,8},{8,4},{12,0},{16,28},{20,24},{24,20},{28,16},{1,13},{... | collective-permute-start | bytes 110600 | tf_op jit(solution)/shard_map/ppermute | solution.py:46
  39.8 4.5 %collective-permute-start.17 = (f32[2048,128]{1,0:T(8,128)S(1)}, f32[2048,128]{1,0:T(8,128)S(1)}, u32[]{:S(2)}, u32[]{:S(2)}) collective-permute-start(f32[2048,128]{1,0:T(8,128)S(1)} %collective-permute-done.8.far_own.refs_2_), channel_id=1, source_target_pairs={{0,1},{1,0},{2,3},{3,2},{4,5},{5,4},{6,7},{7,6},{8,9},{9,8},{10,11... | collective-permute-start | bytes 3145736 | tf_op jit(solution)/shard_map/ppermute | solution.py:46
  39.9 5.8 %collective-permute-start.16 = (f32[72,128]{1,0:T(8,128)S(1)}, f32[72,128]{1,0:T(8,128)S(1)}, u32[]{:S(2)}, u32[]{:S(2)}) collective-permute-start(f32[72,128]{1,0:T(8,128)S(1)} %add_add_fusion), channel_id=1, source_target_pairs={{0,2},{1,3},{2,0},{3,1},{4,6},{5,7},{6,4},{7,5},{8,10},{9,11},{10,... | collective-permute-start | bytes 110600 | tf_op jit(solution)/shard_map/ppermute | solution.py:46
  41.1 5.8 %collective-permute-start.19 = (f32[72,128]{1,0:T(8,128)S(1)}, f32[72,128]{1,0:T(8,128)S(1)}, u32[]{:S(2)}, u32[]{:S(2)}) collective-permute-start(f32[72,128]{1,0:T(8,128)S(1)} %add_add_fusion), channel_id=1, source_target_pairs={{0,18},{1,19},{2,16},{3,17},{4,22},{5,23},{6,20},{7,21},{8,26},{9,... | collective-permute-start | bytes 110600 | tf_op jit(solution)/shard_map/ppermute | solution.py:406
  44.3 4.9 %collective-permute-start.18 = (f32[72,128]{1,0:T(8,128)S(1)}, f32[72,128]{1,0:T(8,128)S(1)}, u32[]{:S(2)}, u32[]{:S(2)}) collective-permute-start(f32[72,128]{1,0:T(8,128)S(1)} %add_add_fusion), channel_id=1, source_target_pairs={{0,16},{4,20},{8,24},{12,28},{16,0},{20,4},{24,8},{28,12},{1,17},{... | collective-permute-start | bytes 110600 | tf_op jit(solution)/shard_map/ppermute | solution.py:46

commit v3 on v2

--- a/solution.py
+++ b/solution.py
@@ -11,7 +11,7 @@
 BF16 = jnp.bfloat16
 VMEM = pl.BlockSpec(memory_space=pltpu.VMEM)
 PARAMS = pltpu.CompilerParams(vmem_limit_bytes=40 * 2**20)
-CLOSE = 5e-4
+CLOSE = 2e-3
 STEPS = 5
 CHUNKS = 1
 
@@ -137,7 +137,7 @@
     d_ref[...] = diag
 
 
-def edge_kernel(edge_a, edge_b, p_ref, c_ref, d_ref, near_a, near_b, step_ref, msg_ref):
+def edge_kernel(edge_a, edge_b, p_ref, c_ref, d_ref, near_b, near_a, step_ref, msg_ref):
     layer, width = edge_a.shape
     layers = p_ref.shape[0] // layer
     half = width // 2
@@ -226,20 +226,24 @@
     return jnp.where(row == col, 1.0, 0.0).astype(F32)
 
 
-def rotations(pairs, high, x_ref):
+def rotations(pairs, high, x_ref, finish):
     width = pairs[0][0].shape[1]
     half = width // 2
     eye = eye_of(width)
+    sign = jnp.where(high, 2.0, -2.0)
     ratios, normals = [], []
     for own, other in pairs:
         cross = jnp.concatenate(
             [jnp.where(high, other[:half], own[:half]), jnp.where(high, own[:half], other[:half])], axis=0
         )
-        cross = jnp.where(high, cross.T, cross)
-        rows = jnp.broadcast_to(own[half:half + 1], (width, width)).T
-        ratio = cross / (rows + other[half:half + 1])
+        cross_t = cross.T
+        own_diag, other_diag = own[half:half + 1], other[half:half + 1]
+        own_rows = jnp.broadcast_to(own_diag, (width, width)).T
+        other_rows = jnp.broadcast_to(other_diag, (width, width)).T
+        ratio = jnp.where(high, cross_t, cross) / (own_rows + other_diag)
+        ratio_t = jnp.where(high, cross, cross_t) / (other_rows + own_diag)
         ratios.append(ratio)
-        normals.append(eye + product(ratio, ratio.T))
+        normals.append(eye + product(ratio, ratio_t))
     bound = jnp.max(jnp.sum(jnp.abs(normals[0]), axis=0, keepdims=True), axis=1, keepdims=True)
     for normal in normals[1:]:
         size = jnp.max(jnp.sum(jnp.abs(normal), axis=0, keepdims=True), axis=1, keepdims=True)
@@ -260,41 +264,36 @@
     for _ in range(STEPS - 1):
         err, fresh = next_of(err)
         boths = [product_3(fresh * (2.0 * eye - both[:, width:]), both) for both in boths]
-    for k, both in enumerate(boths):
-        x_ref[k] = both
-
-    def step(err):
-        err, fresh = next_of(err)
-        for k in range(len(pairs)):
-            both = x_ref[k]
-            x_ref[k] = product_3(fresh * (2.0 * eye - both[:, width:]), both)
-        return err
-
-    lax.while_loop(lambda err: err > CLOSE, step, jnp.max(err))
-
-    def refine(_=None):
+
+    def refined(inverses):
         size = 0.0
-        for k, (ratio, normal) in enumerate(zip(ratios, normals)):
-            inverse = x_ref[k, :, :width]
+        turns = []
+        for k, (inverse, ratio, normal) in enumerate(zip(inverses, ratios, normals)):
             left_over = eye - product(inverse, normal)
             both = jnp.concatenate([inverse, product(inverse, ratio)], axis=1)
-            x_ref[k] = both + product_3(left_over, both)
+            both = both + product_3(left_over, both)
+            x_ref[k] = both[:, :width]
+            turns.append((2.0 * both[:, :width] - eye, sign * both[:, width:]))
             size = jnp.maximum(size, jnp.max(jnp.sum(jnp.abs(left_over), axis=0)))
+        finish(turns)
         return size
 
-    lax.while_loop(lambda size: size > CLOSE, refine, refine())
-    sign = jnp.where(high, 2.0, -2.0)
-    return [
-        (2.0 * x_ref[k, :, :width] - eye, sign * x_ref[k, :, width:]) for k in range(len(pairs))
-    ]
-
-
-def first_kernel(own_msg, core_msg, y_msg, far_msg, own_t, far_t, x_ref):
+    size = refined([both[:, :width] for both in boths])
+    lax.while_loop(
+        lambda size: size > CLOSE, lambda _: refined([x_ref[k] for k in range(len(pairs))]), size
+    )
+
+
+def first_kernel(far_msg, y_msg, core_msg, own_msg, own_t, far_t, x_ref):
     width = own_msg.shape[1]
+
+    def finish(turns):
+        for (keep, take), out in zip(turns, (own_t, far_t)):
+            out[:, :width] = keep
+            out[:, width:] = take
+
     pairs = [(own_msg[...], core_msg[...]), (y_msg[...], far_msg[...])]
-    for (keep, take), out in zip(rotations(pairs, place()[0] == 1, x_ref), (own_t, far_t)):
-        out[:, :width] = keep
-        out[:, width:] = take
+    rotations(pairs, place()[0] == 1, x_ref, finish)
 
 
 def apply_kernel(near_ref, far_ref, far_peer_ref, own_t, far_t, msg_ref):
@@ -347,65 +346,70 @@
 
 def last_kernel(own_msg, y_msg, high_ref, low_ref, out, x_ref, m_ref, o_ref, sems):
     width = own_msg.shape[1]
-    ((keep, take),) = rotations([(own_msg[...], y_msg[...])], place()[4] == 1, x_ref)
-    m_ref[:, :width], m_ref[:, width:] = halves(jnp.concatenate([keep, take.T], axis=0))
     step = o_ref.shape[1]
-    copies = []
-    for k in range(o_ref.shape[0]):
-        rows = slice(k * step, (k + 1) * step)
-        o_ref[k] = wide_product(high_ref[rows, :], low_ref[rows, :], m_ref)
-        copies.append(pltpu.make_async_copy(o_ref.at[k], out.at[pl.ds(k * step, step)], sems.at[k]))
-        copies[-1].start()
-    for copy in copies:
-        copy.wait()
+
+    def finish(turns):
+        keep, take = turns[0]
+        m_ref[:, :width], m_ref[:, width:] = halves(jnp.concatenate([keep, take.T], axis=0))
+        copies = []
+        for k in range(o_ref.shape[0]):
+            rows = slice(k * step, (k + 1) * step)
+            o_ref[k] = wide_product(high_ref[rows, :], low_ref[rows, :], m_ref)
+            copies.append(pltpu.make_async_copy(o_ref.at[k], out.at[pl.ds(k * step, step)], sems.at[k]))
+            copies[-1].start()
+        for copy in copies:
+            copy.wait()
+
+    rotations([(own_msg[...], y_msg[...])], place()[4] == 1, x_ref, finish)
 
 
 def power_of_two(count):
     return count & (count - 1) == 0
 
 
-def summed_over(value, bits):
-    if len(bits) == 1:
-        return value + exchanged(value, "space", bits[0])
-    one, two = bits
-    near, far, both = (exchanged(value, "space", mask) for mask in (one, two, one | two))
-    return (value + near) + (far + both)
-
-
-def bits_of(count):
-    return [1 << bit for bit in range(count.bit_length() - 1)]
-
-
-def summed_but_one(value):
+def stages_of(count):
+    bits = [1 << bit for bit in range(count.bit_length() - 1)]
+    pairs = [tuple(bits[k:k + 2]) for k in range(0, len(bits) - 1, 2)]
+    if len(bits) % 2 == 0:
+        pairs[-1:] = [pairs[-1][:1]]
+    return pairs + [(bits[-1],)]
+
+
+def summed_over(value, stages):
+    for bits in stages:
+        if len(bits) == 1:
+            value = value + exchanged(value, "space", bits[0])
+        else:
+            one, two = bits
+            both, far, near = (exchanged(value, "space", mask) for mask in (one | two, two, one))
+            value = (both + far) + (near + value)
+    return value
+
+
+def summed_over_space(value, beside_it):
     count = lax.axis_size("space")
     if not power_of_two(count):
-        return lax.psum(value, "space"), 0
-    bits = bits_of(count)
-    if len(bits) % 2 == 0:
-        value = summed_over(value, bits[:1])
-    for k in range(1 - len(bits) % 2, len(bits) - 1, 2):
-        value = summed_over(value, bits[k:k + 2])
-    return value, bits[-1]
-
-
-def summed_over_space(value, beside_it):
-    value, bit = summed_but_one(value)
-    if bit == 0:
-        return value
-    there = exchanged(value, "space", bit)
+        return lax.psum(value, "space")
+    stages = stages_of(count)
+    value = summed_over(value, stages[:-1])
+    there = exchanged(value, "space", stages[-1][0])
     return lax.optimization_barrier((value, beside_it))[0] + there
 
 
-def summed_with_y(value, bit, beside_it):
-    if bit == 0:
+def summed_with_y(value, beside_it):
+    count, blocks = lax.axis_size("space"), lax.axis_size("blk")
+    if not power_of_two(count):
+        value = lax.psum(value, "space")
         return value, exchanged(value, "blk", 2)
-    count, blocks = lax.axis_size("space"), lax.axis_size("blk")
+    stages = stages_of(count)
+    value = summed_over(value, stages[:-1])
+    bit = stages[-1][0]
+    route = [(i * blocks + j, (i ^ bit) * blocks + (j ^ 2)) for i in range(count) for j in range(blocks)]
+    other_there = lax.ppermute(value, ("space", "blk"), route)
     there = exchanged(value, "space", bit)
     other = exchanged(value, "blk", 2)
-    route = [(i * blocks + j, (i ^ bit) * blocks + (j ^ 2)) for i in range(count) for j in range(blocks)]
-    other_there = lax.ppermute(value, ("space", "blk"), route)
-    value, other = lax.optimization_barrier((value, other, beside_it))[:2]
-    return value + there, other + other_there
+    other_there, there, other = lax.optimization_barrier((other_there, there, other, beside_it))[:3]
+    return value + there, other_there + other
 
 
 def shards(snapshots):
@@ -453,7 +457,7 @@
         [shape_of(cells, width), shape_of(width, width), shape_of(8, width)], [], 0.1, "inner_grams",
     )
     steps, msg = call(
-        edge_kernel, [edge_a, edge_b, peer, cross, diag, near_a, near_b],
+        edge_kernel, [edge_a, edge_b, peer, cross, diag, near_b, near_a],
         [shape_of(2 * layer, width), shape_of(half_rows, width)], [], 0.1, "edge_grams",
     )
     peer_steps = exchanged(steps, "blk", 1)
@@ -464,21 +468,20 @@
         2.5, "near_grams",
     )
     msg = summed_over_space(msg, near_grams)
-    core_msg, y_msg, far_msg = (exchanged(msg, "blk", mask) for mask in (1, 2, 3))
+    far_msg, y_msg, core_msg = (exchanged(msg, "blk", mask) for mask in (3, 2, 1))
     (far_grams,) = call(
         far_kernel, [high_t, low_t, far_own], [shape_of(2 * width, width)], [], 0.7, "far_grams"
     )
     far_peer_grams = exchanged(far_grams, "blk", 1)
     msg, far_grams = lax.optimization_barrier((msg, far_grams))
     own_t, far_t = call(
-        first_kernel, [msg, core_msg, y_msg, far_msg], [shape_of(width, 2 * width)] * 2,
-        [pltpu.VMEM((2, width, 2 * width), F32)], 4, "first_rotation",
+        first_kernel, [far_msg, y_msg, core_msg, msg], [shape_of(width, 2 * width)] * 2,
+        [pltpu.VMEM((2, width, width), F32)], 4, "first_rotation",
     )
     (msg,) = call(
         apply_kernel, [near_grams, far_grams, far_peer_grams, own_t, far_t],
         [shape_of(half_rows, width)], [], 1.2, "rotated_grams",
     )
-    msg, last = summed_but_one(msg)
     far_own = lax.optimization_barrier((far_own, msg))[0]
     far_peer = exchanged(far_own, "blk", 1)
     bits = jax.ShapeDtypeStruct((cells, 2 * width), BF16)
@@ -486,7 +489,7 @@
         turn_kernel, [*chunks, peer, far_own, far_peer, own_t, far_t], [bits, bits],
         [pltpu.VMEM((2, 2 * width, 2 * width), BF16)], 1.4, "turned_blocks",
     )
-    own_msg, y_msg = summed_with_y(msg, last, highs)
+    own_msg, y_msg = summed_with_y(msg, highs)
 
     step = 512
     mixed = pl.pallas_call(
@@ -495,7 +498,7 @@
         out_specs=pl.BlockSpec(memory_space=pl.ANY),
         out_shape=shape_of(cells, width),
         scratch_shapes=[
-            pltpu.VMEM((1, width, 2 * width), F32),
+            pltpu.VMEM((1, width, width), F32),
             pltpu.VMEM((2 * width, 2 * width), BF16),
             pltpu.VMEM((cells // step, step, width), F32),
             pltpu.SemaphoreType.DMA((cells // step,)),

time: 52.8 us -> 51.5 us (0.975)
  waiting for transfers between devices: 14.9 us -> 14 us
    ppermute x1, starting transfers between devices: 1.56 us -> 4.34 us  [shards(): near_a = lax.ppermute(edge_a, 'space', route_a)]
    ppermute x17, starting transfers between devices: 19.5 us -> 16.8 us  [exchanged(): return lax.ppermute(value, axis, [(i, i ^ mask) for i in range(count)])]
    ppermute x1, waiting for transfers between devices: 2.23 us -> 3.98 us  [shards(): near_a = lax.ppermute(edge_a, 'space', route_a)]
    ppermute x17, waiting for transfers between devices: 11.5 us -> 9.99 us  [exchanged(): return lax.ppermute(value, axis, [(i, i ^ mask) for i in range(count)])]
    ppermute x1, waiting for transfers between devices: 1.18 us -> 0.01 us  [summed_with_y(): other_there = lax.ppermute(value, ('space', 'blk'), route)]
  transfers between devices with their start and end apart: 20 -> 20, of which waited for: 10 -> 11; matrix products, arithmetic and copies ran while one was open for 0% -> 0% of each run, Pallas kernels for 17% -> 17%
where the time goes in v3:
time: 51.5 us; the launch traced here: 51.4 us
  starting transfers between devices  24.9 us (48%)
  waiting for transfers between devices  14 us (27%)
  Pallas kernels  12.3 us (24%)
    ppermute x17, starting transfers between devices, exchanged(): return lax.ppermute(value, axis, [(i, i ^ mask) for i in range(count)])  16.8 us
    ppermute x17, waiting for transfers between devices, exchanged(): return lax.ppermute(value, axis, [(i, i ^ mask) for i in range(count)])  9.99 us
    pallas_call x7, Pallas kernels, call(): pl.pallas_call(body, in_specs=[VMEM] * len(inputs), out_specs=[VMEM] * le...  7.99 us
    ppermute x1, starting transfers between devices, shards(): near_a = lax.ppermute(edge_a, 'space', route_a)  4.34 us
    ppermute x1, waiting for transfers between devices, shards(): near_a = lax.ppermute(edge_a, 'space', route_a)  3.98 us
    pallas_call x1, Pallas kernels, shards(): pl.pallas_call(last_kernel, in_specs=[VMEM] * 4, out_specs=pl.BlockSpec(m...  3.31 us
    ppermute x1, starting transfers between devices, summed_with_y(): other_there = lax.ppermute(value, ('space', 'blk'), route)  3.13 us
  transfers between devices with their start and end apart: 20, of which 11 were waited for; matrix products, arithmetic and copies ran while one was open for 0% of the time, Pallas kernels for 17%

profile of v3, /device:TPU:0, one launch (start us, length us, event | category | flops | bytes accessed | tf_op | source)
XLA Modules:
  0.0 51.4 jit_solution(212654986320156035)
XLA Ops:
  0.0 0.5 collective-permute-start
  0.5 2.6 %collective-permute-start.8 = (f32[2048,128]{1,0:T(8,128)}, f32[2048,128]{1,0:T(8,128)S(1)}, u32[]{:S(2)}, u32[]{:S(2)}) collective-permute-start(f32[2048,128]{1,0:T(8,128)} %bitcast.3), channel_id=1, source_target_pairs={{0,2},{1,3},{2,0},{3,1},{4,6},{5,7},{6,4},{7,5},{8,10},{9,11},{10,... | collective-permute-start | bytes 3145736 | tf_op jit(solution)/shard_map/ppermute | solution.py:46
  3.0 1.0 %edges.1 = (f32[256,128]{1,0:T(8,128)S(1)}, f32[256,128]{1,0:T(8,128)S(1)}) custom-call(f32[2048,128]{1,0:T(8,128)} %bitcast.4), custom_call_target="tpu_custom_call" | custom-call | flops 100000000 | bytes 1 | tf_op jit(solution)/shard_map/edges/pallas_call | solution.py:441
  4.0 0.7 %collective-permute-start.1 = (f32[256,128]{1,0:T(8,128)S(1)}, f32[256,128]{1,0:T(8,128)S(1)}, u32[]{:S(2)}, u32[]{:S(2)}) collective-permute-start(f32[256,128]{1,0:T(8,128)S(1)} %get-tuple-element.28.edge_b), channel_id=1, source_target_pairs={{4,8},{12,16},{20,24},{8,4},{16,12},{24,20},{5,9},{13,17},{21,25},... | collective-permute-start | bytes 393224 | tf_op jit(solution)/shard_map/ppermute | solution.py:452
  4.7 4.3 %collective-permute-start.2 = (f32[256,128]{1,0:T(8,128)S(1)}, f32[256,128]{1,0:T(8,128)S(1)}, u32[]{:S(2)}, u32[]{:S(2)}) collective-permute-start(f32[256,128]{1,0:T(8,128)S(1)} %get-tuple-element.27.edge_a), channel_id=1, source_target_pairs={{0,4},{4,0},{8,12},{12,8},{16,20},{20,16},{24,28},{28,24},{1,5},{5... | collective-permute-start | bytes 393224 | tf_op jit(solution)/shard_map/ppermute | solution.py:451
  9.1 0.0 collective-permute-done.refs_1_.p_ref
  9.1 1.2 %inner_grams.1 = (f32[2048,128]{1,0:T(8,128)S(1)}, f32[128,128]{1,0:T(8,128)S(1)}, f32[8,128]{1,0:T(8,128)S(1)}) custom-call(f32[2048,128]{1,0:T(8,128)S(1)} %bitcast.5, f32[2048,128]{1,0:T(8,128)S(1)} %collective-permute-done.refs_1_.p_ref), custom_call_target="tpu_custom_call" | custom-call | flops 100000000 | bytes 1 | tf_op jit(solution)/shard_map/inner_grams/pallas_call | solution.py:427
  10.2 0.0 collective-permute-done.1.near_b
  10.2 4.0 %collective-permute-done.2.near_a = f32[256,128]{1,0:T(8,128)S(1)} collective-permute-done((f32[256,128]{1,0:T(8,128)S(1)}, f32[256,128]{1,0:T(8,128)S(1)}, u32[]{:S(2)}, u32[]{:S(2)}) %collective-permute-start.2) | collective-permute-done | bytes 131104 | tf_op jit(solution)/shard_map/ppermute | solution.py:451
  14.2 0.3 edge_grams.1
  14.6 3.6 %collective-permute-start.4 = (f32[72,128]{1,0:T(8,128)S(1)}, f32[72,128]{1,0:T(8,128)S(1)}, u32[]{:S(2)}, u32[]{:S(2)}) collective-permute-start(f32[72,128]{1,0:T(8,128)S(1)} %get-tuple-element.33), channel_id=1, source_target_pairs={{0,12},{4,8},{8,4},{12,0},{16,28},{20,24},{24,20},{28,16},{1,13},{... | collective-permute-start | bytes 110600 | tf_op jit(solution)/shard_map/ppermute | solution.py:46
  18.1 0.4 collective-permute-start.5
  18.6 0.2 collective-permute-start.6
  18.8 0.0 collective-permute-start.3
  18.8 1.3 %collective-permute-done.4 = f32[72,128]{1,0:T(8,128)S(1)} collective-permute-done((f32[72,128]{1,0:T(8,128)S(1)}, f32[72,128]{1,0:T(8,128)S(1)}, u32[]{:S(2)}, u32[]{:S(2)}) %collective-permute-start.4) | collective-permute-done | bytes 36896 | tf_op jit(solution)/shard_map/ppermute | solution.py:46
  20.1 2.0 %collective-permute-done.5 = f32[72,128]{1,0:T(8,128)S(1)} collective-permute-done((f32[72,128]{1,0:T(8,128)S(1)}, f32[72,128]{1,0:T(8,128)S(1)}, u32[]{:S(2)}, u32[]{:S(2)}) %collective-permute-start.5) | collective-permute-done | bytes 36896 | tf_op jit(solution)/shard_map/ppermute | solution.py:46
  22.1 0.4 collective-permute-done.6
  22.5 2.7 %collective-permute-start.7 = (f32[72,128]{1,0:T(8,128)S(1)}, f32[72,128]{1,0:T(8,128)S(1)}, u32[]{:S(2)}, u32[]{:S(2)}) collective-permute-start(f32[72,128]{1,0:T(8,128)S(1)} %add_add_fusion.1), channel_id=1, source_target_pairs={{0,16},{4,20},{8,24},{12,28},{16,0},{20,4},{24,8},{28,12},{1,17},{... | collective-permute-start | bytes 110600 | tf_op jit(solution)/shard_map/ppermute | solution.py:46
  25.2 0.0 collective-permute-done.3.peer_step
  25.2 1.8 %near_grams.1 = (f32[256,256]{1,0:T(8,128)S(1)}, bf16[256,2048]{1,0:T(8,128)(2,1)S(1)}, bf16[256,2048]{1,0:T(8,128)(2,1)S(1)}) custom-call(f32[2048,128]{1,0:T(8,128)S(1)} %get-tuple-element.26.wo, f32[512,128]{1,0:T(8,128)S(1)} %get-tuple-element.31.own_step, f32[512,128]{1,0:T(8,128)S(1)} %collective-permute-done.3.peer_step, f32[2048,128]{1,0:T(8,128)S(1)} %bitcast.6, ...), custom_call_target="tpu_custom_call" | custom-call | flops 2500000000 | bytes 1 | tf_op jit(solution)/shard_map/near_grams/pallas_call | solution.py:427
  27.0 0.4 collective-permute-done.7
  27.5 0.0 collective-permute-start.10
  27.5 0.6 %collective-permute-start.11 = (f32[72,128]{1,0:T(8,128)S(1)}, f32[72,128]{1,0:T(8,128)S(1)}, u32[]{:S(2)}, u32[]{:S(2)}) collective-permute-start(f32[72,128]{1,0:T(8,128)S(1)} %add.30.own_msg), channel_id=1, source_target_pairs={{0,2},{1,3},{2,0},{3,1},{4,6},{5,7},{6,4},{7,5},{8,10},{9,11},{10,... | collective-permute-start | bytes 110600 | tf_op jit(solution)/shard_map/ppermute | solution.py:46
  28.1 1.3 %collective-permute-start.12 = (f32[72,128]{1,0:T(8,128)S(1)}, f32[72,128]{1,0:T(8,128)S(1)}, u32[]{:S(2)}, u32[]{:S(2)}) collective-permute-start(f32[72,128]{1,0:T(8,128)S(1)} %add.30.own_msg), channel_id=1, source_target_pairs={{0,1},{1,0},{2,3},{3,2},{4,5},{5,4},{6,7},{7,6},{8,9},{9,8},{10,11... | collective-permute-start | bytes 110600 | tf_op jit(solution)/shard_map/ppermute | solution.py:46
  29.3 0.0 collective-permute-done.8.far_own.refs_2_
  29.3 0.7 %far_grams.1.far_ref = f32[256,128]{1,0:T(8,128)S(1)} custom-call(bf16[256,2048]{1,0:T(8,128)(2,1)S(1)} %get-tuple-element.35.high_t, bf16[256,2048]{1,0:T(8,128)(2,1)S(1)} %get-tuple-element.36.low_t, f32[2048,128]{1,0:T(8,128)S(1)} %collective-permute-done.8.far_own.refs_2_), custom_call_target="tpu_custom_call" | custom-call | flops 700000000 | bytes 1 | tf_op jit(solution)/shard_map/far_grams/pallas_call | solution.py:427
  30.1 0.1 collective-permute-start.9
  30.1 0.7 %collective-permute-done.10.far_msg = f32[72,128]{1,0:T(8,128)S(1)} collective-permute-done((f32[72,128]{1,0:T(8,128)S(1)}, f32[72,128]{1,0:T(8,128)S(1)}, u32[]{:S(2)}, u32[]{:S(2)}) %collective-permute-start.10) | collective-permute-done | bytes 36896 | tf_op jit(solution)/shard_map/ppermute | solution.py:46
  30.9 0.8 %collective-permute-done.11.y_msg = f32[72,128]{1,0:T(8,128)S(1)} collective-permute-done((f32[72,128]{1,0:T(8,128)S(1)}, f32[72,128]{1,0:T(8,128)S(1)}, u32[]{:S(2)}, u32[]{:S(2)}) %collective-permute-start.11) | collective-permute-done | bytes 36896 | tf_op jit(solution)/shard_map/ppermute | solution.py:46
  31.7 0.0 collective-permute-done.12.core_msg
  31.7 2.1 %first_rotation.1 = (f32[128,256]{1,0:T(8,128)S(1)}, f32[128,256]{1,0:T(8,128)S(1)}) custom-call(f32[72,128]{1,0:T(8,128)S(1)} %collective-permute-done.10.far_msg, f32[72,128]{1,0:T(8,128)S(1)} %collective-permute-done.11.y_msg, f32[72,128]{1,0:T(8,128)S(1)} %collective-permute-done.12.core_msg, f32[72,128]{1,0:T(8,128)S(1)} %add.30.own_msg), custom_call_target="tpu_custom_call" | custom-call | flops 4000000000 | bytes 1 | tf_op jit(solution)/shard_map/first_rotation/pallas_call | solution.py:427
  33.8 0.0 collective-permute-done.9.far_peer_ref
  33.8 0.5 rotated_grams.1
  34.2 0.1 collective-permute-start.19
  34.3 1.6 %collective-permute-start.13 = (f32[72,128]{1,0:T(8,128)S(1)}, f32[72,128]{1,0:T(8,128)S(1)}, u32[]{:S(2)}, u32[]{:S(2)}) collective-permute-start(f32[72,128]{1,0:T(8,128)S(1)} %rotated_grams.1), channel_id=1, source_target_pairs={{0,12},{4,8},{8,4},{12,0},{16,28},{20,24},{24,20},{28,16},{1,13},{... | collective-permute-start | bytes 110600 | tf_op jit(solution)/shard_map/ppermute | solution.py:46
  35.9 0.1 collective-permute-start.14
  36.1 1.8 %collective-permute-start.15 = (f32[72,128]{1,0:T(8,128)S(1)}, f32[72,128]{1,0:T(8,128)S(1)}, u32[]{:S(2)}, u32[]{:S(2)}) collective-permute-start(f32[72,128]{1,0:T(8,128)S(1)} %rotated_grams.1), channel_id=1, source_target_pairs={{0,4},{4,0},{8,12},{12,8},{16,20},{20,16},{24,28},{28,24},{1,5},{5... | collective-permute-start | bytes 110600 | tf_op jit(solution)/shard_map/ppermute | solution.py:46
  37.9 1.5 %collective-permute-done.13 = f32[72,128]{1,0:T(8,128)S(1)} collective-permute-done((f32[72,128]{1,0:T(8,128)S(1)}, f32[72,128]{1,0:T(8,128)S(1)}, u32[]{:S(2)}, u32[]{:S(2)}) %collective-permute-start.13) | collective-permute-done | bytes 36896 | tf_op jit(solution)/shard_map/ppermute | solution.py:46
  39.4 0.5 %collective-permute-done.14 = f32[72,128]{1,0:T(8,128)S(1)} collective-permute-done((f32[72,128]{1,0:T(8,128)S(1)}, f32[72,128]{1,0:T(8,128)S(1)}, u32[]{:S(2)}, u32[]{:S(2)}) %collective-permute-start.14) | collective-permute-done | bytes 36896 | tf_op jit(solution)/shard_map/ppermute | solution.py:46
  39.9 0.1 collective-permute-done.15
  40.0 3.1 %collective-permute-start.16 = (f32[72,128]{1,0:T(8,128)S(1)}, f32[72,128]{1,0:T(8,128)S(1)}, u32[]{:S(2)}, u32[]{:S(2)}) collective-permute-start(f32[72,128]{1,0:T(8,128)S(1)} %add_add_fusion), channel_id=1, source_target_pairs={{0,18},{1,19},{2,16},{3,17},{4,22},{5,23},{6,20},{7,21},{8,26},{9,... | collective-permute-start | bytes 110600 | tf_op jit(solution)/shard_map/ppermute | solution.py:408
  43.2 0.0 collective-permute-start.17
  43.2 1.3 %collective-permute-start.18 = (f32[72,128]{1,0:T(8,128)S(1)}, f32[72,128]{1,0:T(8,128)S(1)}, u32[]{:S(2)}, u32[]{:S(2)}) collective-permute-start(f32[72,128]{1,0:T(8,128)S(1)} %add_add_fusion), channel_id=1, source_target_pairs={{0,2},{1,3},{2,0},{3,1},{4,6},{5,7},{6,4},{7,5},{8,10},{9,11},{10,... | collective-permute-start | bytes 110600 | tf_op jit(solution)/shard_map/ppermute | solution.py:46
  44.5 0.0 collective-permute-done.19.refs_3_
  44.5 1.4 %turned_blocks.1 = (bf16[2048,256]{1,0:T(8,128)(2,1)S(1)}, bf16[2048,256]{1,0:T(8,128)(2,1)S(1)}) custom-call(f32[2048,128]{1,0:T(8,128)S(1)} %bitcast.7, f32[2048,128]{1,0:T(8,128)S(1)} %collective-permute-done.refs_1_.p_ref, f32[2048,128]{1,0:T(8,128)S(1)} %collective-permute-done.8.far_own.refs_2_, f32[2048,128]{1,0:T(8,128)S(1)} %collective-permute-done.19.refs_3_, ...), custom_call_target="tpu_custom_call" | custom-call | flops 1400000000 | bytes 1 | tf_op jit(solution)/shard_map/turned_blocks/pallas_call | solution.py:427
  45.9 2.1 %collective-permute-done.17 = f32[72,128]{1,0:T(8,128)S(1)} collective-permute-done((f32[72,128]{1,0:T(8,128)S(1)}, f32[72,128]{1,0:T(8,128)S(1)}, u32[]{:S(2)}, u32[]{:S(2)}) %collective-permute-start.17) | collective-permute-done | bytes 36896 | tf_op jit(solution)/shard_map/ppermute | solution.py:46
  48.0 0.0 collective-permute-done.18
  48.1 3.3 %last_rotation.1 = f32[2048,128]{1,0:T(8,128)} custom-call(f32[72,128]{1,0:T(8,128)S(1)} %add.34.own_msg, f32[72,128]{1,0:T(8,128)S(1)} %add.35.y_msg, bf16[2048,256]{1,0:T(8,128)(2,1)S(1)} %get-tuple-element.42.high_ref, bf16[2048,256]{1,0:T(8,128)(2,1)S(1)} %get-tuple-element.46.low_ref), custom_call_target="tpu_custom_call" | custom-call | flops 4000000000 | bytes 1 | tf_op jit(solution)/shard_map/last_rotation/pallas_call | solution.py:495
  (8 shorter events, 0.0 us)
Async XLA Ops:
  0.0 9.1 %copy-start = (f32[8,16,16,128]{3,2,1,0:T(8,128)S(1)}, f32[8,16,16,128]{3,2,1,0:T(8,128)}, u32[]{:S(2)}) copy-start(f32[8,16,16,128]{3,2,1,0:T(8,128)} %param.1) | copy-start | bytes 3145732
  0.0 9.1 %collective-permute-start = (f32[2048,128]{1,0:T(8,128)}, f32[2048,128]{1,0:T(8,128)S(1)}, u32[]{:S(2)}, u32[]{:S(2)}) collective-permute-start(f32[2048,128]{1,0:T(8,128)} %bitcast.2), channel_id=1, source_target_pairs={{0,1},{1,0},{2,3},{3,2},{4,5},{5,4},{6,7},{7,6},{8,9},{9,8},{10,11... | collective-permute-start | bytes 3145736 | tf_op jit(solution)/shard_map/ppermute | solution.py:46
  0.5 28.9 %collective-permute-start.8 = (f32[2048,128]{1,0:T(8,128)}, f32[2048,128]{1,0:T(8,128)S(1)}, u32[]{:S(2)}, u32[]{:S(2)}) collective-permute-start(f32[2048,128]{1,0:T(8,128)} %bitcast.3), channel_id=1, source_target_pairs={{0,2},{1,3},{2,0},{3,1},{4,6},{5,7},{6,4},{7,5},{8,10},{9,11},{10,... | collective-permute-start | bytes 3145736 | tf_op jit(solution)/shard_map/ppermute | solution.py:46
  4.0 6.2 %collective-permute-start.1 = (f32[256,128]{1,0:T(8,128)S(1)}, f32[256,128]{1,0:T(8,128)S(1)}, u32[]{:S(2)}, u32[]{:S(2)}) collective-permute-start(f32[256,128]{1,0:T(8,128)S(1)} %get-tuple-element.28.edge_b), channel_id=1, source_target_pairs={{4,8},{12,16},{20,24},{8,4},{16,12},{24,20},{5,9},{13,17},{21,25},... | collective-permute-start | bytes 393224 | tf_op jit(solution)/shard_map/ppermute | solution.py:452
  4.7 9.5 %collective-permute-start.2 = (f32[256,128]{1,0:T(8,128)S(1)}, f32[256,128]{1,0:T(8,128)S(1)}, u32[]{:S(2)}, u32[]{:S(2)}) collective-permute-start(f32[256,128]{1,0:T(8,128)S(1)} %get-tuple-element.27.edge_a), channel_id=1, source_target_pairs={{0,4},{4,0},{8,12},{12,8},{16,20},{20,16},{24,28},{28,24},{1,5},{5... | collective-permute-start | bytes 393224 | tf_op jit(solution)/shard_map/ppermute | solution.py:451
  14.6 5.5 %collective-permute-start.4 = (f32[72,128]{1,0:T(8,128)S(1)}, f32[72,128]{1,0:T(8,128)S(1)}, u32[]{:S(2)}, u32[]{:S(2)}) collective-permute-start(f32[72,128]{1,0:T(8,128)S(1)} %get-tuple-element.33), channel_id=1, source_target_pairs={{0,12},{4,8},{8,4},{12,0},{16,28},{20,24},{24,20},{28,16},{1,13},{... | collective-permute-start | bytes 110600 | tf_op jit(solution)/shard_map/ppermute | solution.py:46
  18.1 4.0 %collective-permute-start.5 = (f32[72,128]{1,0:T(8,128)S(1)}, f32[72,128]{1,0:T(8,128)S(1)}, u32[]{:S(2)}, u32[]{:S(2)}) collective-permute-start(f32[72,128]{1,0:T(8,128)S(1)} %get-tuple-element.33), channel_id=1, source_target_pairs={{0,8},{4,12},{8,0},{12,4},{16,24},{20,28},{24,16},{28,20},{1,9},{5... | collective-permute-start | bytes 110600 | tf_op jit(solution)/shard_map/ppermute | solution.py:46
  18.6 4.0 %collective-permute-start.6 = (f32[72,128]{1,0:T(8,128)S(1)}, f32[72,128]{1,0:T(8,128)S(1)}, u32[]{:S(2)}, u32[]{:S(2)}) collective-permute-start(f32[72,128]{1,0:T(8,128)S(1)} %get-tuple-element.33), channel_id=1, source_target_pairs={{0,4},{4,0},{8,12},{12,8},{16,20},{20,16},{24,28},{28,24},{1,5},{5... | collective-permute-start | bytes 110600 | tf_op jit(solution)/shard_map/ppermute | solution.py:46
  18.8 6.4 %collective-permute-start.3 = (f32[512,128]{1,0:T(8,128)S(1)}, f32[512,128]{1,0:T(8,128)S(1)}, u32[]{:S(2)}, u32[]{:S(2)}) collective-permute-start(f32[512,128]{1,0:T(8,128)S(1)} %get-tuple-element.31.own_step), channel_id=1, source_target_pairs={{0,1},{1,0},{2,3},{3,2},{4,5},{5,4},{6,7},{7,6},{8,9},{9,8},{10,11... | collective-permute-start | bytes 786440 | tf_op jit(solution)/shard_map/ppermute | solution.py:46
  22.5 4.9 %collective-permute-start.7 = (f32[72,128]{1,0:T(8,128)S(1)}, f32[72,128]{1,0:T(8,128)S(1)}, u32[]{:S(2)}, u32[]{:S(2)}) collective-permute-start(f32[72,128]{1,0:T(8,128)S(1)} %add_add_fusion.1), channel_id=1, source_target_pairs={{0,16},{4,20},{8,24},{12,28},{16,0},{20,4},{24,8},{28,12},{1,17},{... | collective-permute-start | bytes 110600 | tf_op jit(solution)/shard_map/ppermute | solution.py:46
  27.5 3.4 %collective-permute-start.10 = (f32[72,128]{1,0:T(8,128)S(1)}, f32[72,128]{1,0:T(8,128)S(1)}, u32[]{:S(2)}, u32[]{:S(2)}) collective-permute-start(f32[72,128]{1,0:T(8,128)S(1)} %add.30.own_msg), channel_id=1, source_target_pairs={{0,3},{1,2},{2,1},{3,0},{4,7},{5,6},{6,5},{7,4},{8,11},{9,10},{10,... | collective-permute-start | bytes 110600 | tf_op jit(solution)/shard_map/ppermute | solution.py:46
  27.5 4.2 %collective-permute-start.11 = (f32[72,128]{1,0:T(8,128)S(1)}, f32[72,128]{1,0:T(8,128)S(1)}, u32[]{:S(2)}, u32[]{:S(2)}) collective-permute-start(f32[72,128]{1,0:T(8,128)S(1)} %add.30.own_msg), channel_id=1, source_target_pairs={{0,2},{1,3},{2,0},{3,1},{4,6},{5,7},{6,4},{7,5},{8,10},{9,11},{10,... | collective-permute-start | bytes 110600 | tf_op jit(solution)/shard_map/ppermute | solution.py:46
  28.1 3.6 %collective-permute-start.12 = (f32[72,128]{1,0:T(8,128)S(1)}, f32[72,128]{1,0:T(8,128)S(1)}, u32[]{:S(2)}, u32[]{:S(2)}) collective-permute-start(f32[72,128]{1,0:T(8,128)S(1)} %add.30.own_msg), channel_id=1, source_target_pairs={{0,1},{1,0},{2,3},{3,2},{4,5},{5,4},{6,7},{7,6},{8,9},{9,8},{10,11... | collective-permute-start | bytes 110600 | tf_op jit(solution)/shard_map/ppermute | solution.py:46
  30.1 3.7 %collective-permute-start.9 = (f32[256,128]{1,0:T(8,128)S(1)}, f32[256,128]{1,0:T(8,128)S(1)}, u32[]{:S(2)}, u32[]{:S(2)}) collective-permute-start(f32[256,128]{1,0:T(8,128)S(1)} %far_grams.1.far_ref), channel_id=1, source_target_pairs={{0,1},{1,0},{2,3},{3,2},{4,5},{5,4},{6,7},{7,6},{8,9},{9,8},{10,11... | collective-permute-start | bytes 393224 | tf_op jit(solution)/shard_map/ppermute | solution.py:46
  34.2 10.3 %collective-permute-start.19 = (f32[2048,128]{1,0:T(8,128)S(1)}, f32[2048,128]{1,0:T(8,128)S(1)}, u32[]{:S(2)}, u32[]{:S(2)}) collective-permute-start(f32[2048,128]{1,0:T(8,128)S(1)} %collective-permute-done.8.far_own.refs_2_), channel_id=1, source_target_pairs={{0,1},{1,0},{2,3},{3,2},{4,5},{5,4},{6,7},{7,6},{8,9},{9,8},{10,11... | collective-permute-start | bytes 3145736 | tf_op jit(solution)/shard_map/ppermute | solution.py:46
  34.3 5.0 %collective-permute-start.13 = (f32[72,128]{1,0:T(8,128)S(1)}, f32[72,128]{1,0:T(8,128)S(1)}, u32[]{:S(2)}, u32[]{:S(2)}) collective-permute-start(f32[72,128]{1,0:T(8,128)S(1)} %rotated_grams.1), channel_id=1, source_target_pairs={{0,12},{4,8},{8,4},{12,0},{16,28},{20,24},{24,20},{28,16},{1,13},{... | collective-permute-start | bytes 110600 | tf_op jit(solution)/shard_map/ppermute | solution.py:46
  35.9 4.0 %collective-permute-start.14 = (f32[72,128]{1,0:T(8,128)S(1)}, f32[72,128]{1,0:T(8,128)S(1)}, u32[]{:S(2)}, u32[]{:S(2)}) collective-permute-start(f32[72,128]{1,0:T(8,128)S(1)} %rotated_grams.1), channel_id=1, source_target_pairs={{0,8},{4,12},{8,0},{12,4},{16,24},{20,28},{24,16},{28,20},{1,9},{5... | collective-permute-start | bytes 110600 | tf_op jit(solution)/shard_map/ppermute | solution.py:46
  36.1 4.0 %collective-permute-start.15 = (f32[72,128]{1,0:T(8,128)S(1)}, f32[72,128]{1,0:T(8,128)S(1)}, u32[]{:S(2)}, u32[]{:S(2)}) collective-permute-start(f32[72,128]{1,0:T(8,128)S(1)} %rotated_grams.1), channel_id=1, source_target_pairs={{0,4},{4,0},{8,12},{12,8},{16,20},{20,16},{24,28},{28,24},{1,5},{5... | collective-permute-start | bytes 110600 | tf_op jit(solution)/shard_map/ppermute | solution.py:46
  40.0 5.9 %collective-permute-start.16 = (f32[72,128]{1,0:T(8,128)S(1)}, f32[72,128]{1,0:T(8,128)S(1)}, u32[]{:S(2)}, u32[]{:S(2)}) collective-permute-start(f32[72,128]{1,0:T(8,128)S(1)} %add_add_fusion), channel_id=1, source_target_pairs={{0,18},{1,19},{2,16},{3,17},{4,22},{5,23},{6,20},{7,21},{8,26},{9,... | collective-permute-start | bytes 110600 | tf_op jit(solution)/shard_map/ppermute | solution.py:408
  43.2 4.9 %collective-permute-start.17 = (f32[72,128]{1,0:T(8,128)S(1)}, f32[72,128]{1,0:T(8,128)S(1)}, u32[]{:S(2)}, u32[]{:S(2)}) collective-permute-start(f32[72,128]{1,0:T(8,128)S(1)} %add_add_fusion), channel_id=1, source_target_pairs={{0,16},{4,20},{8,24},{12,28},{16,0},{20,4},{24,8},{28,12},{1,17},{... | collective-permute-start | bytes 110600 | tf_op jit(solution)/shard_map/ppermute | solution.py:46
  43.2 4.9 %collective-permute-start.18 = (f32[72,128]{1,0:T(8,128)S(1)}, f32[72,128]{1,0:T(8,128)S(1)}, u32[]{:S(2)}, u32[]{:S(2)}) collective-permute-start(f32[72,128]{1,0:T(8,128)S(1)} %add_add_fusion), channel_id=1, source_target_pairs={{0,2},{1,3},{2,0},{3,1},{4,6},{5,7},{6,4},{7,5},{8,10},{9,11},{10,... | collective-permute-start | bytes 110600 | tf_op jit(solution)/shard_map/ppermute | solution.py:46

commit v4 on v3

--- a/solution.py
+++ b/solution.py
@@ -137,7 +137,7 @@
     d_ref[...] = diag
 
 
-def edge_kernel(edge_a, edge_b, p_ref, c_ref, d_ref, near_b, near_a, step_ref, msg_ref):
+def edge_kernel(edge_a, edge_b, p_ref, c_ref, d_ref, near_a, near_b, step_ref, msg_ref):
     layer, width = edge_a.shape
     layers = p_ref.shape[0] // layer
     half = width // 2
@@ -457,7 +457,7 @@
         [shape_of(cells, width), shape_of(width, width), shape_of(8, width)], [], 0.1, "inner_grams",
     )
     steps, msg = call(
-        edge_kernel, [edge_a, edge_b, peer, cross, diag, near_b, near_a],
+        edge_kernel, [edge_a, edge_b, peer, cross, diag, near_a, near_b],
         [shape_of(2 * layer, width), shape_of(half_rows, width)], [], 0.1, "edge_grams",
     )
     peer_steps = exchanged(steps, "blk", 1)

time: 51.5 us -> 50.3 us (0.977)
  waiting for transfers between devices: 14 us -> 12.6 us
    ppermute x1, starting transfers between devices: 4.34 us -> 1.56 us  [shards(): near_a = lax.ppermute(edge_a, 'space', route_a)]
    ppermute x17, starting transfers between devices: 16.8 us -> 19.4 us  [exchanged(): return lax.ppermute(value, axis, [(i, i ^ mask) for i in range(count)])]
    ppermute x1, waiting for transfers between devices: 3.98 us -> 2.23 us  [shards(): near_a = lax.ppermute(edge_a, 'space', route_a)]
  transfers between devices with their start and end apart: 20 -> 20, of which waited for: 11 -> 12; matrix products, arithmetic and copies ran while one was open for 0% -> 0% of each run, Pallas kernels for 17% -> 17%
where the time goes in v4:
time: 50.3 us; the launch traced here: 50.1 us
  starting transfers between devices  25 us (50%)
  waiting for transfers between devices  12.6 us (25%)
  Pallas kernels  12.3 us (24%)
    ppermute x17, starting transfers between devices, exchanged(): return lax.ppermute(value, axis, [(i, i ^ mask) for i in range(count)])  19.4 us
    ppermute x17, waiting for transfers between devices, exchanged(): return lax.ppermute(value, axis, [(i, i ^ mask) for i in range(count)])  10.4 us
    pallas_call x7, Pallas kernels, call(): pl.pallas_call(body, in_specs=[VMEM] * len(inputs), out_specs=[VMEM] * le...  7.99 us
    ppermute x1, starting transfers between devices, summed_with_y(): other_there = lax.ppermute(value, ('space', 'blk'), route)  3.41 us
    pallas_call x1, Pallas kernels, shards(): pl.pallas_call(last_kernel, in_specs=[VMEM] * 4, out_specs=pl.BlockSpec(m...  3.31 us
    ppermute x1, waiting for transfers between devices, shards(): near_a = lax.ppermute(edge_a, 'space', route_a)  2.23 us
    ppermute x1, starting transfers between devices, shards(): near_a = lax.ppermute(edge_a, 'space', route_a)  1.56 us
  transfers between devices with their start and end apart: 20, of which 12 were waited for; matrix products, arithmetic and copies ran while one was open for 0% of the time, Pallas kernels for 17%

profile of v4, /device:TPU:0, one launch (start us, length us, event | category | flops | bytes accessed | tf_op | source)
XLA Modules:
  0.0 50.1 jit_solution(8444163207741086967)
XLA Ops:
  0.0 0.5 collective-permute-start
  0.5 2.6 %collective-permute-start.8 = (f32[2048,128]{1,0:T(8,128)}, f32[2048,128]{1,0:T(8,128)S(1)}, u32[]{:S(2)}, u32[]{:S(2)}) collective-permute-start(f32[2048,128]{1,0:T(8,128)} %bitcast.3), channel_id=1, source_target_pairs={{0,2},{1,3},{2,0},{3,1},{4,6},{5,7},{6,4},{7,5},{8,10},{9,11},{10,... | collective-permute-start | bytes 3145736 | tf_op jit(solution)/shard_map/ppermute | solution.py:46
  3.0 1.0 %edges.1 = (f32[256,128]{1,0:T(8,128)S(1)}, f32[256,128]{1,0:T(8,128)S(1)}) custom-call(f32[2048,128]{1,0:T(8,128)} %bitcast.4), custom_call_target="tpu_custom_call" | custom-call | flops 100000000 | bytes 1 | tf_op jit(solution)/shard_map/edges/pallas_call | solution.py:441
  4.0 1.6 %collective-permute-start.1 = (f32[256,128]{1,0:T(8,128)S(1)}, f32[256,128]{1,0:T(8,128)S(1)}, u32[]{:S(2)}, u32[]{:S(2)}) collective-permute-start(f32[256,128]{1,0:T(8,128)S(1)} %get-tuple-element.27.edge_a), channel_id=1, source_target_pairs={{0,4},{4,0},{8,12},{12,8},{16,20},{20,16},{24,28},{28,24},{1,5},{5... | collective-permute-start | bytes 393224 | tf_op jit(solution)/shard_map/ppermute | solution.py:451
  5.6 0.7 %collective-permute-start.2 = (f32[256,128]{1,0:T(8,128)S(1)}, f32[256,128]{1,0:T(8,128)S(1)}, u32[]{:S(2)}, u32[]{:S(2)}) collective-permute-start(f32[256,128]{1,0:T(8,128)S(1)} %get-tuple-element.28.edge_b), channel_id=1, source_target_pairs={{4,8},{12,16},{20,24},{8,4},{16,12},{24,20},{5,9},{13,17},{21,25},... | collective-permute-start | bytes 393224 | tf_op jit(solution)/shard_map/ppermute | solution.py:452
  6.3 0.0 collective-permute-done.refs_1_.p_ref
  6.3 1.2 %inner_grams.1 = (f32[2048,128]{1,0:T(8,128)S(1)}, f32[128,128]{1,0:T(8,128)S(1)}, f32[8,128]{1,0:T(8,128)S(1)}) custom-call(f32[2048,128]{1,0:T(8,128)S(1)} %bitcast.5, f32[2048,128]{1,0:T(8,128)S(1)} %collective-permute-done.refs_1_.p_ref), custom_call_target="tpu_custom_call" | custom-call | flops 100000000 | bytes 1 | tf_op jit(solution)/shard_map/inner_grams/pallas_call | solution.py:427
  7.4 2.2 %collective-permute-done.1.near_a = f32[256,128]{1,0:T(8,128)S(1)} collective-permute-done((f32[256,128]{1,0:T(8,128)S(1)}, f32[256,128]{1,0:T(8,128)S(1)}, u32[]{:S(2)}, u32[]{:S(2)}) %collective-permute-start.1) | collective-permute-done | bytes 131104 | tf_op jit(solution)/shard_map/ppermute | solution.py:451
  9.7 0.0 collective-permute-done.2.near_b
  9.7 0.3 edge_grams.1
  10.0 5.6 %collective-permute-start.4 = (f32[72,128]{1,0:T(8,128)S(1)}, f32[72,128]{1,0:T(8,128)S(1)}, u32[]{:S(2)}, u32[]{:S(2)}) collective-permute-start(f32[72,128]{1,0:T(8,128)S(1)} %get-tuple-element.33), channel_id=1, source_target_pairs={{0,12},{4,8},{8,4},{12,0},{16,28},{20,24},{24,20},{28,16},{1,13},{... | collective-permute-start | bytes 110600 | tf_op jit(solution)/shard_map/ppermute | solution.py:46
  15.6 0.5 collective-permute-start.5
  16.1 1.0 %collective-permute-start.6 = (f32[72,128]{1,0:T(8,128)S(1)}, f32[72,128]{1,0:T(8,128)S(1)}, u32[]{:S(2)}, u32[]{:S(2)}) collective-permute-start(f32[72,128]{1,0:T(8,128)S(1)} %get-tuple-element.33), channel_id=1, source_target_pairs={{0,4},{4,0},{8,12},{12,8},{16,20},{20,16},{24,28},{28,24},{1,5},{5... | collective-permute-start | bytes 110600 | tf_op jit(solution)/shard_map/ppermute | solution.py:46
  17.1 0.0 collective-permute-start.3
  17.1 0.5 %collective-permute-done.4 = f32[72,128]{1,0:T(8,128)S(1)} collective-permute-done((f32[72,128]{1,0:T(8,128)S(1)}, f32[72,128]{1,0:T(8,128)S(1)}, u32[]{:S(2)}, u32[]{:S(2)}) %collective-permute-start.4) | collective-permute-done | bytes 36896 | tf_op jit(solution)/shard_map/ppermute | solution.py:46
  17.7 1.9 %collective-permute-done.5 = f32[72,128]{1,0:T(8,128)S(1)} collective-permute-done((f32[72,128]{1,0:T(8,128)S(1)}, f32[72,128]{1,0:T(8,128)S(1)}, u32[]{:S(2)}, u32[]{:S(2)}) %collective-permute-start.5) | collective-permute-done | bytes 36896 | tf_op jit(solution)/shard_map/ppermute | solution.py:46
  19.6 0.5 collective-permute-done.6
  20.0 2.7 %collective-permute-start.7 = (f32[72,128]{1,0:T(8,128)S(1)}, f32[72,128]{1,0:T(8,128)S(1)}, u32[]{:S(2)}, u32[]{:S(2)}) collective-permute-start(f32[72,128]{1,0:T(8,128)S(1)} %add_add_fusion.1), channel_id=1, source_target_pairs={{0,16},{4,20},{8,24},{12,28},{16,0},{20,4},{24,8},{28,12},{1,17},{... | collective-permute-start | bytes 110600 | tf_op jit(solution)/shard_map/ppermute | solution.py:46
  22.7 0.0 collective-permute-done.3.peer_step
  22.7 1.8 %near_grams.1 = (f32[256,256]{1,0:T(8,128)S(1)}, bf16[256,2048]{1,0:T(8,128)(2,1)S(1)}, bf16[256,2048]{1,0:T(8,128)(2,1)S(1)}) custom-call(f32[2048,128]{1,0:T(8,128)S(1)} %get-tuple-element.26.wo, f32[512,128]{1,0:T(8,128)S(1)} %get-tuple-element.31.own_step, f32[512,128]{1,0:T(8,128)S(1)} %collective-permute-done.3.peer_step, f32[2048,128]{1,0:T(8,128)S(1)} %bitcast.6, ...), custom_call_target="tpu_custom_call" | custom-call | flops 2500000000 | bytes 1 | tf_op jit(solution)/shard_map/near_grams/pallas_call | solution.py:427
  24.5 0.4 collective-permute-done.7
  25.0 0.0 collective-permute-start.10
  25.0 0.4 collective-permute-start.11
  25.4 1.4 %collective-permute-start.12 = (f32[72,128]{1,0:T(8,128)S(1)}, f32[72,128]{1,0:T(8,128)S(1)}, u32[]{:S(2)}, u32[]{:S(2)}) collective-permute-start(f32[72,128]{1,0:T(8,128)S(1)} %add.30.own_msg), channel_id=1, source_target_pairs={{0,1},{1,0},{2,3},{3,2},{4,5},{5,4},{6,7},{7,6},{8,9},{9,8},{10,11... | collective-permute-start | bytes 110600 | tf_op jit(solution)/shard_map/ppermute | solution.py:46
  26.8 0.2 collective-permute-done.8.far_own.refs_2_
  27.0 0.7 %far_grams.1.far_ref = f32[256,128]{1,0:T(8,128)S(1)} custom-call(bf16[256,2048]{1,0:T(8,128)(2,1)S(1)} %get-tuple-element.35.high_t, bf16[256,2048]{1,0:T(8,128)(2,1)S(1)} %get-tuple-element.36.low_t, f32[2048,128]{1,0:T(8,128)S(1)} %collective-permute-done.8.far_own.refs_2_), custom_call_target="tpu_custom_call" | custom-call | flops 700000000 | bytes 1 | tf_op jit(solution)/shard_map/far_grams/pallas_call | solution.py:427
  27.7 0.1 collective-permute-start.9
  27.8 0.6 %collective-permute-done.10.far_msg = f32[72,128]{1,0:T(8,128)S(1)} collective-permute-done((f32[72,128]{1,0:T(8,128)S(1)}, f32[72,128]{1,0:T(8,128)S(1)}, u32[]{:S(2)}, u32[]{:S(2)}) %collective-permute-start.10) | collective-permute-done | bytes 36896 | tf_op jit(solution)/shard_map/ppermute | solution.py:46
  28.4 0.8 %collective-permute-done.11.y_msg = f32[72,128]{1,0:T(8,128)S(1)} collective-permute-done((f32[72,128]{1,0:T(8,128)S(1)}, f32[72,128]{1,0:T(8,128)S(1)}, u32[]{:S(2)}, u32[]{:S(2)}) %collective-permute-start.11) | collective-permute-done | bytes 36896 | tf_op jit(solution)/shard_map/ppermute | solution.py:46
  29.2 0.0 collective-permute-done.12.core_msg
  29.2 2.1 %first_rotation.1 = (f32[128,256]{1,0:T(8,128)S(1)}, f32[128,256]{1,0:T(8,128)S(1)}) custom-call(f32[72,128]{1,0:T(8,128)S(1)} %collective-permute-done.10.far_msg, f32[72,128]{1,0:T(8,128)S(1)} %collective-permute-done.11.y_msg, f32[72,128]{1,0:T(8,128)S(1)} %collective-permute-done.12.core_msg, f32[72,128]{1,0:T(8,128)S(1)} %add.30.own_msg), custom_call_target="tpu_custom_call" | custom-call | flops 4000000000 | bytes 1 | tf_op jit(solution)/shard_map/first_rotation/pallas_call | solution.py:427
  31.3 0.0 collective-permute-done.9.far_peer_ref
  31.3 0.5 rotated_grams.1
  31.7 0.1 collective-permute-start.19
  31.8 2.6 %collective-permute-start.13 = (f32[72,128]{1,0:T(8,128)S(1)}, f32[72,128]{1,0:T(8,128)S(1)}, u32[]{:S(2)}, u32[]{:S(2)}) collective-permute-start(f32[72,128]{1,0:T(8,128)S(1)} %rotated_grams.1), channel_id=1, source_target_pairs={{0,12},{4,8},{8,4},{12,0},{16,28},{20,24},{24,20},{28,16},{1,13},{... | collective-permute-start | bytes 110600 | tf_op jit(solution)/shard_map/ppermute | solution.py:46
  34.4 0.1 collective-permute-start.14
  34.5 0.8 %collective-permute-start.15 = (f32[72,128]{1,0:T(8,128)S(1)}, f32[72,128]{1,0:T(8,128)S(1)}, u32[]{:S(2)}, u32[]{:S(2)}) collective-permute-start(f32[72,128]{1,0:T(8,128)S(1)} %rotated_grams.1), channel_id=1, source_target_pairs={{0,4},{4,0},{8,12},{12,8},{16,20},{20,16},{24,28},{28,24},{1,5},{5... | collective-permute-start | bytes 110600 | tf_op jit(solution)/shard_map/ppermute | solution.py:46
  35.4 1.4 %collective-permute-done.13 = f32[72,128]{1,0:T(8,128)S(1)} collective-permute-done((f32[72,128]{1,0:T(8,128)S(1)}, f32[72,128]{1,0:T(8,128)S(1)}, u32[]{:S(2)}, u32[]{:S(2)}) %collective-permute-start.13) | collective-permute-done | bytes 36896 | tf_op jit(solution)/shard_map/ppermute | solution.py:46
  36.7 1.6 %collective-permute-done.14 = f32[72,128]{1,0:T(8,128)S(1)} collective-permute-done((f32[72,128]{1,0:T(8,128)S(1)}, f32[72,128]{1,0:T(8,128)S(1)}, u32[]{:S(2)}, u32[]{:S(2)}) %collective-permute-start.14) | collective-permute-done | bytes 36896 | tf_op jit(solution)/shard_map/ppermute | solution.py:46
  38.4 0.1 collective-permute-done.15
  38.5 3.4 %collective-permute-start.16 = (f32[72,128]{1,0:T(8,128)S(1)}, f32[72,128]{1,0:T(8,128)S(1)}, u32[]{:S(2)}, u32[]{:S(2)}) collective-permute-start(f32[72,128]{1,0:T(8,128)S(1)} %add_add_fusion), channel_id=1, source_target_pairs={{0,18},{1,19},{2,16},{3,17},{4,22},{5,23},{6,20},{7,21},{8,26},{9,... | collective-permute-start | bytes 110600 | tf_op jit(solution)/shard_map/ppermute | solution.py:408
  41.9 0.5 %collective-permute-start.17 = (f32[72,128]{1,0:T(8,128)S(1)}, f32[72,128]{1,0:T(8,128)S(1)}, u32[]{:S(2)}, u32[]{:S(2)}) collective-permute-start(f32[72,128]{1,0:T(8,128)S(1)} %add_add_fusion), channel_id=1, source_target_pairs={{0,16},{4,20},{8,24},{12,28},{16,0},{20,4},{24,8},{28,12},{1,17},{... | collective-permute-start | bytes 110600 | tf_op jit(solution)/shard_map/ppermute | solution.py:46
  42.5 0.5 %collective-permute-start.18 = (f32[72,128]{1,0:T(8,128)S(1)}, f32[72,128]{1,0:T(8,128)S(1)}, u32[]{:S(2)}, u32[]{:S(2)}) collective-permute-start(f32[72,128]{1,0:T(8,128)S(1)} %add_add_fusion), channel_id=1, source_target_pairs={{0,2},{1,3},{2,0},{3,1},{4,6},{5,7},{6,4},{7,5},{8,10},{9,11},{10,... | collective-permute-start | bytes 110600 | tf_op jit(solution)/shard_map/ppermute | solution.py:46
  43.0 0.0 collective-permute-done.19.refs_3_
  43.0 1.4 %turned_blocks.1 = (bf16[2048,256]{1,0:T(8,128)(2,1)S(1)}, bf16[2048,256]{1,0:T(8,128)(2,1)S(1)}) custom-call(f32[2048,128]{1,0:T(8,128)S(1)} %bitcast.7, f32[2048,128]{1,0:T(8,128)S(1)} %collective-permute-done.refs_1_.p_ref, f32[2048,128]{1,0:T(8,128)S(1)} %collective-permute-done.8.far_own.refs_2_, f32[2048,128]{1,0:T(8,128)S(1)} %collective-permute-done.19.refs_3_, ...), custom_call_target="tpu_custom_call" | custom-call | flops 1400000000 | bytes 1 | tf_op jit(solution)/shard_map/turned_blocks/pallas_call | solution.py:427
  44.4 2.4 %collective-permute-done.17 = f32[72,128]{1,0:T(8,128)S(1)} collective-permute-done((f32[72,128]{1,0:T(8,128)S(1)}, f32[72,128]{1,0:T(8,128)S(1)}, u32[]{:S(2)}, u32[]{:S(2)}) %collective-permute-start.17) | collective-permute-done | bytes 36896 | tf_op jit(solution)/shard_map/ppermute | solution.py:46
  46.8 0.0 collective-permute-done.18
  46.8 3.3 %last_rotation.1 = f32[2048,128]{1,0:T(8,128)} custom-call(f32[72,128]{1,0:T(8,128)S(1)} %add.34.own_msg, f32[72,128]{1,0:T(8,128)S(1)} %add.35.y_msg, bf16[2048,256]{1,0:T(8,128)(2,1)S(1)} %get-tuple-element.42.high_ref, bf16[2048,256]{1,0:T(8,128)(2,1)S(1)} %get-tuple-element.46.low_ref), custom_call_target="tpu_custom_call" | custom-call | flops 4000000000 | bytes 1 | tf_op jit(solution)/shard_map/last_rotation/pallas_call | solution.py:495
  (8 shorter events, 0.1 us)
Async XLA Ops:
  0.0 6.3 %copy-start = (f32[8,16,16,128]{3,2,1,0:T(8,128)S(1)}, f32[8,16,16,128]{3,2,1,0:T(8,128)}, u32[]{:S(2)}) copy-start(f32[8,16,16,128]{3,2,1,0:T(8,128)} %param.1) | copy-start | bytes 3145732
  0.0 6.3 %collective-permute-start = (f32[2048,128]{1,0:T(8,128)}, f32[2048,128]{1,0:T(8,128)S(1)}, u32[]{:S(2)}, u32[]{:S(2)}) collective-permute-start(f32[2048,128]{1,0:T(8,128)} %bitcast.2), channel_id=1, source_target_pairs={{0,1},{1,0},{2,3},{3,2},{4,5},{5,4},{6,7},{7,6},{8,9},{9,8},{10,11... | collective-permute-start | bytes 3145736 | tf_op jit(solution)/shard_map/ppermute | solution.py:46
  0.5 26.6 %collective-permute-start.8 = (f32[2048,128]{1,0:T(8,128)}, f32[2048,128]{1,0:T(8,128)S(1)}, u32[]{:S(2)}, u32[]{:S(2)}) collective-permute-start(f32[2048,128]{1,0:T(8,128)} %bitcast.3), channel_id=1, source_target_pairs={{0,2},{1,3},{2,0},{3,1},{4,6},{5,7},{6,4},{7,5},{8,10},{9,11},{10,... | collective-permute-start | bytes 3145736 | tf_op jit(solution)/shard_map/ppermute | solution.py:46
  4.0 5.6 %collective-permute-start.1 = (f32[256,128]{1,0:T(8,128)S(1)}, f32[256,128]{1,0:T(8,128)S(1)}, u32[]{:S(2)}, u32[]{:S(2)}) collective-permute-start(f32[256,128]{1,0:T(8,128)S(1)} %get-tuple-element.27.edge_a), channel_id=1, source_target_pairs={{0,4},{4,0},{8,12},{12,8},{16,20},{20,16},{24,28},{28,24},{1,5},{5... | collective-permute-start | bytes 393224 | tf_op jit(solution)/shard_map/ppermute | solution.py:451
  5.6 4.1 %collective-permute-start.2 = (f32[256,128]{1,0:T(8,128)S(1)}, f32[256,128]{1,0:T(8,128)S(1)}, u32[]{:S(2)}, u32[]{:S(2)}) collective-permute-start(f32[256,128]{1,0:T(8,128)S(1)} %get-tuple-element.28.edge_b), channel_id=1, source_target_pairs={{4,8},{12,16},{20,24},{8,4},{16,12},{24,20},{5,9},{13,17},{21,25},... | collective-permute-start | bytes 393224 | tf_op jit(solution)/shard_map/ppermute | solution.py:452
  10.0 7.6 %collective-permute-start.4 = (f32[72,128]{1,0:T(8,128)S(1)}, f32[72,128]{1,0:T(8,128)S(1)}, u32[]{:S(2)}, u32[]{:S(2)}) collective-permute-start(f32[72,128]{1,0:T(8,128)S(1)} %get-tuple-element.33), channel_id=1, source_target_pairs={{0,12},{4,8},{8,4},{12,0},{16,28},{20,24},{24,20},{28,16},{1,13},{... | collective-permute-start | bytes 110600 | tf_op jit(solution)/shard_map/ppermute | solution.py:46
  15.6 4.0 %collective-permute-start.5 = (f32[72,128]{1,0:T(8,128)S(1)}, f32[72,128]{1,0:T(8,128)S(1)}, u32[]{:S(2)}, u32[]{:S(2)}) collective-permute-start(f32[72,128]{1,0:T(8,128)S(1)} %get-tuple-element.33), channel_id=1, source_target_pairs={{0,8},{4,12},{8,0},{12,4},{16,24},{20,28},{24,16},{28,20},{1,9},{5... | collective-permute-start | bytes 110600 | tf_op jit(solution)/shard_map/ppermute | solution.py:46
  16.1 4.0 %collective-permute-start.6 = (f32[72,128]{1,0:T(8,128)S(1)}, f32[72,128]{1,0:T(8,128)S(1)}, u32[]{:S(2)}, u32[]{:S(2)}) collective-permute-start(f32[72,128]{1,0:T(8,128)S(1)} %get-tuple-element.33), channel_id=1, source_target_pairs={{0,4},{4,0},{8,12},{12,8},{16,20},{20,16},{24,28},{28,24},{1,5},{5... | collective-permute-start | bytes 110600 | tf_op jit(solution)/shard_map/ppermute | solution.py:46
  17.1 5.6 %collective-permute-start.3 = (f32[512,128]{1,0:T(8,128)S(1)}, f32[512,128]{1,0:T(8,128)S(1)}, u32[]{:S(2)}, u32[]{:S(2)}) collective-permute-start(f32[512,128]{1,0:T(8,128)S(1)} %get-tuple-element.31.own_step), channel_id=1, source_target_pairs={{0,1},{1,0},{2,3},{3,2},{4,5},{5,4},{6,7},{7,6},{8,9},{9,8},{10,11... | collective-permute-start | bytes 786440 | tf_op jit(solution)/shard_map/ppermute | solution.py:46
  20.0 4.9 %collective-permute-start.7 = (f32[72,128]{1,0:T(8,128)S(1)}, f32[72,128]{1,0:T(8,128)S(1)}, u32[]{:S(2)}, u32[]{:S(2)}) collective-permute-start(f32[72,128]{1,0:T(8,128)S(1)} %add_add_fusion.1), channel_id=1, source_target_pairs={{0,16},{4,20},{8,24},{12,28},{16,0},{20,4},{24,8},{28,12},{1,17},{... | collective-permute-start | bytes 110600 | tf_op jit(solution)/shard_map/ppermute | solution.py:46
  25.0 3.4 %collective-permute-start.10 = (f32[72,128]{1,0:T(8,128)S(1)}, f32[72,128]{1,0:T(8,128)S(1)}, u32[]{:S(2)}, u32[]{:S(2)}) collective-permute-start(f32[72,128]{1,0:T(8,128)S(1)} %add.30.own_msg), channel_id=1, source_target_pairs={{0,3},{1,2},{2,1},{3,0},{4,7},{5,6},{6,5},{7,4},{8,11},{9,10},{10,... | collective-permute-start | bytes 110600 | tf_op jit(solution)/shard_map/ppermute | solution.py:46
  25.0 4.2 %collective-permute-start.11 = (f32[72,128]{1,0:T(8,128)S(1)}, f32[72,128]{1,0:T(8,128)S(1)}, u32[]{:S(2)}, u32[]{:S(2)}) collective-permute-start(f32[72,128]{1,0:T(8,128)S(1)} %add.30.own_msg), channel_id=1, source_target_pairs={{0,2},{1,3},{2,0},{3,1},{4,6},{5,7},{6,4},{7,5},{8,10},{9,11},{10,... | collective-permute-start | bytes 110600 | tf_op jit(solution)/shard_map/ppermute | solution.py:46
  25.4 3.7 %collective-permute-start.12 = (f32[72,128]{1,0:T(8,128)S(1)}, f32[72,128]{1,0:T(8,128)S(1)}, u32[]{:S(2)}, u32[]{:S(2)}) collective-permute-start(f32[72,128]{1,0:T(8,128)S(1)} %add.30.own_msg), channel_id=1, source_target_pairs={{0,1},{1,0},{2,3},{3,2},{4,5},{5,4},{6,7},{7,6},{8,9},{9,8},{10,11... | collective-permute-start | bytes 110600 | tf_op jit(solution)/shard_map/ppermute | solution.py:46
  27.7 3.5 %collective-permute-start.9 = (f32[256,128]{1,0:T(8,128)S(1)}, f32[256,128]{1,0:T(8,128)S(1)}, u32[]{:S(2)}, u32[]{:S(2)}) collective-permute-start(f32[256,128]{1,0:T(8,128)S(1)} %far_grams.1.far_ref), channel_id=1, source_target_pairs={{0,1},{1,0},{2,3},{3,2},{4,5},{5,4},{6,7},{7,6},{8,9},{9,8},{10,11... | collective-permute-start | bytes 393224 | tf_op jit(solution)/shard_map/ppermute | solution.py:46
  31.7 11.2 %collective-permute-start.19 = (f32[2048,128]{1,0:T(8,128)S(1)}, f32[2048,128]{1,0:T(8,128)S(1)}, u32[]{:S(2)}, u32[]{:S(2)}) collective-permute-start(f32[2048,128]{1,0:T(8,128)S(1)} %collective-permute-done.8.far_own.refs_2_), channel_id=1, source_target_pairs={{0,1},{1,0},{2,3},{3,2},{4,5},{5,4},{6,7},{7,6},{8,9},{9,8},{10,11... | collective-permute-start | bytes 3145736 | tf_op jit(solution)/shard_map/ppermute | solution.py:46
  31.8 4.9 %collective-permute-start.13 = (f32[72,128]{1,0:T(8,128)S(1)}, f32[72,128]{1,0:T(8,128)S(1)}, u32[]{:S(2)}, u32[]{:S(2)}) collective-permute-start(f32[72,128]{1,0:T(8,128)S(1)} %rotated_grams.1), channel_id=1, source_target_pairs={{0,12},{4,8},{8,4},{12,0},{16,28},{20,24},{24,20},{28,16},{1,13},{... | collective-permute-start | bytes 110600 | tf_op jit(solution)/shard_map/ppermute | solution.py:46
  34.4 4.0 %collective-permute-start.14 = (f32[72,128]{1,0:T(8,128)S(1)}, f32[72,128]{1,0:T(8,128)S(1)}, u32[]{:S(2)}, u32[]{:S(2)}) collective-permute-start(f32[72,128]{1,0:T(8,128)S(1)} %rotated_grams.1), channel_id=1, source_target_pairs={{0,8},{4,12},{8,0},{12,4},{16,24},{20,28},{24,16},{28,20},{1,9},{5... | collective-permute-start | bytes 110600 | tf_op jit(solution)/shard_map/ppermute | solution.py:46
  34.5 4.0 %collective-permute-start.15 = (f32[72,128]{1,0:T(8,128)S(1)}, f32[72,128]{1,0:T(8,128)S(1)}, u32[]{:S(2)}, u32[]{:S(2)}) collective-permute-start(f32[72,128]{1,0:T(8,128)S(1)} %rotated_grams.1), channel_id=1, source_target_pairs={{0,4},{4,0},{8,12},{12,8},{16,20},{20,16},{24,28},{28,24},{1,5},{5... | collective-permute-start | bytes 110600 | tf_op jit(solution)/shard_map/ppermute | solution.py:46
  38.5 5.9 %collective-permute-start.16 = (f32[72,128]{1,0:T(8,128)S(1)}, f32[72,128]{1,0:T(8,128)S(1)}, u32[]{:S(2)}, u32[]{:S(2)}) collective-permute-start(f32[72,128]{1,0:T(8,128)S(1)} %add_add_fusion), channel_id=1, source_target_pairs={{0,18},{1,19},{2,16},{3,17},{4,22},{5,23},{6,20},{7,21},{8,26},{9,... | collective-permute-start | bytes 110600 | tf_op jit(solution)/shard_map/ppermute | solution.py:408
  41.9 4.9 %collective-permute-start.17 = (f32[72,128]{1,0:T(8,128)S(1)}, f32[72,128]{1,0:T(8,128)S(1)}, u32[]{:S(2)}, u32[]{:S(2)}) collective-permute-start(f32[72,128]{1,0:T(8,128)S(1)} %add_add_fusion), channel_id=1, source_target_pairs={{0,16},{4,20},{8,24},{12,28},{16,0},{20,4},{24,8},{28,12},{1,17},{... | collective-permute-start | bytes 110600 | tf_op jit(solution)/shard_map/ppermute | solution.py:46
  42.5 4.3 %collective-permute-start.18 = (f32[72,128]{1,0:T(8,128)S(1)}, f32[72,128]{1,0:T(8,128)S(1)}, u32[]{:S(2)}, u32[]{:S(2)}) collective-permute-start(f32[72,128]{1,0:T(8,128)S(1)} %add_add_fusion), channel_id=1, source_target_pairs={{0,2},{1,3},{2,0},{3,1},{4,6},{5,7},{6,4},{7,5},{8,10},{9,11},{10,... | collective-permute-start | bytes 110600 | tf_op jit(solution)/shard_map/ppermute | solution.py:46

commit v5 on v4

--- a/solution.py
+++ b/solution.py
@@ -70,25 +70,20 @@
 def product(left, right):
     a, b, c = thirds(left)
     x, y, z = thirds(right)
-
-    def pair(one, two, three, four):
-        return jnp.dot(
-            jnp.concatenate([one, two], axis=1), jnp.concatenate([three, four], axis=0),
-            preferred_element_type=F32,
-        )
-
-    return pair(a, a, x, y) + (pair(b, a, x, z) + pair(c, b, x, y))
+    return jnp.dot(
+        jnp.concatenate([c, b, a, b, a, a], axis=1), jnp.concatenate([x, y, z, x, y, x], axis=0),
+        preferred_element_type=F32,
+    )
 
 
 def product_3(left, right):
     left_high, left_low = halves(left)
     right_high, right_low = halves(right)
-    deep = jnp.dot(
-        jnp.concatenate([left_high, left_low], axis=1),
-        jnp.concatenate([right_high, right_high], axis=0),
+    return jnp.dot(
+        jnp.concatenate([left_low, left_high, left_high], axis=1),
+        jnp.concatenate([right_high, right_low, right_high], axis=0),
         preferred_element_type=F32,
     )
-    return deep + jnp.dot(left_high, right_low, preferred_element_type=F32)
 
 
 def product_nt(left, right):

time: 50.3 us -> 50.4 us (level)
  no operation moved by 1% of the time
where the time goes in v5:
time: 50.4 us; the launch traced here: 50.3 us
  starting transfers between devices  25 us (50%)
  waiting for transfers between devices  12.6 us (25%)
  Pallas kernels  12.5 us (25%)
    ppermute x17, starting transfers between devices, exchanged(): return lax.ppermute(value, axis, [(i, i ^ mask) for i in range(count)])  19.4 us
    ppermute x17, waiting for transfers between devices, exchanged(): return lax.ppermute(value, axis, [(i, i ^ mask) for i in range(count)])  10.4 us
    pallas_call x7, Pallas kernels, call(): pl.pallas_call(body, in_specs=[VMEM] * len(inputs), out_specs=[VMEM] * le...  8.12 us
    ppermute x1, starting transfers between devices, summed_with_y(): other_there = lax.ppermute(value, ('space', 'blk'), route)  3.42 us
    pallas_call x1, Pallas kernels, shards(): pl.pallas_call(last_kernel, in_specs=[VMEM] * 4, out_specs=pl.BlockSpec(m...  3.36 us
    ppermute x1, waiting for transfers between devices, shards(): near_a = lax.ppermute(edge_a, 'space', route_a)  2.23 us
    ppermute x1, starting transfers between devices, shards(): near_a = lax.ppermute(edge_a, 'space', route_a)  1.56 us
  transfers between devices with their start and end apart: 20, of which 12 were waited for; matrix products, arithmetic and copies ran while one was open for 0% of the time, Pallas kernels for 17%

profile of v5, /device:TPU:0, one launch (start us, length us, event | category | flops | bytes accessed | tf_op | source)
XLA Modules:
  0.0 50.3 jit_solution(10311400940225542619)
XLA Ops:
  0.0 0.5 collective-permute-start
  0.5 2.6 %collective-permute-start.8 = (f32[2048,128]{1,0:T(8,128)}, f32[2048,128]{1,0:T(8,128)S(1)}, u32[]{:S(2)}, u32[]{:S(2)}) collective-permute-start(f32[2048,128]{1,0:T(8,128)} %bitcast.3), channel_id=1, source_target_pairs={{0,2},{1,3},{2,0},{3,1},{4,6},{5,7},{6,4},{7,5},{8,10},{9,11},{10,... | collective-permute-start | bytes 3145736 | tf_op jit(solution)/shard_map/ppermute | solution.py:46
  3.0 1.0 %edges.1 = (f32[256,128]{1,0:T(8,128)S(1)}, f32[256,128]{1,0:T(8,128)S(1)}) custom-call(f32[2048,128]{1,0:T(8,128)} %bitcast.4), custom_call_target="tpu_custom_call" | custom-call | flops 100000000 | bytes 1 | tf_op jit(solution)/shard_map/edges/pallas_call | solution.py:436
  4.0 1.6 %collective-permute-start.1 = (f32[256,128]{1,0:T(8,128)S(1)}, f32[256,128]{1,0:T(8,128)S(1)}, u32[]{:S(2)}, u32[]{:S(2)}) collective-permute-start(f32[256,128]{1,0:T(8,128)S(1)} %get-tuple-element.27.edge_a), channel_id=1, source_target_pairs={{0,4},{4,0},{8,12},{12,8},{16,20},{20,16},{24,28},{28,24},{1,5},{5... | collective-permute-start | bytes 393224 | tf_op jit(solution)/shard_map/ppermute | solution.py:446
  5.6 0.7 %collective-permute-start.2 = (f32[256,128]{1,0:T(8,128)S(1)}, f32[256,128]{1,0:T(8,128)S(1)}, u32[]{:S(2)}, u32[]{:S(2)}) collective-permute-start(f32[256,128]{1,0:T(8,128)S(1)} %get-tuple-element.28.edge_b), channel_id=1, source_target_pairs={{4,8},{12,16},{20,24},{8,4},{16,12},{24,20},{5,9},{13,17},{21,25},... | collective-permute-start | bytes 393224 | tf_op jit(solution)/shard_map/ppermute | solution.py:447
  6.3 0.0 collective-permute-done.refs_1_.p_ref
  6.3 1.2 %inner_grams.1 = (f32[2048,128]{1,0:T(8,128)S(1)}, f32[128,128]{1,0:T(8,128)S(1)}, f32[8,128]{1,0:T(8,128)S(1)}) custom-call(f32[2048,128]{1,0:T(8,128)S(1)} %bitcast.5, f32[2048,128]{1,0:T(8,128)S(1)} %collective-permute-done.refs_1_.p_ref), custom_call_target="tpu_custom_call" | custom-call | flops 100000000 | bytes 1 | tf_op jit(solution)/shard_map/inner_grams/pallas_call | solution.py:422
  7.4 2.2 %collective-permute-done.1.near_a = f32[256,128]{1,0:T(8,128)S(1)} collective-permute-done((f32[256,128]{1,0:T(8,128)S(1)}, f32[256,128]{1,0:T(8,128)S(1)}, u32[]{:S(2)}, u32[]{:S(2)}) %collective-permute-start.1) | collective-permute-done | bytes 131104 | tf_op jit(solution)/shard_map/ppermute | solution.py:446
  9.7 0.0 collective-permute-done.2.near_b
  9.7 0.3 edge_grams.1
  10.0 5.6 %collective-permute-start.4 = (f32[72,128]{1,0:T(8,128)S(1)}, f32[72,128]{1,0:T(8,128)S(1)}, u32[]{:S(2)}, u32[]{:S(2)}) collective-permute-start(f32[72,128]{1,0:T(8,128)S(1)} %get-tuple-element.33), channel_id=1, source_target_pairs={{0,12},{4,8},{8,4},{12,0},{16,28},{20,24},{24,20},{28,16},{1,13},{... | collective-permute-start | bytes 110600 | tf_op jit(solution)/shard_map/ppermute | solution.py:46
  15.6 0.5 collective-permute-start.5
  16.1 1.0 %collective-permute-start.6 = (f32[72,128]{1,0:T(8,128)S(1)}, f32[72,128]{1,0:T(8,128)S(1)}, u32[]{:S(2)}, u32[]{:S(2)}) collective-permute-start(f32[72,128]{1,0:T(8,128)S(1)} %get-tuple-element.33), channel_id=1, source_target_pairs={{0,4},{4,0},{8,12},{12,8},{16,20},{20,16},{24,28},{28,24},{1,5},{5... | collective-permute-start | bytes 110600 | tf_op jit(solution)/shard_map/ppermute | solution.py:46
  17.1 0.0 collective-permute-start.3
  17.1 0.5 %collective-permute-done.4 = f32[72,128]{1,0:T(8,128)S(1)} collective-permute-done((f32[72,128]{1,0:T(8,128)S(1)}, f32[72,128]{1,0:T(8,128)S(1)}, u32[]{:S(2)}, u32[]{:S(2)}) %collective-permute-start.4) | collective-permute-done | bytes 36896 | tf_op jit(solution)/shard_map/ppermute | solution.py:46
  17.7 1.9 %collective-permute-done.5 = f32[72,128]{1,0:T(8,128)S(1)} collective-permute-done((f32[72,128]{1,0:T(8,128)S(1)}, f32[72,128]{1,0:T(8,128)S(1)}, u32[]{:S(2)}, u32[]{:S(2)}) %collective-permute-start.5) | collective-permute-done | bytes 36896 | tf_op jit(solution)/shard_map/ppermute | solution.py:46
  19.6 0.5 collective-permute-done.6
  20.0 2.7 %collective-permute-start.7 = (f32[72,128]{1,0:T(8,128)S(1)}, f32[72,128]{1,0:T(8,128)S(1)}, u32[]{:S(2)}, u32[]{:S(2)}) collective-permute-start(f32[72,128]{1,0:T(8,128)S(1)} %add_add_fusion.1), channel_id=1, source_target_pairs={{0,16},{4,20},{8,24},{12,28},{16,0},{20,4},{24,8},{28,12},{1,17},{... | collective-permute-start | bytes 110600 | tf_op jit(solution)/shard_map/ppermute | solution.py:46
  22.7 0.0 collective-permute-done.3.peer_step
  22.7 1.8 %near_grams.1 = (f32[256,256]{1,0:T(8,128)S(1)}, bf16[256,2048]{1,0:T(8,128)(2,1)S(1)}, bf16[256,2048]{1,0:T(8,128)(2,1)S(1)}) custom-call(f32[2048,128]{1,0:T(8,128)S(1)} %get-tuple-element.26.wo, f32[512,128]{1,0:T(8,128)S(1)} %get-tuple-element.31.own_step, f32[512,128]{1,0:T(8,128)S(1)} %collective-permute-done.3.peer_step, f32[2048,128]{1,0:T(8,128)S(1)} %bitcast.6, ...), custom_call_target="tpu_custom_call" | custom-call | flops 2500000000 | bytes 1 | tf_op jit(solution)/shard_map/near_grams/pallas_call | solution.py:422
  24.5 0.4 collective-permute-done.7
  25.0 0.0 collective-permute-start.10
  25.0 0.4 collective-permute-start.11
  25.4 1.4 %collective-permute-start.12 = (f32[72,128]{1,0:T(8,128)S(1)}, f32[72,128]{1,0:T(8,128)S(1)}, u32[]{:S(2)}, u32[]{:S(2)}) collective-permute-start(f32[72,128]{1,0:T(8,128)S(1)} %add.30.own_msg), channel_id=1, source_target_pairs={{0,1},{1,0},{2,3},{3,2},{4,5},{5,4},{6,7},{7,6},{8,9},{9,8},{10,11... | collective-permute-start | bytes 110600 | tf_op jit(solution)/shard_map/ppermute | solution.py:46
  26.8 0.2 collective-permute-done.8.far_own.refs_2_
  27.0 0.7 %far_grams.1.far_ref = f32[256,128]{1,0:T(8,128)S(1)} custom-call(bf16[256,2048]{1,0:T(8,128)(2,1)S(1)} %get-tuple-element.35.high_t, bf16[256,2048]{1,0:T(8,128)(2,1)S(1)} %get-tuple-element.36.low_t, f32[2048,128]{1,0:T(8,128)S(1)} %collective-permute-done.8.far_own.refs_2_), custom_call_target="tpu_custom_call" | custom-call | flops 700000000 | bytes 1 | tf_op jit(solution)/shard_map/far_grams/pallas_call | solution.py:422
  27.7 0.1 collective-permute-start.9
  27.8 0.6 %collective-permute-done.10.far_msg = f32[72,128]{1,0:T(8,128)S(1)} collective-permute-done((f32[72,128]{1,0:T(8,128)S(1)}, f32[72,128]{1,0:T(8,128)S(1)}, u32[]{:S(2)}, u32[]{:S(2)}) %collective-permute-start.10) | collective-permute-done | bytes 36896 | tf_op jit(solution)/shard_map/ppermute | solution.py:46
  28.4 0.8 %collective-permute-done.11.y_msg = f32[72,128]{1,0:T(8,128)S(1)} collective-permute-done((f32[72,128]{1,0:T(8,128)S(1)}, f32[72,128]{1,0:T(8,128)S(1)}, u32[]{:S(2)}, u32[]{:S(2)}) %collective-permute-start.11) | collective-permute-done | bytes 36896 | tf_op jit(solution)/shard_map/ppermute | solution.py:46
  29.2 0.0 collective-permute-done.12.core_msg
  29.2 2.2 %first_rotation.1 = (f32[128,256]{1,0:T(8,128)S(1)}, f32[128,256]{1,0:T(8,128)S(1)}) custom-call(f32[72,128]{1,0:T(8,128)S(1)} %collective-permute-done.10.far_msg, f32[72,128]{1,0:T(8,128)S(1)} %collective-permute-done.11.y_msg, f32[72,128]{1,0:T(8,128)S(1)} %collective-permute-done.12.core_msg, f32[72,128]{1,0:T(8,128)S(1)} %add.30.own_msg), custom_call_target="tpu_custom_call" | custom-call | flops 4000000000 | bytes 1 | tf_op jit(solution)/shard_map/first_rotation/pallas_call | solution.py:422
  31.3 0.0 collective-permute-done.9.far_peer_ref
  31.3 0.5 %rotated_grams.1 = f32[72,128]{1,0:T(8,128)S(1)} custom-call(f32[256,256]{1,0:T(8,128)S(1)} %get-tuple-element.32.near_ref, f32[256,128]{1,0:T(8,128)S(1)} %far_grams.1.far_ref, f32[256,128]{1,0:T(8,128)S(1)} %collective-permute-done.9.far_peer_ref, f32[128,256]{1,0:T(8,128)S(1)} %get-tuple-element.39.own_t.refs_4_, ...), custom_call_target="tpu_custom_call" | custom-call | flops 1200000000 | bytes 1 | tf_op jit(solution)/shard_map/rotated_grams/pallas_call | solution.py:422
  31.9 0.1 collective-permute-start.19
  32.0 2.6 %collective-permute-start.13 = (f32[72,128]{1,0:T(8,128)S(1)}, f32[72,128]{1,0:T(8,128)S(1)}, u32[]{:S(2)}, u32[]{:S(2)}) collective-permute-start(f32[72,128]{1,0:T(8,128)S(1)} %rotated_grams.1), channel_id=1, source_target_pairs={{0,12},{4,8},{8,4},{12,0},{16,28},{20,24},{24,20},{28,16},{1,13},{... | collective-permute-start | bytes 110600 | tf_op jit(solution)/shard_map/ppermute | solution.py:46
  34.5 0.1 collective-permute-start.14
  34.7 0.9 %collective-permute-start.15 = (f32[72,128]{1,0:T(8,128)S(1)}, f32[72,128]{1,0:T(8,128)S(1)}, u32[]{:S(2)}, u32[]{:S(2)}) collective-permute-start(f32[72,128]{1,0:T(8,128)S(1)} %rotated_grams.1), channel_id=1, source_target_pairs={{0,4},{4,0},{8,12},{12,8},{16,20},{20,16},{24,28},{28,24},{1,5},{5... | collective-permute-start | bytes 110600 | tf_op jit(solution)/shard_map/ppermute | solution.py:46
  35.5 1.4 %collective-permute-done.13 = f32[72,128]{1,0:T(8,128)S(1)} collective-permute-done((f32[72,128]{1,0:T(8,128)S(1)}, f32[72,128]{1,0:T(8,128)S(1)}, u32[]{:S(2)}, u32[]{:S(2)}) %collective-permute-start.13) | collective-permute-done | bytes 36896 | tf_op jit(solution)/shard_map/ppermute | solution.py:46
  36.9 1.6 %collective-permute-done.14 = f32[72,128]{1,0:T(8,128)S(1)} collective-permute-done((f32[72,128]{1,0:T(8,128)S(1)}, f32[72,128]{1,0:T(8,128)S(1)}, u32[]{:S(2)}, u32[]{:S(2)}) %collective-permute-start.14) | collective-permute-done | bytes 36896 | tf_op jit(solution)/shard_map/ppermute | solution.py:46
  38.5 0.1 collective-permute-done.15
  38.6 3.4 %collective-permute-start.16 = (f32[72,128]{1,0:T(8,128)S(1)}, f32[72,128]{1,0:T(8,128)S(1)}, u32[]{:S(2)}, u32[]{:S(2)}) collective-permute-start(f32[72,128]{1,0:T(8,128)S(1)} %add_add_fusion), channel_id=1, source_target_pairs={{0,18},{1,19},{2,16},{3,17},{4,22},{5,23},{6,20},{7,21},{8,26},{9,... | collective-permute-start | bytes 110600 | tf_op jit(solution)/shard_map/ppermute | solution.py:403
  42.0 0.5 %collective-permute-start.17 = (f32[72,128]{1,0:T(8,128)S(1)}, f32[72,128]{1,0:T(8,128)S(1)}, u32[]{:S(2)}, u32[]{:S(2)}) collective-permute-start(f32[72,128]{1,0:T(8,128)S(1)} %add_add_fusion), channel_id=1, source_target_pairs={{0,16},{4,20},{8,24},{12,28},{16,0},{20,4},{24,8},{28,12},{1,17},{... | collective-permute-start | bytes 110600 | tf_op jit(solution)/shard_map/ppermute | solution.py:46
  42.6 0.5 %collective-permute-start.18 = (f32[72,128]{1,0:T(8,128)S(1)}, f32[72,128]{1,0:T(8,128)S(1)}, u32[]{:S(2)}, u32[]{:S(2)}) collective-permute-start(f32[72,128]{1,0:T(8,128)S(1)} %add_add_fusion), channel_id=1, source_target_pairs={{0,2},{1,3},{2,0},{3,1},{4,6},{5,7},{6,4},{7,5},{8,10},{9,11},{10,... | collective-permute-start | bytes 110600 | tf_op jit(solution)/shard_map/ppermute | solution.py:46
  43.1 0.0 collective-permute-done.19.refs_3_
  43.1 1.4 %turned_blocks.1 = (bf16[2048,256]{1,0:T(8,128)(2,1)S(1)}, bf16[2048,256]{1,0:T(8,128)(2,1)S(1)}) custom-call(f32[2048,128]{1,0:T(8,128)S(1)} %bitcast.7, f32[2048,128]{1,0:T(8,128)S(1)} %collective-permute-done.refs_1_.p_ref, f32[2048,128]{1,0:T(8,128)S(1)} %collective-permute-done.8.far_own.refs_2_, f32[2048,128]{1,0:T(8,128)S(1)} %collective-permute-done.19.refs_3_, ...), custom_call_target="tpu_custom_call" | custom-call | flops 1400000000 | bytes 1 | tf_op jit(solution)/shard_map/turned_blocks/pallas_call | solution.py:422
  44.5 0.0 collective-permute-done.16
  44.5 2.4 %collective-permute-done.17 = f32[72,128]{1,0:T(8,128)S(1)} collective-permute-done((f32[72,128]{1,0:T(8,128)S(1)}, f32[72,128]{1,0:T(8,128)S(1)}, u32[]{:S(2)}, u32[]{:S(2)}) %collective-permute-start.17) | collective-permute-done | bytes 36896 | tf_op jit(solution)/shard_map/ppermute | solution.py:46
  46.9 3.4 %last_rotation.1 = f32[2048,128]{1,0:T(8,128)} custom-call(f32[72,128]{1,0:T(8,128)S(1)} %add.34.own_msg, f32[72,128]{1,0:T(8,128)S(1)} %add.35.y_msg, bf16[2048,256]{1,0:T(8,128)(2,1)S(1)} %get-tuple-element.42.high_ref, bf16[2048,256]{1,0:T(8,128)(2,1)S(1)} %get-tuple-element.46.low_ref), custom_call_target="tpu_custom_call" | custom-call | flops 4000000000 | bytes 1 | tf_op jit(solution)/shard_map/last_rotation/pallas_call | solution.py:490
  (8 shorter events, 0.1 us)
Async XLA Ops:
  0.0 6.3 %copy-start = (f32[8,16,16,128]{3,2,1,0:T(8,128)S(1)}, f32[8,16,16,128]{3,2,1,0:T(8,128)}, u32[]{:S(2)}) copy-start(f32[8,16,16,128]{3,2,1,0:T(8,128)} %param.1) | copy-start | bytes 3145732
  0.0 6.3 %collective-permute-start = (f32[2048,128]{1,0:T(8,128)}, f32[2048,128]{1,0:T(8,128)S(1)}, u32[]{:S(2)}, u32[]{:S(2)}) collective-permute-start(f32[2048,128]{1,0:T(8,128)} %bitcast.2), channel_id=1, source_target_pairs={{0,1},{1,0},{2,3},{3,2},{4,5},{5,4},{6,7},{7,6},{8,9},{9,8},{10,11... | collective-permute-start | bytes 3145736 | tf_op jit(solution)/shard_map/ppermute | solution.py:46
  0.5 26.6 %collective-permute-start.8 = (f32[2048,128]{1,0:T(8,128)}, f32[2048,128]{1,0:T(8,128)S(1)}, u32[]{:S(2)}, u32[]{:S(2)}) collective-permute-start(f32[2048,128]{1,0:T(8,128)} %bitcast.3), channel_id=1, source_target_pairs={{0,2},{1,3},{2,0},{3,1},{4,6},{5,7},{6,4},{7,5},{8,10},{9,11},{10,... | collective-permute-start | bytes 3145736 | tf_op jit(solution)/shard_map/ppermute | solution.py:46
  4.0 5.6 %collective-permute-start.1 = (f32[256,128]{1,0:T(8,128)S(1)}, f32[256,128]{1,0:T(8,128)S(1)}, u32[]{:S(2)}, u32[]{:S(2)}) collective-permute-start(f32[256,128]{1,0:T(8,128)S(1)} %get-tuple-element.27.edge_a), channel_id=1, source_target_pairs={{0,4},{4,0},{8,12},{12,8},{16,20},{20,16},{24,28},{28,24},{1,5},{5... | collective-permute-start | bytes 393224 | tf_op jit(solution)/shard_map/ppermute | solution.py:446
  5.6 4.1 %collective-permute-start.2 = (f32[256,128]{1,0:T(8,128)S(1)}, f32[256,128]{1,0:T(8,128)S(1)}, u32[]{:S(2)}, u32[]{:S(2)}) collective-permute-start(f32[256,128]{1,0:T(8,128)S(1)} %get-tuple-element.28.edge_b), channel_id=1, source_target_pairs={{4,8},{12,16},{20,24},{8,4},{16,12},{24,20},{5,9},{13,17},{21,25},... | collective-permute-start | bytes 393224 | tf_op jit(solution)/shard_map/ppermute | solution.py:447
  10.0 7.6 %collective-permute-start.4 = (f32[72,128]{1,0:T(8,128)S(1)}, f32[72,128]{1,0:T(8,128)S(1)}, u32[]{:S(2)}, u32[]{:S(2)}) collective-permute-start(f32[72,128]{1,0:T(8,128)S(1)} %get-tuple-element.33), channel_id=1, source_target_pairs={{0,12},{4,8},{8,4},{12,0},{16,28},{20,24},{24,20},{28,16},{1,13},{... | collective-permute-start | bytes 110600 | tf_op jit(solution)/shard_map/ppermute | solution.py:46
  15.6 4.0 %collective-permute-start.5 = (f32[72,128]{1,0:T(8,128)S(1)}, f32[72,128]{1,0:T(8,128)S(1)}, u32[]{:S(2)}, u32[]{:S(2)}) collective-permute-start(f32[72,128]{1,0:T(8,128)S(1)} %get-tuple-element.33), channel_id=1, source_target_pairs={{0,8},{4,12},{8,0},{12,4},{16,24},{20,28},{24,16},{28,20},{1,9},{5... | collective-permute-start | bytes 110600 | tf_op jit(solution)/shard_map/ppermute | solution.py:46
  16.1 4.0 %collective-permute-start.6 = (f32[72,128]{1,0:T(8,128)S(1)}, f32[72,128]{1,0:T(8,128)S(1)}, u32[]{:S(2)}, u32[]{:S(2)}) collective-permute-start(f32[72,128]{1,0:T(8,128)S(1)} %get-tuple-element.33), channel_id=1, source_target_pairs={{0,4},{4,0},{8,12},{12,8},{16,20},{20,16},{24,28},{28,24},{1,5},{5... | collective-permute-start | bytes 110600 | tf_op jit(solution)/shard_map/ppermute | solution.py:46
  17.1 5.6 %collective-permute-start.3 = (f32[512,128]{1,0:T(8,128)S(1)}, f32[512,128]{1,0:T(8,128)S(1)}, u32[]{:S(2)}, u32[]{:S(2)}) collective-permute-start(f32[512,128]{1,0:T(8,128)S(1)} %get-tuple-element.31.own_step), channel_id=1, source_target_pairs={{0,1},{1,0},{2,3},{3,2},{4,5},{5,4},{6,7},{7,6},{8,9},{9,8},{10,11... | collective-permute-start | bytes 786440 | tf_op jit(solution)/shard_map/ppermute | solution.py:46
  20.0 4.9 %collective-permute-start.7 = (f32[72,128]{1,0:T(8,128)S(1)}, f32[72,128]{1,0:T(8,128)S(1)}, u32[]{:S(2)}, u32[]{:S(2)}) collective-permute-start(f32[72,128]{1,0:T(8,128)S(1)} %add_add_fusion.1), channel_id=1, source_target_pairs={{0,16},{4,20},{8,24},{12,28},{16,0},{20,4},{24,8},{28,12},{1,17},{... | collective-permute-start | bytes 110600 | tf_op jit(solution)/shard_map/ppermute | solution.py:46
  25.0 3.4 %collective-permute-start.10 = (f32[72,128]{1,0:T(8,128)S(1)}, f32[72,128]{1,0:T(8,128)S(1)}, u32[]{:S(2)}, u32[]{:S(2)}) collective-permute-start(f32[72,128]{1,0:T(8,128)S(1)} %add.30.own_msg), channel_id=1, source_target_pairs={{0,3},{1,2},{2,1},{3,0},{4,7},{5,6},{6,5},{7,4},{8,11},{9,10},{10,... | collective-permute-start | bytes 110600 | tf_op jit(solution)/shard_map/ppermute | solution.py:46
  25.0 4.2 %collective-permute-start.11 = (f32[72,128]{1,0:T(8,128)S(1)}, f32[72,128]{1,0:T(8,128)S(1)}, u32[]{:S(2)}, u32[]{:S(2)}) collective-permute-start(f32[72,128]{1,0:T(8,128)S(1)} %add.30.own_msg), channel_id=1, source_target_pairs={{0,2},{1,3},{2,0},{3,1},{4,6},{5,7},{6,4},{7,5},{8,10},{9,11},{10,... | collective-permute-start | bytes 110600 | tf_op jit(solution)/shard_map/ppermute | solution.py:46
  25.4 3.7 %collective-permute-start.12 = (f32[72,128]{1,0:T(8,128)S(1)}, f32[72,128]{1,0:T(8,128)S(1)}, u32[]{:S(2)}, u32[]{:S(2)}) collective-permute-start(f32[72,128]{1,0:T(8,128)S(1)} %add.30.own_msg), channel_id=1, source_target_pairs={{0,1},{1,0},{2,3},{3,2},{4,5},{5,4},{6,7},{7,6},{8,9},{9,8},{10,11... | collective-permute-start | bytes 110600 | tf_op jit(solution)/shard_map/ppermute | solution.py:46
  27.7 3.6 %collective-permute-start.9 = (f32[256,128]{1,0:T(8,128)S(1)}, f32[256,128]{1,0:T(8,128)S(1)}, u32[]{:S(2)}, u32[]{:S(2)}) collective-permute-start(f32[256,128]{1,0:T(8,128)S(1)} %far_grams.1.far_ref), channel_id=1, source_target_pairs={{0,1},{1,0},{2,3},{3,2},{4,5},{5,4},{6,7},{7,6},{8,9},{9,8},{10,11... | collective-permute-start | bytes 393224 | tf_op jit(solution)/shard_map/ppermute | solution.py:46
  31.9 11.2 %collective-permute-start.19 = (f32[2048,128]{1,0:T(8,128)S(1)}, f32[2048,128]{1,0:T(8,128)S(1)}, u32[]{:S(2)}, u32[]{:S(2)}) collective-permute-start(f32[2048,128]{1,0:T(8,128)S(1)} %collective-permute-done.8.far_own.refs_2_), channel_id=1, source_target_pairs={{0,1},{1,0},{2,3},{3,2},{4,5},{5,4},{6,7},{7,6},{8,9},{9,8},{10,11... | collective-permute-start | bytes 3145736 | tf_op jit(solution)/shard_map/ppermute | solution.py:46
  32.0 4.9 %collective-permute-start.13 = (f32[72,128]{1,0:T(8,128)S(1)}, f32[72,128]{1,0:T(8,128)S(1)}, u32[]{:S(2)}, u32[]{:S(2)}) collective-permute-start(f32[72,128]{1,0:T(8,128)S(1)} %rotated_grams.1), channel_id=1, source_target_pairs={{0,12},{4,8},{8,4},{12,0},{16,28},{20,24},{24,20},{28,16},{1,13},{... | collective-permute-start | bytes 110600 | tf_op jit(solution)/shard_map/ppermute | solution.py:46
  34.5 4.0 %collective-permute-start.14 = (f32[72,128]{1,0:T(8,128)S(1)}, f32[72,128]{1,0:T(8,128)S(1)}, u32[]{:S(2)}, u32[]{:S(2)}) collective-permute-start(f32[72,128]{1,0:T(8,128)S(1)} %rotated_grams.1), channel_id=1, source_target_pairs={{0,8},{4,12},{8,0},{12,4},{16,24},{20,28},{24,16},{28,20},{1,9},{5... | collective-permute-start | bytes 110600 | tf_op jit(solution)/shard_map/ppermute | solution.py:46
  34.7 4.0 %collective-permute-start.15 = (f32[72,128]{1,0:T(8,128)S(1)}, f32[72,128]{1,0:T(8,128)S(1)}, u32[]{:S(2)}, u32[]{:S(2)}) collective-permute-start(f32[72,128]{1,0:T(8,128)S(1)} %rotated_grams.1), channel_id=1, source_target_pairs={{0,4},{4,0},{8,12},{12,8},{16,20},{20,16},{24,28},{28,24},{1,5},{5... | collective-permute-start | bytes 110600 | tf_op jit(solution)/shard_map/ppermute | solution.py:46
  38.6 5.9 %collective-permute-start.16 = (f32[72,128]{1,0:T(8,128)S(1)}, f32[72,128]{1,0:T(8,128)S(1)}, u32[]{:S(2)}, u32[]{:S(2)}) collective-permute-start(f32[72,128]{1,0:T(8,128)S(1)} %add_add_fusion), channel_id=1, source_target_pairs={{0,18},{1,19},{2,16},{3,17},{4,22},{5,23},{6,20},{7,21},{8,26},{9,... | collective-permute-start | bytes 110600 | tf_op jit(solution)/shard_map/ppermute | solution.py:403
  42.0 4.9 %collective-permute-start.17 = (f32[72,128]{1,0:T(8,128)S(1)}, f32[72,128]{1,0:T(8,128)S(1)}, u32[]{:S(2)}, u32[]{:S(2)}) collective-permute-start(f32[72,128]{1,0:T(8,128)S(1)} %add_add_fusion), channel_id=1, source_target_pairs={{0,16},{4,20},{8,24},{12,28},{16,0},{20,4},{24,8},{28,12},{1,17},{... | collective-permute-start | bytes 110600 | tf_op jit(solution)/shard_map/ppermute | solution.py:46
  42.6 4.3 %collective-permute-start.18 = (f32[72,128]{1,0:T(8,128)S(1)}, f32[72,128]{1,0:T(8,128)S(1)}, u32[]{:S(2)}, u32[]{:S(2)}) collective-permute-start(f32[72,128]{1,0:T(8,128)S(1)} %add_add_fusion), channel_id=1, source_target_pairs={{0,2},{1,3},{2,0},{3,1},{4,6},{5,7},{6,4},{7,5},{8,10},{9,11},{10,... | collective-permute-start | bytes 110600 | tf_op jit(solution)/shard_map/ppermute | solution.py:46

commit v6 on v4

--- a/solution.py
+++ b/solution.py
@@ -367,12 +367,15 @@
     return count & (count - 1) == 0
 
 
-def stages_of(count):
-    bits = [1 << bit for bit in range(count.bit_length() - 1)]
+def stages_of(bits):
     pairs = [tuple(bits[k:k + 2]) for k in range(0, len(bits) - 1, 2)]
     if len(bits) % 2 == 0:
         pairs[-1:] = [pairs[-1][:1]]
     return pairs + [(bits[-1],)]
+
+
+def bits_of(count):
+    return [1 << bit for bit in range(count.bit_length() - 1)]
 
 
 def summed_over(value, stages):
@@ -390,7 +393,7 @@
     count = lax.axis_size("space")
     if not power_of_two(count):
         return lax.psum(value, "space")
-    stages = stages_of(count)
+    stages = stages_of(bits_of(count))
     value = summed_over(value, stages[:-1])
     there = exchanged(value, "space", stages[-1][0])
     return lax.optimization_barrier((value, beside_it))[0] + there
@@ -401,7 +404,8 @@
     if not power_of_two(count):
         value = lax.psum(value, "space")
         return value, exchanged(value, "blk", 2)
-    stages = stages_of(count)
+    bits = bits_of(count)
+    stages = stages_of(bits[:1] + bits[2:] + bits[1:2])
     value = summed_over(value, stages[:-1])
     bit = stages[-1][0]
     route = [(i * blocks + j, (i ^ bit) * blocks + (j ^ 2)) for i in range(count) for j in range(blocks)]

time: 50.3 us -> 50.6 us (level)
    ppermute x1, starting transfers between devices: 3.41 us -> 2.04 us  [summed_with_y(): other_there = lax.ppermute(value, ('space', 'blk'), route)]
    ppermute x17, starting transfers between devices: 19.4 us -> 20.7 us  [exchanged(): return lax.ppermute(value, axis, [(i, i ^ mask) for i in range(count)])]
where the time goes in v6:
time: 50.6 us; the launch traced here: 50.5 us
  starting transfers between devices  25 us (49%)
  waiting for transfers between devices  13 us (26%)
  Pallas kernels  12.3 us (24%)
    ppermute x17, starting transfers between devices, exchanged(): return lax.ppermute(value, axis, [(i, i ^ mask) for i in range(count)])  20.7 us
    ppermute x17, waiting for transfers between devices, exchanged(): return lax.ppermute(value, axis, [(i, i ^ mask) for i in range(count)])  10.8 us
    pallas_call x7, Pallas kernels, call(): pl.pallas_call(body, in_specs=[VMEM] * len(inputs), out_specs=[VMEM] * le...  7.99 us
    pallas_call x1, Pallas kernels, shards(): pl.pallas_call(last_kernel, in_specs=[VMEM] * 4, out_specs=pl.BlockSpec(m...  3.31 us
    ppermute x1, waiting for transfers between devices, shards(): near_a = lax.ppermute(edge_a, 'space', route_a)  2.23 us
    ppermute x1, starting transfers between devices, summed_with_y(): other_there = lax.ppermute(value, ('space', 'blk'), route)  2.04 us
    ppermute x1, starting transfers between devices, shards(): near_a = lax.ppermute(edge_a, 'space', route_a)  1.56 us
  transfers between devices with their start and end apart: 20, of which 12 were waited for; matrix products, arithmetic and copies ran while one was open for 0% of the time, Pallas kernels for 17%

profile of v6, /device:TPU:0, one launch (start us, length us, event | category | flops | bytes accessed | tf_op | source)
XLA Modules:
  0.0 50.5 jit_solution(7978836205353345293)
XLA Ops:
  0.0 0.5 collective-permute-start
  0.5 2.6 %collective-permute-start.8 = (f32[2048,128]{1,0:T(8,128)}, f32[2048,128]{1,0:T(8,128)S(1)}, u32[]{:S(2)}, u32[]{:S(2)}) collective-permute-start(f32[2048,128]{1,0:T(8,128)} %bitcast.3), channel_id=1, source_target_pairs={{0,2},{1,3},{2,0},{3,1},{4,6},{5,7},{6,4},{7,5},{8,10},{9,11},{10,... | collective-permute-start | bytes 3145736 | tf_op jit(solution)/shard_map/ppermute | solution.py:46
  3.0 1.0 %edges.1 = (f32[256,128]{1,0:T(8,128)S(1)}, f32[256,128]{1,0:T(8,128)S(1)}) custom-call(f32[2048,128]{1,0:T(8,128)} %bitcast.4), custom_call_target="tpu_custom_call" | custom-call | flops 100000000 | bytes 1 | tf_op jit(solution)/shard_map/edges/pallas_call | solution.py:445
  4.0 1.6 %collective-permute-start.1 = (f32[256,128]{1,0:T(8,128)S(1)}, f32[256,128]{1,0:T(8,128)S(1)}, u32[]{:S(2)}, u32[]{:S(2)}) collective-permute-start(f32[256,128]{1,0:T(8,128)S(1)} %get-tuple-element.27.edge_a), channel_id=1, source_target_pairs={{0,4},{4,0},{8,12},{12,8},{16,20},{20,16},{24,28},{28,24},{1,5},{5... | collective-permute-start | bytes 393224 | tf_op jit(solution)/shard_map/ppermute | solution.py:455
  5.6 0.7 %collective-permute-start.2 = (f32[256,128]{1,0:T(8,128)S(1)}, f32[256,128]{1,0:T(8,128)S(1)}, u32[]{:S(2)}, u32[]{:S(2)}) collective-permute-start(f32[256,128]{1,0:T(8,128)S(1)} %get-tuple-element.28.edge_b), channel_id=1, source_target_pairs={{4,8},{12,16},{20,24},{8,4},{16,12},{24,20},{5,9},{13,17},{21,25},... | collective-permute-start | bytes 393224 | tf_op jit(solution)/shard_map/ppermute | solution.py:456
  6.3 0.0 collective-permute-done.refs_1_.p_ref
  6.3 1.2 %inner_grams.1 = (f32[2048,128]{1,0:T(8,128)S(1)}, f32[128,128]{1,0:T(8,128)S(1)}, f32[8,128]{1,0:T(8,128)S(1)}) custom-call(f32[2048,128]{1,0:T(8,128)S(1)} %bitcast.5, f32[2048,128]{1,0:T(8,128)S(1)} %collective-permute-done.refs_1_.p_ref), custom_call_target="tpu_custom_call" | custom-call | flops 100000000 | bytes 1 | tf_op jit(solution)/shard_map/inner_grams/pallas_call | solution.py:431
  7.4 2.2 %collective-permute-done.1.near_a = f32[256,128]{1,0:T(8,128)S(1)} collective-permute-done((f32[256,128]{1,0:T(8,128)S(1)}, f32[256,128]{1,0:T(8,128)S(1)}, u32[]{:S(2)}, u32[]{:S(2)}) %collective-permute-start.1) | collective-permute-done | bytes 131104 | tf_op jit(solution)/shard_map/ppermute | solution.py:455
  9.7 0.0 collective-permute-done.2.near_b
  9.7 0.3 edge_grams.1
  10.0 5.6 %collective-permute-start.4 = (f32[72,128]{1,0:T(8,128)S(1)}, f32[72,128]{1,0:T(8,128)S(1)}, u32[]{:S(2)}, u32[]{:S(2)}) collective-permute-start(f32[72,128]{1,0:T(8,128)S(1)} %get-tuple-element.33), channel_id=1, source_target_pairs={{0,12},{4,8},{8,4},{12,0},{16,28},{20,24},{24,20},{28,16},{1,13},{... | collective-permute-start | bytes 110600 | tf_op jit(solution)/shard_map/ppermute | solution.py:46
  15.6 0.5 collective-permute-start.5
  16.1 1.0 %collective-permute-start.6 = (f32[72,128]{1,0:T(8,128)S(1)}, f32[72,128]{1,0:T(8,128)S(1)}, u32[]{:S(2)}, u32[]{:S(2)}) collective-permute-start(f32[72,128]{1,0:T(8,128)S(1)} %get-tuple-element.33), channel_id=1, source_target_pairs={{0,4},{4,0},{8,12},{12,8},{16,20},{20,16},{24,28},{28,24},{1,5},{5... | collective-permute-start | bytes 110600 | tf_op jit(solution)/shard_map/ppermute | solution.py:46
  17.1 0.0 collective-permute-start.3
  17.1 0.5 %collective-permute-done.4 = f32[72,128]{1,0:T(8,128)S(1)} collective-permute-done((f32[72,128]{1,0:T(8,128)S(1)}, f32[72,128]{1,0:T(8,128)S(1)}, u32[]{:S(2)}, u32[]{:S(2)}) %collective-permute-start.4) | collective-permute-done | bytes 36896 | tf_op jit(solution)/shard_map/ppermute | solution.py:46
  17.7 1.9 %collective-permute-done.5 = f32[72,128]{1,0:T(8,128)S(1)} collective-permute-done((f32[72,128]{1,0:T(8,128)S(1)}, f32[72,128]{1,0:T(8,128)S(1)}, u32[]{:S(2)}, u32[]{:S(2)}) %collective-permute-start.5) | collective-permute-done | bytes 36896 | tf_op jit(solution)/shard_map/ppermute | solution.py:46
  19.6 0.5 collective-permute-done.6
  20.0 2.7 %collective-permute-start.7 = (f32[72,128]{1,0:T(8,128)S(1)}, f32[72,128]{1,0:T(8,128)S(1)}, u32[]{:S(2)}, u32[]{:S(2)}) collective-permute-start(f32[72,128]{1,0:T(8,128)S(1)} %add_add_fusion.1), channel_id=1, source_target_pairs={{0,16},{4,20},{8,24},{12,28},{16,0},{20,4},{24,8},{28,12},{1,17},{... | collective-permute-start | bytes 110600 | tf_op jit(solution)/shard_map/ppermute | solution.py:46
  22.7 0.0 collective-permute-done.3.peer_step
  22.7 1.8 %near_grams.1 = (f32[256,256]{1,0:T(8,128)S(1)}, bf16[256,2048]{1,0:T(8,128)(2,1)S(1)}, bf16[256,2048]{1,0:T(8,128)(2,1)S(1)}) custom-call(f32[2048,128]{1,0:T(8,128)S(1)} %get-tuple-element.26.wo, f32[512,128]{1,0:T(8,128)S(1)} %get-tuple-element.31.own_step, f32[512,128]{1,0:T(8,128)S(1)} %collective-permute-done.3.peer_step, f32[2048,128]{1,0:T(8,128)S(1)} %bitcast.6, ...), custom_call_target="tpu_custom_call" | custom-call | flops 2500000000 | bytes 1 | tf_op jit(solution)/shard_map/near_grams/pallas_call | solution.py:431
  24.5 0.4 collective-permute-done.7
  25.0 0.0 collective-permute-start.10
  25.0 0.4 collective-permute-start.11
  25.4 1.4 %collective-permute-start.12 = (f32[72,128]{1,0:T(8,128)S(1)}, f32[72,128]{1,0:T(8,128)S(1)}, u32[]{:S(2)}, u32[]{:S(2)}) collective-permute-start(f32[72,128]{1,0:T(8,128)S(1)} %add.30.own_msg), channel_id=1, source_target_pairs={{0,1},{1,0},{2,3},{3,2},{4,5},{5,4},{6,7},{7,6},{8,9},{9,8},{10,11... | collective-permute-start | bytes 110600 | tf_op jit(solution)/shard_map/ppermute | solution.py:46
  26.8 0.2 collective-permute-done.8.far_own.refs_2_
  27.0 0.7 %far_grams.1.far_ref = f32[256,128]{1,0:T(8,128)S(1)} custom-call(bf16[256,2048]{1,0:T(8,128)(2,1)S(1)} %get-tuple-element.35.high_t, bf16[256,2048]{1,0:T(8,128)(2,1)S(1)} %get-tuple-element.36.low_t, f32[2048,128]{1,0:T(8,128)S(1)} %collective-permute-done.8.far_own.refs_2_), custom_call_target="tpu_custom_call" | custom-call | flops 700000000 | bytes 1 | tf_op jit(solution)/shard_map/far_grams/pallas_call | solution.py:431
  27.7 0.1 collective-permute-start.9
  27.8 0.6 %collective-permute-done.10.far_msg = f32[72,128]{1,0:T(8,128)S(1)} collective-permute-done((f32[72,128]{1,0:T(8,128)S(1)}, f32[72,128]{1,0:T(8,128)S(1)}, u32[]{:S(2)}, u32[]{:S(2)}) %collective-permute-start.10) | collective-permute-done | bytes 36896 | tf_op jit(solution)/shard_map/ppermute | solution.py:46
  28.4 0.8 %collective-permute-done.11.y_msg = f32[72,128]{1,0:T(8,128)S(1)} collective-permute-done((f32[72,128]{1,0:T(8,128)S(1)}, f32[72,128]{1,0:T(8,128)S(1)}, u32[]{:S(2)}, u32[]{:S(2)}) %collective-permute-start.11) | collective-permute-done | bytes 36896 | tf_op jit(solution)/shard_map/ppermute | solution.py:46
  29.2 0.0 collective-permute-done.12.core_msg
  29.2 2.1 %first_rotation.1 = (f32[128,256]{1,0:T(8,128)S(1)}, f32[128,256]{1,0:T(8,128)S(1)}) custom-call(f32[72,128]{1,0:T(8,128)S(1)} %collective-permute-done.10.far_msg, f32[72,128]{1,0:T(8,128)S(1)} %collective-permute-done.11.y_msg, f32[72,128]{1,0:T(8,128)S(1)} %collective-permute-done.12.core_msg, f32[72,128]{1,0:T(8,128)S(1)} %add.30.own_msg), custom_call_target="tpu_custom_call" | custom-call | flops 4000000000 | bytes 1 | tf_op jit(solution)/shard_map/first_rotation/pallas_call | solution.py:431
  31.3 0.0 collective-permute-done.9.far_peer_ref
  31.3 0.5 rotated_grams.1
  31.7 0.1 collective-permute-start.19
  31.8 3.6 %collective-permute-start.13 = (f32[72,128]{1,0:T(8,128)S(1)}, f32[72,128]{1,0:T(8,128)S(1)}, u32[]{:S(2)}, u32[]{:S(2)}) collective-permute-start(f32[72,128]{1,0:T(8,128)S(1)} %rotated_grams.1), channel_id=1, source_target_pairs={{0,20},{4,16},{8,28},{12,24},{16,4},{20,0},{24,12},{28,8},{1,21},{... | collective-permute-start | bytes 110600 | tf_op jit(solution)/shard_map/ppermute | solution.py:46
  35.4 0.0 collective-permute-start.14
  35.4 0.8 %collective-permute-start.15 = (f32[72,128]{1,0:T(8,128)S(1)}, f32[72,128]{1,0:T(8,128)S(1)}, u32[]{:S(2)}, u32[]{:S(2)}) collective-permute-start(f32[72,128]{1,0:T(8,128)S(1)} %rotated_grams.1), channel_id=1, source_target_pairs={{0,4},{4,0},{8,12},{12,8},{16,20},{20,16},{24,28},{28,24},{1,5},{5... | collective-permute-start | bytes 110600 | tf_op jit(solution)/shard_map/ppermute | solution.py:46
  36.3 1.4 %collective-permute-done.13 = f32[72,128]{1,0:T(8,128)S(1)} collective-permute-done((f32[72,128]{1,0:T(8,128)S(1)}, f32[72,128]{1,0:T(8,128)S(1)}, u32[]{:S(2)}, u32[]{:S(2)}) %collective-permute-start.13) | collective-permute-done | bytes 36896 | tf_op jit(solution)/shard_map/ppermute | solution.py:46
  37.6 2.6 %collective-permute-done.14 = f32[72,128]{1,0:T(8,128)S(1)} collective-permute-done((f32[72,128]{1,0:T(8,128)S(1)}, f32[72,128]{1,0:T(8,128)S(1)}, u32[]{:S(2)}, u32[]{:S(2)}) %collective-permute-start.14) | collective-permute-done | bytes 36896 | tf_op jit(solution)/shard_map/ppermute | solution.py:46
  40.3 0.0 collective-permute-done.15
  40.3 2.0 %collective-permute-start.16 = (f32[72,128]{1,0:T(8,128)S(1)}, f32[72,128]{1,0:T(8,128)S(1)}, u32[]{:S(2)}, u32[]{:S(2)}) collective-permute-start(f32[72,128]{1,0:T(8,128)S(1)} %add_add_fusion), channel_id=1, source_target_pairs={{0,10},{1,11},{2,8},{3,9},{4,14},{5,15},{6,12},{7,13},{8,2},{9,3},... | collective-permute-start | bytes 110600 | tf_op jit(solution)/shard_map/ppermute | solution.py:412
  42.3 0.8 %collective-permute-start.17 = (f32[72,128]{1,0:T(8,128)S(1)}, f32[72,128]{1,0:T(8,128)S(1)}, u32[]{:S(2)}, u32[]{:S(2)}) collective-permute-start(f32[72,128]{1,0:T(8,128)S(1)} %add_add_fusion), channel_id=1, source_target_pairs={{0,8},{4,12},{8,0},{12,4},{16,24},{20,28},{24,16},{28,20},{1,9},{5... | collective-permute-start | bytes 110600 | tf_op jit(solution)/shard_map/ppermute | solution.py:46
  43.2 0.7 %collective-permute-start.18 = (f32[72,128]{1,0:T(8,128)S(1)}, f32[72,128]{1,0:T(8,128)S(1)}, u32[]{:S(2)}, u32[]{:S(2)}) collective-permute-start(f32[72,128]{1,0:T(8,128)S(1)} %add_add_fusion), channel_id=1, source_target_pairs={{0,2},{1,3},{2,0},{3,1},{4,6},{5,7},{6,4},{7,5},{8,10},{9,11},{10,... | collective-permute-start | bytes 110600 | tf_op jit(solution)/shard_map/ppermute | solution.py:46
  43.9 1.4 %turned_blocks.1 = (bf16[2048,256]{1,0:T(8,128)(2,1)S(1)}, bf16[2048,256]{1,0:T(8,128)(2,1)S(1)}) custom-call(f32[2048,128]{1,0:T(8,128)S(1)} %bitcast.7, f32[2048,128]{1,0:T(8,128)S(1)} %collective-permute-done.refs_1_.p_ref, f32[2048,128]{1,0:T(8,128)S(1)} %collective-permute-done.8.far_own.refs_2_, f32[2048,128]{1,0:T(8,128)S(1)} %collective-permute-done.19.refs_3_, ...), custom_call_target="tpu_custom_call" | custom-call | flops 1400000000 | bytes 1 | tf_op jit(solution)/shard_map/turned_blocks/pallas_call | solution.py:431
  45.3 0.0 collective-permute-done.16
  45.3 1.0 %collective-permute-done.17 = f32[72,128]{1,0:T(8,128)S(1)} collective-permute-done((f32[72,128]{1,0:T(8,128)S(1)}, f32[72,128]{1,0:T(8,128)S(1)}, u32[]{:S(2)}, u32[]{:S(2)}) %collective-permute-start.17) | collective-permute-done | bytes 36896 | tf_op jit(solution)/shard_map/ppermute | solution.py:46
  46.3 0.8 %collective-permute-done.18 = f32[72,128]{1,0:T(8,128)S(1)} collective-permute-done((f32[72,128]{1,0:T(8,128)S(1)}, f32[72,128]{1,0:T(8,128)S(1)}, u32[]{:S(2)}, u32[]{:S(2)}) %collective-permute-start.18) | collective-permute-done | bytes 36896 | tf_op jit(solution)/shard_map/ppermute | solution.py:46
  47.2 3.3 %last_rotation.1 = f32[2048,128]{1,0:T(8,128)} custom-call(f32[72,128]{1,0:T(8,128)S(1)} %add.34.own_msg, f32[72,128]{1,0:T(8,128)S(1)} %add.35.y_msg, bf16[2048,256]{1,0:T(8,128)(2,1)S(1)} %get-tuple-element.42.high_ref, bf16[2048,256]{1,0:T(8,128)(2,1)S(1)} %get-tuple-element.46.low_ref), custom_call_target="tpu_custom_call" | custom-call | flops 4000000000 | bytes 1 | tf_op jit(solution)/shard_map/last_rotation/pallas_call | solution.py:499
  (8 shorter events, 0.0 us)
Async XLA Ops:
  0.0 6.3 %copy-start = (f32[8,16,16,128]{3,2,1,0:T(8,128)S(1)}, f32[8,16,16,128]{3,2,1,0:T(8,128)}, u32[]{:S(2)}) copy-start(f32[8,16,16,128]{3,2,1,0:T(8,128)} %param.1) | copy-start | bytes 3145732
  0.0 6.3 %collective-permute-start = (f32[2048,128]{1,0:T(8,128)}, f32[2048,128]{1,0:T(8,128)S(1)}, u32[]{:S(2)}, u32[]{:S(2)}) collective-permute-start(f32[2048,128]{1,0:T(8,128)} %bitcast.2), channel_id=1, source_target_pairs={{0,1},{1,0},{2,3},{3,2},{4,5},{5,4},{6,7},{7,6},{8,9},{9,8},{10,11... | collective-permute-start | bytes 3145736 | tf_op jit(solution)/shard_map/ppermute | solution.py:46
  0.5 26.6 %collective-permute-start.8 = (f32[2048,128]{1,0:T(8,128)}, f32[2048,128]{1,0:T(8,128)S(1)}, u32[]{:S(2)}, u32[]{:S(2)}) collective-permute-start(f32[2048,128]{1,0:T(8,128)} %bitcast.3), channel_id=1, source_target_pairs={{0,2},{1,3},{2,0},{3,1},{4,6},{5,7},{6,4},{7,5},{8,10},{9,11},{10,... | collective-permute-start | bytes 3145736 | tf_op jit(solution)/shard_map/ppermute | solution.py:46
  4.0 5.6 %collective-permute-start.1 = (f32[256,128]{1,0:T(8,128)S(1)}, f32[256,128]{1,0:T(8,128)S(1)}, u32[]{:S(2)}, u32[]{:S(2)}) collective-permute-start(f32[256,128]{1,0:T(8,128)S(1)} %get-tuple-element.27.edge_a), channel_id=1, source_target_pairs={{0,4},{4,0},{8,12},{12,8},{16,20},{20,16},{24,28},{28,24},{1,5},{5... | collective-permute-start | bytes 393224 | tf_op jit(solution)/shard_map/ppermute | solution.py:455
  5.6 4.1 %collective-permute-start.2 = (f32[256,128]{1,0:T(8,128)S(1)}, f32[256,128]{1,0:T(8,128)S(1)}, u32[]{:S(2)}, u32[]{:S(2)}) collective-permute-start(f32[256,128]{1,0:T(8,128)S(1)} %get-tuple-element.28.edge_b), channel_id=1, source_target_pairs={{4,8},{12,16},{20,24},{8,4},{16,12},{24,20},{5,9},{13,17},{21,25},... | collective-permute-start | bytes 393224 | tf_op jit(solution)/shard_map/ppermute | solution.py:456
  10.0 7.6 %collective-permute-start.4 = (f32[72,128]{1,0:T(8,128)S(1)}, f32[72,128]{1,0:T(8,128)S(1)}, u32[]{:S(2)}, u32[]{:S(2)}) collective-permute-start(f32[72,128]{1,0:T(8,128)S(1)} %get-tuple-element.33), channel_id=1, source_target_pairs={{0,12},{4,8},{8,4},{12,0},{16,28},{20,24},{24,20},{28,16},{1,13},{... | collective-permute-start | bytes 110600 | tf_op jit(solution)/shard_map/ppermute | solution.py:46
  15.6 4.0 %collective-permute-start.5 = (f32[72,128]{1,0:T(8,128)S(1)}, f32[72,128]{1,0:T(8,128)S(1)}, u32[]{:S(2)}, u32[]{:S(2)}) collective-permute-start(f32[72,128]{1,0:T(8,128)S(1)} %get-tuple-element.33), channel_id=1, source_target_pairs={{0,8},{4,12},{8,0},{12,4},{16,24},{20,28},{24,16},{28,20},{1,9},{5... | collective-permute-start | bytes 110600 | tf_op jit(solution)/shard_map/ppermute | solution.py:46
  16.1 4.0 %collective-permute-start.6 = (f32[72,128]{1,0:T(8,128)S(1)}, f32[72,128]{1,0:T(8,128)S(1)}, u32[]{:S(2)}, u32[]{:S(2)}) collective-permute-start(f32[72,128]{1,0:T(8,128)S(1)} %get-tuple-element.33), channel_id=1, source_target_pairs={{0,4},{4,0},{8,12},{12,8},{16,20},{20,16},{24,28},{28,24},{1,5},{5... | collective-permute-start | bytes 110600 | tf_op jit(solution)/shard_map/ppermute | solution.py:46
  17.1 5.6 %collective-permute-start.3 = (f32[512,128]{1,0:T(8,128)S(1)}, f32[512,128]{1,0:T(8,128)S(1)}, u32[]{:S(2)}, u32[]{:S(2)}) collective-permute-start(f32[512,128]{1,0:T(8,128)S(1)} %get-tuple-element.31.own_step), channel_id=1, source_target_pairs={{0,1},{1,0},{2,3},{3,2},{4,5},{5,4},{6,7},{7,6},{8,9},{9,8},{10,11... | collective-permute-start | bytes 786440 | tf_op jit(solution)/shard_map/ppermute | solution.py:46
  20.0 4.9 %collective-permute-start.7 = (f32[72,128]{1,0:T(8,128)S(1)}, f32[72,128]{1,0:T(8,128)S(1)}, u32[]{:S(2)}, u32[]{:S(2)}) collective-permute-start(f32[72,128]{1,0:T(8,128)S(1)} %add_add_fusion.1), channel_id=1, source_target_pairs={{0,16},{4,20},{8,24},{12,28},{16,0},{20,4},{24,8},{28,12},{1,17},{... | collective-permute-start | bytes 110600 | tf_op jit(solution)/shard_map/ppermute | solution.py:46
  25.0 3.4 %collective-permute-start.10 = (f32[72,128]{1,0:T(8,128)S(1)}, f32[72,128]{1,0:T(8,128)S(1)}, u32[]{:S(2)}, u32[]{:S(2)}) collective-permute-start(f32[72,128]{1,0:T(8,128)S(1)} %add.30.own_msg), channel_id=1, source_target_pairs={{0,3},{1,2},{2,1},{3,0},{4,7},{5,6},{6,5},{7,4},{8,11},{9,10},{10,... | collective-permute-start | bytes 110600 | tf_op jit(solution)/shard_map/ppermute | solution.py:46
  25.0 4.2 %collective-permute-start.11 = (f32[72,128]{1,0:T(8,128)S(1)}, f32[72,128]{1,0:T(8,128)S(1)}, u32[]{:S(2)}, u32[]{:S(2)}) collective-permute-start(f32[72,128]{1,0:T(8,128)S(1)} %add.30.own_msg), channel_id=1, source_target_pairs={{0,2},{1,3},{2,0},{3,1},{4,6},{5,7},{6,4},{7,5},{8,10},{9,11},{10,... | collective-permute-start | bytes 110600 | tf_op jit(solution)/shard_map/ppermute | solution.py:46
  25.4 3.7 %collective-permute-start.12 = (f32[72,128]{1,0:T(8,128)S(1)}, f32[72,128]{1,0:T(8,128)S(1)}, u32[]{:S(2)}, u32[]{:S(2)}) collective-permute-start(f32[72,128]{1,0:T(8,128)S(1)} %add.30.own_msg), channel_id=1, source_target_pairs={{0,1},{1,0},{2,3},{3,2},{4,5},{5,4},{6,7},{7,6},{8,9},{9,8},{10,11... | collective-permute-start | bytes 110600 | tf_op jit(solution)/shard_map/ppermute | solution.py:46
  27.7 3.5 %collective-permute-start.9 = (f32[256,128]{1,0:T(8,128)S(1)}, f32[256,128]{1,0:T(8,128)S(1)}, u32[]{:S(2)}, u32[]{:S(2)}) collective-permute-start(f32[256,128]{1,0:T(8,128)S(1)} %far_grams.1.far_ref), channel_id=1, source_target_pairs={{0,1},{1,0},{2,3},{3,2},{4,5},{5,4},{6,7},{7,6},{8,9},{9,8},{10,11... | collective-permute-start | bytes 393224 | tf_op jit(solution)/shard_map/ppermute | solution.py:46
  31.7 12.1 %collective-permute-start.19 = (f32[2048,128]{1,0:T(8,128)S(1)}, f32[2048,128]{1,0:T(8,128)S(1)}, u32[]{:S(2)}, u32[]{:S(2)}) collective-permute-start(f32[2048,128]{1,0:T(8,128)S(1)} %collective-permute-done.8.far_own.refs_2_), channel_id=1, source_target_pairs={{0,1},{1,0},{2,3},{3,2},{4,5},{5,4},{6,7},{7,6},{8,9},{9,8},{10,11... | collective-permute-start | bytes 3145736 | tf_op jit(solution)/shard_map/ppermute | solution.py:46
  31.8 5.8 %collective-permute-start.13 = (f32[72,128]{1,0:T(8,128)S(1)}, f32[72,128]{1,0:T(8,128)S(1)}, u32[]{:S(2)}, u32[]{:S(2)}) collective-permute-start(f32[72,128]{1,0:T(8,128)S(1)} %rotated_grams.1), channel_id=1, source_target_pairs={{0,20},{4,16},{8,28},{12,24},{16,4},{20,0},{24,12},{28,8},{1,21},{... | collective-permute-start | bytes 110600 | tf_op jit(solution)/shard_map/ppermute | solution.py:46
  35.4 4.9 %collective-permute-start.14 = (f32[72,128]{1,0:T(8,128)S(1)}, f32[72,128]{1,0:T(8,128)S(1)}, u32[]{:S(2)}, u32[]{:S(2)}) collective-permute-start(f32[72,128]{1,0:T(8,128)S(1)} %rotated_grams.1), channel_id=1, source_target_pairs={{0,16},{4,20},{8,24},{12,28},{16,0},{20,4},{24,8},{28,12},{1,17},{... | collective-permute-start | bytes 110600 | tf_op jit(solution)/shard_map/ppermute | solution.py:46
  35.4 4.9 %collective-permute-start.15 = (f32[72,128]{1,0:T(8,128)S(1)}, f32[72,128]{1,0:T(8,128)S(1)}, u32[]{:S(2)}, u32[]{:S(2)}) collective-permute-start(f32[72,128]{1,0:T(8,128)S(1)} %rotated_grams.1), channel_id=1, source_target_pairs={{0,4},{4,0},{8,12},{12,8},{16,20},{20,16},{24,28},{28,24},{1,5},{5... | collective-permute-start | bytes 110600 | tf_op jit(solution)/shard_map/ppermute | solution.py:46
  40.3 5.0 %collective-permute-start.16 = (f32[72,128]{1,0:T(8,128)S(1)}, f32[72,128]{1,0:T(8,128)S(1)}, u32[]{:S(2)}, u32[]{:S(2)}) collective-permute-start(f32[72,128]{1,0:T(8,128)S(1)} %add_add_fusion), channel_id=1, source_target_pairs={{0,10},{1,11},{2,8},{3,9},{4,14},{5,15},{6,12},{7,13},{8,2},{9,3},... | collective-permute-start | bytes 110600 | tf_op jit(solution)/shard_map/ppermute | solution.py:412
  42.3 4.0 %collective-permute-start.17 = (f32[72,128]{1,0:T(8,128)S(1)}, f32[72,128]{1,0:T(8,128)S(1)}, u32[]{:S(2)}, u32[]{:S(2)}) collective-permute-start(f32[72,128]{1,0:T(8,128)S(1)} %add_add_fusion), channel_id=1, source_target_pairs={{0,8},{4,12},{8,0},{12,4},{16,24},{20,28},{24,16},{28,20},{1,9},{5... | collective-permute-start | bytes 110600 | tf_op jit(solution)/shard_map/ppermute | solution.py:46
  43.2 4.0 %collective-permute-start.18 = (f32[72,128]{1,0:T(8,128)S(1)}, f32[72,128]{1,0:T(8,128)S(1)}, u32[]{:S(2)}, u32[]{:S(2)}) collective-permute-start(f32[72,128]{1,0:T(8,128)S(1)} %add_add_fusion), channel_id=1, source_target_pairs={{0,2},{1,3},{2,0},{3,1},{4,6},{5,7},{6,4},{7,5},{8,10},{9,11},{10,... | collective-permute-start | bytes 110600 | tf_op jit(solution)/shard_map/ppermute | solution.py:46

commit v7 on v4

--- a/solution.py
+++ b/solution.py
@@ -13,6 +13,7 @@
 PARAMS = pltpu.CompilerParams(vmem_limit_bytes=40 * 2**20)
 CLOSE = 2e-3
 STEPS = 5
+MORE = 8
 CHUNKS = 1
 
 
@@ -280,7 +281,9 @@
 
     size = refined([both[:, :width] for both in boths])
     lax.while_loop(
-        lambda size: size > CLOSE, lambda _: refined([x_ref[k] for k in range(len(pairs))]), size
+        lambda carry: (carry[0] > CLOSE) & (carry[1] < MORE),
+        lambda carry: (refined([x_ref[k] for k in range(len(pairs))]), carry[1] + 1),
+        (size, jnp.int32(0)),
     )
 
 

time: 50.3 us -> 50.3 us (level)
  no operation moved by 1% of the time
where the time goes in v7:
time: 50.3 us; the launch traced here: 50.1 us
  starting transfers between devices  25 us (50%)
  waiting for transfers between devices  12.6 us (25%)
  Pallas kernels  12.3 us (24%)
    ppermute x17, starting transfers between devices, exchanged(): return lax.ppermute(value, axis, [(i, i ^ mask) for i in range(count)])  19.4 us
    ppermute x17, waiting for transfers between devices, exchanged(): return lax.ppermute(value, axis, [(i, i ^ mask) for i in range(count)])  10.4 us
    pallas_call x7, Pallas kernels, call(): pl.pallas_call(body, in_specs=[VMEM] * len(inputs), out_specs=[VMEM] * le...  7.99 us
    ppermute x1, starting transfers between devices, summed_with_y(): other_there = lax.ppermute(value, ('space', 'blk'), route)  3.41 us
    pallas_call x1, Pallas kernels, shards(): pl.pallas_call(last_kernel, in_specs=[VMEM] * 4, out_specs=pl.BlockSpec(m...  3.31 us
    ppermute x1, waiting for transfers between devices, shards(): near_a = lax.ppermute(edge_a, 'space', route_a)  2.23 us
    ppermute x1, starting transfers between devices, shards(): near_a = lax.ppermute(edge_a, 'space', route_a)  1.56 us
  transfers between devices with their start and end apart: 20, of which 12 were waited for; matrix products, arithmetic and copies ran while one was open for 0% of the time, Pallas kernels for 17%

profile of v7, /device:TPU:0, one launch (start us, length us, event | category | flops | bytes accessed | tf_op | source)
XLA Modules:
  0.0 50.1 jit_solution(13137578964675048847)
XLA Ops:
  0.0 0.5 collective-permute-start
  0.5 2.6 %collective-permute-start.8 = (f32[2048,128]{1,0:T(8,128)}, f32[2048,128]{1,0:T(8,128)S(1)}, u32[]{:S(2)}, u32[]{:S(2)}) collective-permute-start(f32[2048,128]{1,0:T(8,128)} %bitcast.3), channel_id=1, source_target_pairs={{0,2},{1,3},{2,0},{3,1},{4,6},{5,7},{6,4},{7,5},{8,10},{9,11},{10,... | collective-permute-start | bytes 3145736 | tf_op jit(solution)/shard_map/ppermute | solution.py:47
  3.0 1.0 %edges.1 = (f32[256,128]{1,0:T(8,128)S(1)}, f32[256,128]{1,0:T(8,128)S(1)}) custom-call(f32[2048,128]{1,0:T(8,128)} %bitcast.4), custom_call_target="tpu_custom_call" | custom-call | flops 100000000 | bytes 1 | tf_op jit(solution)/shard_map/edges/pallas_call | solution.py:444
  4.0 1.6 %collective-permute-start.1 = (f32[256,128]{1,0:T(8,128)S(1)}, f32[256,128]{1,0:T(8,128)S(1)}, u32[]{:S(2)}, u32[]{:S(2)}) collective-permute-start(f32[256,128]{1,0:T(8,128)S(1)} %get-tuple-element.27.edge_a), channel_id=1, source_target_pairs={{0,4},{4,0},{8,12},{12,8},{16,20},{20,16},{24,28},{28,24},{1,5},{5... | collective-permute-start | bytes 393224 | tf_op jit(solution)/shard_map/ppermute | solution.py:454
  5.6 0.7 %collective-permute-start.2 = (f32[256,128]{1,0:T(8,128)S(1)}, f32[256,128]{1,0:T(8,128)S(1)}, u32[]{:S(2)}, u32[]{:S(2)}) collective-permute-start(f32[256,128]{1,0:T(8,128)S(1)} %get-tuple-element.28.edge_b), channel_id=1, source_target_pairs={{4,8},{12,16},{20,24},{8,4},{16,12},{24,20},{5,9},{13,17},{21,25},... | collective-permute-start | bytes 393224 | tf_op jit(solution)/shard_map/ppermute | solution.py:455
  6.3 0.0 collective-permute-done.refs_1_.p_ref
  6.3 1.2 %inner_grams.1 = (f32[2048,128]{1,0:T(8,128)S(1)}, f32[128,128]{1,0:T(8,128)S(1)}, f32[8,128]{1,0:T(8,128)S(1)}) custom-call(f32[2048,128]{1,0:T(8,128)S(1)} %bitcast.5, f32[2048,128]{1,0:T(8,128)S(1)} %collective-permute-done.refs_1_.p_ref), custom_call_target="tpu_custom_call" | custom-call | flops 100000000 | bytes 1 | tf_op jit(solution)/shard_map/inner_grams/pallas_call | solution.py:430
  7.4 2.2 %collective-permute-done.1.near_a = f32[256,128]{1,0:T(8,128)S(1)} collective-permute-done((f32[256,128]{1,0:T(8,128)S(1)}, f32[256,128]{1,0:T(8,128)S(1)}, u32[]{:S(2)}, u32[]{:S(2)}) %collective-permute-start.1) | collective-permute-done | bytes 131104 | tf_op jit(solution)/shard_map/ppermute | solution.py:454
  9.7 0.0 collective-permute-done.2.near_b
  9.7 0.3 edge_grams.1
  10.0 5.6 %collective-permute-start.4 = (f32[72,128]{1,0:T(8,128)S(1)}, f32[72,128]{1,0:T(8,128)S(1)}, u32[]{:S(2)}, u32[]{:S(2)}) collective-permute-start(f32[72,128]{1,0:T(8,128)S(1)} %get-tuple-element.33), channel_id=1, source_target_pairs={{0,12},{4,8},{8,4},{12,0},{16,28},{20,24},{24,20},{28,16},{1,13},{... | collective-permute-start | bytes 110600 | tf_op jit(solution)/shard_map/ppermute | solution.py:47
  15.6 0.5 collective-permute-start.5
  16.1 1.0 %collective-permute-start.6 = (f32[72,128]{1,0:T(8,128)S(1)}, f32[72,128]{1,0:T(8,128)S(1)}, u32[]{:S(2)}, u32[]{:S(2)}) collective-permute-start(f32[72,128]{1,0:T(8,128)S(1)} %get-tuple-element.33), channel_id=1, source_target_pairs={{0,4},{4,0},{8,12},{12,8},{16,20},{20,16},{24,28},{28,24},{1,5},{5... | collective-permute-start | bytes 110600 | tf_op jit(solution)/shard_map/ppermute | solution.py:47
  17.1 0.0 collective-permute-start.3
  17.1 0.5 %collective-permute-done.4 = f32[72,128]{1,0:T(8,128)S(1)} collective-permute-done((f32[72,128]{1,0:T(8,128)S(1)}, f32[72,128]{1,0:T(8,128)S(1)}, u32[]{:S(2)}, u32[]{:S(2)}) %collective-permute-start.4) | collective-permute-done | bytes 36896 | tf_op jit(solution)/shard_map/ppermute | solution.py:47
  17.7 1.9 %collective-permute-done.5 = f32[72,128]{1,0:T(8,128)S(1)} collective-permute-done((f32[72,128]{1,0:T(8,128)S(1)}, f32[72,128]{1,0:T(8,128)S(1)}, u32[]{:S(2)}, u32[]{:S(2)}) %collective-permute-start.5) | collective-permute-done | bytes 36896 | tf_op jit(solution)/shard_map/ppermute | solution.py:47
  19.6 0.5 collective-permute-done.6
  20.0 2.7 %collective-permute-start.7 = (f32[72,128]{1,0:T(8,128)S(1)}, f32[72,128]{1,0:T(8,128)S(1)}, u32[]{:S(2)}, u32[]{:S(2)}) collective-permute-start(f32[72,128]{1,0:T(8,128)S(1)} %add_add_fusion.1), channel_id=1, source_target_pairs={{0,16},{4,20},{8,24},{12,28},{16,0},{20,4},{24,8},{28,12},{1,17},{... | collective-permute-start | bytes 110600 | tf_op jit(solution)/shard_map/ppermute | solution.py:47
  22.7 0.0 collective-permute-done.3.peer_step
  22.7 1.8 %near_grams.1 = (f32[256,256]{1,0:T(8,128)S(1)}, bf16[256,2048]{1,0:T(8,128)(2,1)S(1)}, bf16[256,2048]{1,0:T(8,128)(2,1)S(1)}) custom-call(f32[2048,128]{1,0:T(8,128)S(1)} %get-tuple-element.26.wo, f32[512,128]{1,0:T(8,128)S(1)} %get-tuple-element.31.own_step, f32[512,128]{1,0:T(8,128)S(1)} %collective-permute-done.3.peer_step, f32[2048,128]{1,0:T(8,128)S(1)} %bitcast.6, ...), custom_call_target="tpu_custom_call" | custom-call | flops 2500000000 | bytes 1 | tf_op jit(solution)/shard_map/near_grams/pallas_call | solution.py:430
  24.5 0.4 collective-permute-done.7
  25.0 0.0 collective-permute-start.10
  25.0 0.4 collective-permute-start.11
  25.4 1.4 %collective-permute-start.12 = (f32[72,128]{1,0:T(8,128)S(1)}, f32[72,128]{1,0:T(8,128)S(1)}, u32[]{:S(2)}, u32[]{:S(2)}) collective-permute-start(f32[72,128]{1,0:T(8,128)S(1)} %add.30.own_msg), channel_id=1, source_target_pairs={{0,1},{1,0},{2,3},{3,2},{4,5},{5,4},{6,7},{7,6},{8,9},{9,8},{10,11... | collective-permute-start | bytes 110600 | tf_op jit(solution)/shard_map/ppermute | solution.py:47
  26.8 0.2 collective-permute-done.8.far_own.refs_2_
  27.0 0.7 %far_grams.1.far_ref = f32[256,128]{1,0:T(8,128)S(1)} custom-call(bf16[256,2048]{1,0:T(8,128)(2,1)S(1)} %get-tuple-element.35.high_t, bf16[256,2048]{1,0:T(8,128)(2,1)S(1)} %get-tuple-element.36.low_t, f32[2048,128]{1,0:T(8,128)S(1)} %collective-permute-done.8.far_own.refs_2_), custom_call_target="tpu_custom_call" | custom-call | flops 700000000 | bytes 1 | tf_op jit(solution)/shard_map/far_grams/pallas_call | solution.py:430
  27.7 0.1 collective-permute-start.9
  27.8 0.6 %collective-permute-done.10.far_msg = f32[72,128]{1,0:T(8,128)S(1)} collective-permute-done((f32[72,128]{1,0:T(8,128)S(1)}, f32[72,128]{1,0:T(8,128)S(1)}, u32[]{:S(2)}, u32[]{:S(2)}) %collective-permute-start.10) | collective-permute-done | bytes 36896 | tf_op jit(solution)/shard_map/ppermute | solution.py:47
  28.4 0.8 %collective-permute-done.11.y_msg = f32[72,128]{1,0:T(8,128)S(1)} collective-permute-done((f32[72,128]{1,0:T(8,128)S(1)}, f32[72,128]{1,0:T(8,128)S(1)}, u32[]{:S(2)}, u32[]{:S(2)}) %collective-permute-start.11) | collective-permute-done | bytes 36896 | tf_op jit(solution)/shard_map/ppermute | solution.py:47
  29.2 0.0 collective-permute-done.12.core_msg
  29.2 2.1 %first_rotation.1 = (f32[128,256]{1,0:T(8,128)S(1)}, f32[128,256]{1,0:T(8,128)S(1)}) custom-call(f32[72,128]{1,0:T(8,128)S(1)} %collective-permute-done.10.far_msg, f32[72,128]{1,0:T(8,128)S(1)} %collective-permute-done.11.y_msg, f32[72,128]{1,0:T(8,128)S(1)} %collective-permute-done.12.core_msg, f32[72,128]{1,0:T(8,128)S(1)} %add.30.own_msg), custom_call_target="tpu_custom_call" | custom-call | flops 4000000000 | bytes 1 | tf_op jit(solution)/shard_map/first_rotation/pallas_call | solution.py:430
  31.3 0.0 collective-permute-done.9.far_peer_ref
  31.3 0.5 rotated_grams.1
  31.7 0.1 collective-permute-start.19
  31.8 2.6 %collective-permute-start.13 = (f32[72,128]{1,0:T(8,128)S(1)}, f32[72,128]{1,0:T(8,128)S(1)}, u32[]{:S(2)}, u32[]{:S(2)}) collective-permute-start(f32[72,128]{1,0:T(8,128)S(1)} %rotated_grams.1), channel_id=1, source_target_pairs={{0,12},{4,8},{8,4},{12,0},{16,28},{20,24},{24,20},{28,16},{1,13},{... | collective-permute-start | bytes 110600 | tf_op jit(solution)/shard_map/ppermute | solution.py:47
  34.4 0.1 collective-permute-start.14
  34.5 0.8 %collective-permute-start.15 = (f32[72,128]{1,0:T(8,128)S(1)}, f32[72,128]{1,0:T(8,128)S(1)}, u32[]{:S(2)}, u32[]{:S(2)}) collective-permute-start(f32[72,128]{1,0:T(8,128)S(1)} %rotated_grams.1), channel_id=1, source_target_pairs={{0,4},{4,0},{8,12},{12,8},{16,20},{20,16},{24,28},{28,24},{1,5},{5... | collective-permute-start | bytes 110600 | tf_op jit(solution)/shard_map/ppermute | solution.py:47
  35.4 1.4 %collective-permute-done.13 = f32[72,128]{1,0:T(8,128)S(1)} collective-permute-done((f32[72,128]{1,0:T(8,128)S(1)}, f32[72,128]{1,0:T(8,128)S(1)}, u32[]{:S(2)}, u32[]{:S(2)}) %collective-permute-start.13) | collective-permute-done | bytes 36896 | tf_op jit(solution)/shard_map/ppermute | solution.py:47
  36.7 1.6 %collective-permute-done.14 = f32[72,128]{1,0:T(8,128)S(1)} collective-permute-done((f32[72,128]{1,0:T(8,128)S(1)}, f32[72,128]{1,0:T(8,128)S(1)}, u32[]{:S(2)}, u32[]{:S(2)}) %collective-permute-start.14) | collective-permute-done | bytes 36896 | tf_op jit(solution)/shard_map/ppermute | solution.py:47
  38.4 0.1 collective-permute-done.15
  38.5 3.4 %collective-permute-start.16 = (f32[72,128]{1,0:T(8,128)S(1)}, f32[72,128]{1,0:T(8,128)S(1)}, u32[]{:S(2)}, u32[]{:S(2)}) collective-permute-start(f32[72,128]{1,0:T(8,128)S(1)} %add_add_fusion), channel_id=1, source_target_pairs={{0,18},{1,19},{2,16},{3,17},{4,22},{5,23},{6,20},{7,21},{8,26},{9,... | collective-permute-start | bytes 110600 | tf_op jit(solution)/shard_map/ppermute | solution.py:411
  41.9 0.5 %collective-permute-start.17 = (f32[72,128]{1,0:T(8,128)S(1)}, f32[72,128]{1,0:T(8,128)S(1)}, u32[]{:S(2)}, u32[]{:S(2)}) collective-permute-start(f32[72,128]{1,0:T(8,128)S(1)} %add_add_fusion), channel_id=1, source_target_pairs={{0,16},{4,20},{8,24},{12,28},{16,0},{20,4},{24,8},{28,12},{1,17},{... | collective-permute-start | bytes 110600 | tf_op jit(solution)/shard_map/ppermute | solution.py:47
  42.5 0.5 %collective-permute-start.18 = (f32[72,128]{1,0:T(8,128)S(1)}, f32[72,128]{1,0:T(8,128)S(1)}, u32[]{:S(2)}, u32[]{:S(2)}) collective-permute-start(f32[72,128]{1,0:T(8,128)S(1)} %add_add_fusion), channel_id=1, source_target_pairs={{0,2},{1,3},{2,0},{3,1},{4,6},{5,7},{6,4},{7,5},{8,10},{9,11},{10,... | collective-permute-start | bytes 110600 | tf_op jit(solution)/shard_map/ppermute | solution.py:47
  43.0 0.0 collective-permute-done.19.refs_3_
  43.0 1.4 %turned_blocks.1 = (bf16[2048,256]{1,0:T(8,128)(2,1)S(1)}, bf16[2048,256]{1,0:T(8,128)(2,1)S(1)}) custom-call(f32[2048,128]{1,0:T(8,128)S(1)} %bitcast.7, f32[2048,128]{1,0:T(8,128)S(1)} %collective-permute-done.refs_1_.p_ref, f32[2048,128]{1,0:T(8,128)S(1)} %collective-permute-done.8.far_own.refs_2_, f32[2048,128]{1,0:T(8,128)S(1)} %collective-permute-done.19.refs_3_, ...), custom_call_target="tpu_custom_call" | custom-call | flops 1400000000 | bytes 1 | tf_op jit(solution)/shard_map/turned_blocks/pallas_call | solution.py:430
  44.4 2.4 %collective-permute-done.17 = f32[72,128]{1,0:T(8,128)S(1)} collective-permute-done((f32[72,128]{1,0:T(8,128)S(1)}, f32[72,128]{1,0:T(8,128)S(1)}, u32[]{:S(2)}, u32[]{:S(2)}) %collective-permute-start.17) | collective-permute-done | bytes 36896 | tf_op jit(solution)/shard_map/ppermute | solution.py:47
  46.8 0.0 collective-permute-done.18
  46.8 3.3 %last_rotation.1 = f32[2048,128]{1,0:T(8,128)} custom-call(f32[72,128]{1,0:T(8,128)S(1)} %add.34.own_msg, f32[72,128]{1,0:T(8,128)S(1)} %add.35.y_msg, bf16[2048,256]{1,0:T(8,128)(2,1)S(1)} %get-tuple-element.42.high_ref, bf16[2048,256]{1,0:T(8,128)(2,1)S(1)} %get-tuple-element.46.low_ref), custom_call_target="tpu_custom_call" | custom-call | flops 4000000000 | bytes 1 | tf_op jit(solution)/shard_map/last_rotation/pallas_call | solution.py:498
  (8 shorter events, 0.1 us)
Async XLA Ops:
  0.0 6.3 %copy-start = (f32[8,16,16,128]{3,2,1,0:T(8,128)S(1)}, f32[8,16,16,128]{3,2,1,0:T(8,128)}, u32[]{:S(2)}) copy-start(f32[8,16,16,128]{3,2,1,0:T(8,128)} %param.1) | copy-start | bytes 3145732
  0.0 6.3 %collective-permute-start = (f32[2048,128]{1,0:T(8,128)}, f32[2048,128]{1,0:T(8,128)S(1)}, u32[]{:S(2)}, u32[]{:S(2)}) collective-permute-start(f32[2048,128]{1,0:T(8,128)} %bitcast.2), channel_id=1, source_target_pairs={{0,1},{1,0},{2,3},{3,2},{4,5},{5,4},{6,7},{7,6},{8,9},{9,8},{10,11... | collective-permute-start | bytes 3145736 | tf_op jit(solution)/shard_map/ppermute | solution.py:47
  0.5 26.6 %collective-permute-start.8 = (f32[2048,128]{1,0:T(8,128)}, f32[2048,128]{1,0:T(8,128)S(1)}, u32[]{:S(2)}, u32[]{:S(2)}) collective-permute-start(f32[2048,128]{1,0:T(8,128)} %bitcast.3), channel_id=1, source_target_pairs={{0,2},{1,3},{2,0},{3,1},{4,6},{5,7},{6,4},{7,5},{8,10},{9,11},{10,... | collective-permute-start | bytes 3145736 | tf_op jit(solution)/shard_map/ppermute | solution.py:47
  4.0 5.6 %collective-permute-start.1 = (f32[256,128]{1,0:T(8,128)S(1)}, f32[256,128]{1,0:T(8,128)S(1)}, u32[]{:S(2)}, u32[]{:S(2)}) collective-permute-start(f32[256,128]{1,0:T(8,128)S(1)} %get-tuple-element.27.edge_a), channel_id=1, source_target_pairs={{0,4},{4,0},{8,12},{12,8},{16,20},{20,16},{24,28},{28,24},{1,5},{5... | collective-permute-start | bytes 393224 | tf_op jit(solution)/shard_map/ppermute | solution.py:454
  5.6 4.1 %collective-permute-start.2 = (f32[256,128]{1,0:T(8,128)S(1)}, f32[256,128]{1,0:T(8,128)S(1)}, u32[]{:S(2)}, u32[]{:S(2)}) collective-permute-start(f32[256,128]{1,0:T(8,128)S(1)} %get-tuple-element.28.edge_b), channel_id=1, source_target_pairs={{4,8},{12,16},{20,24},{8,4},{16,12},{24,20},{5,9},{13,17},{21,25},... | collective-permute-start | bytes 393224 | tf_op jit(solution)/shard_map/ppermute | solution.py:455
  10.0 7.6 %collective-permute-start.4 = (f32[72,128]{1,0:T(8,128)S(1)}, f32[72,128]{1,0:T(8,128)S(1)}, u32[]{:S(2)}, u32[]{:S(2)}) collective-permute-start(f32[72,128]{1,0:T(8,128)S(1)} %get-tuple-element.33), channel_id=1, source_target_pairs={{0,12},{4,8},{8,4},{12,0},{16,28},{20,24},{24,20},{28,16},{1,13},{... | collective-permute-start | bytes 110600 | tf_op jit(solution)/shard_map/ppermute | solution.py:47
  15.6 4.0 %collective-permute-start.5 = (f32[72,128]{1,0:T(8,128)S(1)}, f32[72,128]{1,0:T(8,128)S(1)}, u32[]{:S(2)}, u32[]{:S(2)}) collective-permute-start(f32[72,128]{1,0:T(8,128)S(1)} %get-tuple-element.33), channel_id=1, source_target_pairs={{0,8},{4,12},{8,0},{12,4},{16,24},{20,28},{24,16},{28,20},{1,9},{5... | collective-permute-start | bytes 110600 | tf_op jit(solution)/shard_map/ppermute | solution.py:47
  16.1 4.0 %collective-permute-start.6 = (f32[72,128]{1,0:T(8,128)S(1)}, f32[72,128]{1,0:T(8,128)S(1)}, u32[]{:S(2)}, u32[]{:S(2)}) collective-permute-start(f32[72,128]{1,0:T(8,128)S(1)} %get-tuple-element.33), channel_id=1, source_target_pairs={{0,4},{4,0},{8,12},{12,8},{16,20},{20,16},{24,28},{28,24},{1,5},{5... | collective-permute-start | bytes 110600 | tf_op jit(solution)/shard_map/ppermute | solution.py:47
  17.1 5.6 %collective-permute-start.3 = (f32[512,128]{1,0:T(8,128)S(1)}, f32[512,128]{1,0:T(8,128)S(1)}, u32[]{:S(2)}, u32[]{:S(2)}) collective-permute-start(f32[512,128]{1,0:T(8,128)S(1)} %get-tuple-element.31.own_step), channel_id=1, source_target_pairs={{0,1},{1,0},{2,3},{3,2},{4,5},{5,4},{6,7},{7,6},{8,9},{9,8},{10,11... | collective-permute-start | bytes 786440 | tf_op jit(solution)/shard_map/ppermute | solution.py:47
  20.0 4.9 %collective-permute-start.7 = (f32[72,128]{1,0:T(8,128)S(1)}, f32[72,128]{1,0:T(8,128)S(1)}, u32[]{:S(2)}, u32[]{:S(2)}) collective-permute-start(f32[72,128]{1,0:T(8,128)S(1)} %add_add_fusion.1), channel_id=1, source_target_pairs={{0,16},{4,20},{8,24},{12,28},{16,0},{20,4},{24,8},{28,12},{1,17},{... | collective-permute-start | bytes 110600 | tf_op jit(solution)/shard_map/ppermute | solution.py:47
  25.0 3.4 %collective-permute-start.10 = (f32[72,128]{1,0:T(8,128)S(1)}, f32[72,128]{1,0:T(8,128)S(1)}, u32[]{:S(2)}, u32[]{:S(2)}) collective-permute-start(f32[72,128]{1,0:T(8,128)S(1)} %add.30.own_msg), channel_id=1, source_target_pairs={{0,3},{1,2},{2,1},{3,0},{4,7},{5,6},{6,5},{7,4},{8,11},{9,10},{10,... | collective-permute-start | bytes 110600 | tf_op jit(solution)/shard_map/ppermute | solution.py:47
  25.0 4.2 %collective-permute-start.11 = (f32[72,128]{1,0:T(8,128)S(1)}, f32[72,128]{1,0:T(8,128)S(1)}, u32[]{:S(2)}, u32[]{:S(2)}) collective-permute-start(f32[72,128]{1,0:T(8,128)S(1)} %add.30.own_msg), channel_id=1, source_target_pairs={{0,2},{1,3},{2,0},{3,1},{4,6},{5,7},{6,4},{7,5},{8,10},{9,11},{10,... | collective-permute-start | bytes 110600 | tf_op jit(solution)/shard_map/ppermute | solution.py:47
  25.4 3.7 %collective-permute-start.12 = (f32[72,128]{1,0:T(8,128)S(1)}, f32[72,128]{1,0:T(8,128)S(1)}, u32[]{:S(2)}, u32[]{:S(2)}) collective-permute-start(f32[72,128]{1,0:T(8,128)S(1)} %add.30.own_msg), channel_id=1, source_target_pairs={{0,1},{1,0},{2,3},{3,2},{4,5},{5,4},{6,7},{7,6},{8,9},{9,8},{10,11... | collective-permute-start | bytes 110600 | tf_op jit(solution)/shard_map/ppermute | solution.py:47
  27.7 3.5 %collective-permute-start.9 = (f32[256,128]{1,0:T(8,128)S(1)}, f32[256,128]{1,0:T(8,128)S(1)}, u32[]{:S(2)}, u32[]{:S(2)}) collective-permute-start(f32[256,128]{1,0:T(8,128)S(1)} %far_grams.1.far_ref), channel_id=1, source_target_pairs={{0,1},{1,0},{2,3},{3,2},{4,5},{5,4},{6,7},{7,6},{8,9},{9,8},{10,11... | collective-permute-start | bytes 393224 | tf_op jit(solution)/shard_map/ppermute | solution.py:47
  31.7 11.2 %collective-permute-start.19 = (f32[2048,128]{1,0:T(8,128)S(1)}, f32[2048,128]{1,0:T(8,128)S(1)}, u32[]{:S(2)}, u32[]{:S(2)}) collective-permute-start(f32[2048,128]{1,0:T(8,128)S(1)} %collective-permute-done.8.far_own.refs_2_), channel_id=1, source_target_pairs={{0,1},{1,0},{2,3},{3,2},{4,5},{5,4},{6,7},{7,6},{8,9},{9,8},{10,11... | collective-permute-start | bytes 3145736 | tf_op jit(solution)/shard_map/ppermute | solution.py:47
  31.8 4.9 %collective-permute-start.13 = (f32[72,128]{1,0:T(8,128)S(1)}, f32[72,128]{1,0:T(8,128)S(1)}, u32[]{:S(2)}, u32[]{:S(2)}) collective-permute-start(f32[72,128]{1,0:T(8,128)S(1)} %rotated_grams.1), channel_id=1, source_target_pairs={{0,12},{4,8},{8,4},{12,0},{16,28},{20,24},{24,20},{28,16},{1,13},{... | collective-permute-start | bytes 110600 | tf_op jit(solution)/shard_map/ppermute | solution.py:47
  34.4 4.0 %collective-permute-start.14 = (f32[72,128]{1,0:T(8,128)S(1)}, f32[72,128]{1,0:T(8,128)S(1)}, u32[]{:S(2)}, u32[]{:S(2)}) collective-permute-start(f32[72,128]{1,0:T(8,128)S(1)} %rotated_grams.1), channel_id=1, source_target_pairs={{0,8},{4,12},{8,0},{12,4},{16,24},{20,28},{24,16},{28,20},{1,9},{5... | collective-permute-start | bytes 110600 | tf_op jit(solution)/shard_map/ppermute | solution.py:47
  34.5 4.0 %collective-permute-start.15 = (f32[72,128]{1,0:T(8,128)S(1)}, f32[72,128]{1,0:T(8,128)S(1)}, u32[]{:S(2)}, u32[]{:S(2)}) collective-permute-start(f32[72,128]{1,0:T(8,128)S(1)} %rotated_grams.1), channel_id=1, source_target_pairs={{0,4},{4,0},{8,12},{12,8},{16,20},{20,16},{24,28},{28,24},{1,5},{5... | collective-permute-start | bytes 110600 | tf_op jit(solution)/shard_map/ppermute | solution.py:47
  38.5 5.9 %collective-permute-start.16 = (f32[72,128]{1,0:T(8,128)S(1)}, f32[72,128]{1,0:T(8,128)S(1)}, u32[]{:S(2)}, u32[]{:S(2)}) collective-permute-start(f32[72,128]{1,0:T(8,128)S(1)} %add_add_fusion), channel_id=1, source_target_pairs={{0,18},{1,19},{2,16},{3,17},{4,22},{5,23},{6,20},{7,21},{8,26},{9,... | collective-permute-start | bytes 110600 | tf_op jit(solution)/shard_map/ppermute | solution.py:411
  41.9 4.9 %collective-permute-start.17 = (f32[72,128]{1,0:T(8,128)S(1)}, f32[72,128]{1,0:T(8,128)S(1)}, u32[]{:S(2)}, u32[]{:S(2)}) collective-permute-start(f32[72,128]{1,0:T(8,128)S(1)} %add_add_fusion), channel_id=1, source_target_pairs={{0,16},{4,20},{8,24},{12,28},{16,0},{20,4},{24,8},{28,12},{1,17},{... | collective-permute-start | bytes 110600 | tf_op jit(solution)/shard_map/ppermute | solution.py:47
  42.5 4.3 %collective-permute-start.18 = (f32[72,128]{1,0:T(8,128)S(1)}, f32[72,128]{1,0:T(8,128)S(1)}, u32[]{:S(2)}, u32[]{:S(2)}) collective-permute-start(f32[72,128]{1,0:T(8,128)S(1)} %add_add_fusion), channel_id=1, source_target_pairs={{0,2},{1,3},{2,0},{3,1},{4,6},{5,7},{6,4},{7,5},{8,10},{9,11},{10,... | collective-permute-start | bytes 110600 | tf_op jit(solution)/shard_map/ppermute | solution.py:47

commit v8 on v7

--- a/solution.py
+++ b/solution.py
@@ -494,7 +494,7 @@
     )
     own_msg, y_msg = summed_with_y(msg, highs)
 
-    step = 512
+    step = 256
     mixed = pl.pallas_call(
         last_kernel,
         in_specs=[VMEM] * 4,

time: 50.3 us -> 50.3 us (level)
  no operation moved by 1% of the time
where the time goes in v8:
time: 50.3 us; the launch traced here: 50.1 us
  starting transfers between devices  25 us (50%)
  waiting for transfers between devices  12.6 us (25%)
  Pallas kernels  12.3 us (24%)
    ppermute x17, starting transfers between devices, exchanged(): return lax.ppermute(value, axis, [(i, i ^ mask) for i in range(count)])  19.4 us
    ppermute x17, waiting for transfers between devices, exchanged(): return lax.ppermute(value, axis, [(i, i ^ mask) for i in range(count)])  10.4 us
    pallas_call x7, Pallas kernels, call(): pl.pallas_call(body, in_specs=[VMEM] * len(inputs), out_specs=[VMEM] * le...  7.99 us
    ppermute x1, starting transfers between devices, summed_with_y(): other_there = lax.ppermute(value, ('space', 'blk'), route)  3.41 us
    pallas_call x1, Pallas kernels, shards(): pl.pallas_call(last_kernel, in_specs=[VMEM] * 4, out_specs=pl.BlockSpec(m...  3.31 us
    ppermute x1, waiting for transfers between devices, shards(): near_a = lax.ppermute(edge_a, 'space', route_a)  2.23 us
    ppermute x1, starting transfers between devices, shards(): near_a = lax.ppermute(edge_a, 'space', route_a)  1.56 us
  transfers between devices with their start and end apart: 20, of which 12 were waited for; matrix products, arithmetic and copies ran while one was open for 0% of the time, Pallas kernels for 17%

profile of v8, /device:TPU:0, one launch (start us, length us, event | category | flops | bytes accessed | tf_op | source)
XLA Modules:
  0.0 50.1 jit_solution(13152910427840955123)
XLA Ops:
  0.0 0.5 collective-permute-start
  0.5 2.6 %collective-permute-start.8 = (f32[2048,128]{1,0:T(8,128)}, f32[2048,128]{1,0:T(8,128)S(1)}, u32[]{:S(2)}, u32[]{:S(2)}) collective-permute-start(f32[2048,128]{1,0:T(8,128)} %bitcast.3), channel_id=1, source_target_pairs={{0,2},{1,3},{2,0},{3,1},{4,6},{5,7},{6,4},{7,5},{8,10},{9,11},{10,... | collective-permute-start | bytes 3145736 | tf_op jit(solution)/shard_map/ppermute | solution.py:47
  3.0 1.0 %edges.1 = (f32[256,128]{1,0:T(8,128)S(1)}, f32[256,128]{1,0:T(8,128)S(1)}) custom-call(f32[2048,128]{1,0:T(8,128)} %bitcast.4), custom_call_target="tpu_custom_call" | custom-call | flops 100000000 | bytes 1 | tf_op jit(solution)/shard_map/edges/pallas_call | solution.py:444
  4.0 1.6 %collective-permute-start.1 = (f32[256,128]{1,0:T(8,128)S(1)}, f32[256,128]{1,0:T(8,128)S(1)}, u32[]{:S(2)}, u32[]{:S(2)}) collective-permute-start(f32[256,128]{1,0:T(8,128)S(1)} %get-tuple-element.27.edge_a), channel_id=1, source_target_pairs={{0,4},{4,0},{8,12},{12,8},{16,20},{20,16},{24,28},{28,24},{1,5},{5... | collective-permute-start | bytes 393224 | tf_op jit(solution)/shard_map/ppermute | solution.py:454
  5.6 0.7 %collective-permute-start.2 = (f32[256,128]{1,0:T(8,128)S(1)}, f32[256,128]{1,0:T(8,128)S(1)}, u32[]{:S(2)}, u32[]{:S(2)}) collective-permute-start(f32[256,128]{1,0:T(8,128)S(1)} %get-tuple-element.28.edge_b), channel_id=1, source_target_pairs={{4,8},{12,16},{20,24},{8,4},{16,12},{24,20},{5,9},{13,17},{21,25},... | collective-permute-start | bytes 393224 | tf_op jit(solution)/shard_map/ppermute | solution.py:455
  6.3 0.0 collective-permute-done.refs_1_.p_ref
  6.3 1.2 %inner_grams.1 = (f32[2048,128]{1,0:T(8,128)S(1)}, f32[128,128]{1,0:T(8,128)S(1)}, f32[8,128]{1,0:T(8,128)S(1)}) custom-call(f32[2048,128]{1,0:T(8,128)S(1)} %bitcast.5, f32[2048,128]{1,0:T(8,128)S(1)} %collective-permute-done.refs_1_.p_ref), custom_call_target="tpu_custom_call" | custom-call | flops 100000000 | bytes 1 | tf_op jit(solution)/shard_map/inner_grams/pallas_call | solution.py:430
  7.4 2.2 %collective-permute-done.1.near_a = f32[256,128]{1,0:T(8,128)S(1)} collective-permute-done((f32[256,128]{1,0:T(8,128)S(1)}, f32[256,128]{1,0:T(8,128)S(1)}, u32[]{:S(2)}, u32[]{:S(2)}) %collective-permute-start.1) | collective-permute-done | bytes 131104 | tf_op jit(solution)/shard_map/ppermute | solution.py:454
  9.7 0.0 collective-permute-done.2.near_b
  9.7 0.3 edge_grams.1
  10.0 5.6 %collective-permute-start.4 = (f32[72,128]{1,0:T(8,128)S(1)}, f32[72,128]{1,0:T(8,128)S(1)}, u32[]{:S(2)}, u32[]{:S(2)}) collective-permute-start(f32[72,128]{1,0:T(8,128)S(1)} %get-tuple-element.33), channel_id=1, source_target_pairs={{0,12},{4,8},{8,4},{12,0},{16,28},{20,24},{24,20},{28,16},{1,13},{... | collective-permute-start | bytes 110600 | tf_op jit(solution)/shard_map/ppermute | solution.py:47
  15.6 0.5 collective-permute-start.5
  16.1 1.0 %collective-permute-start.6 = (f32[72,128]{1,0:T(8,128)S(1)}, f32[72,128]{1,0:T(8,128)S(1)}, u32[]{:S(2)}, u32[]{:S(2)}) collective-permute-start(f32[72,128]{1,0:T(8,128)S(1)} %get-tuple-element.33), channel_id=1, source_target_pairs={{0,4},{4,0},{8,12},{12,8},{16,20},{20,16},{24,28},{28,24},{1,5},{5... | collective-permute-start | bytes 110600 | tf_op jit(solution)/shard_map/ppermute | solution.py:47
  17.1 0.0 collective-permute-start.3
  17.1 0.5 %collective-permute-done.4 = f32[72,128]{1,0:T(8,128)S(1)} collective-permute-done((f32[72,128]{1,0:T(8,128)S(1)}, f32[72,128]{1,0:T(8,128)S(1)}, u32[]{:S(2)}, u32[]{:S(2)}) %collective-permute-start.4) | collective-permute-done | bytes 36896 | tf_op jit(solution)/shard_map/ppermute | solution.py:47
  17.7 1.9 %collective-permute-done.5 = f32[72,128]{1,0:T(8,128)S(1)} collective-permute-done((f32[72,128]{1,0:T(8,128)S(1)}, f32[72,128]{1,0:T(8,128)S(1)}, u32[]{:S(2)}, u32[]{:S(2)}) %collective-permute-start.5) | collective-permute-done | bytes 36896 | tf_op jit(solution)/shard_map/ppermute | solution.py:47
  19.6 0.5 collective-permute-done.6
  20.0 2.7 %collective-permute-start.7 = (f32[72,128]{1,0:T(8,128)S(1)}, f32[72,128]{1,0:T(8,128)S(1)}, u32[]{:S(2)}, u32[]{:S(2)}) collective-permute-start(f32[72,128]{1,0:T(8,128)S(1)} %add_add_fusion.1), channel_id=1, source_target_pairs={{0,16},{4,20},{8,24},{12,28},{16,0},{20,4},{24,8},{28,12},{1,17},{... | collective-permute-start | bytes 110600 | tf_op jit(solution)/shard_map/ppermute | solution.py:47
  22.7 0.0 collective-permute-done.3.peer_step
  22.7 1.8 %near_grams.1 = (f32[256,256]{1,0:T(8,128)S(1)}, bf16[256,2048]{1,0:T(8,128)(2,1)S(1)}, bf16[256,2048]{1,0:T(8,128)(2,1)S(1)}) custom-call(f32[2048,128]{1,0:T(8,128)S(1)} %get-tuple-element.26.wo, f32[512,128]{1,0:T(8,128)S(1)} %get-tuple-element.31.own_step, f32[512,128]{1,0:T(8,128)S(1)} %collective-permute-done.3.peer_step, f32[2048,128]{1,0:T(8,128)S(1)} %bitcast.6, ...), custom_call_target="tpu_custom_call" | custom-call | flops 2500000000 | bytes 1 | tf_op jit(solution)/shard_map/near_grams/pallas_call | solution.py:430
  24.5 0.4 collective-permute-done.7
  25.0 0.0 collective-permute-start.10
  25.0 0.4 collective-permute-start.11
  25.4 1.4 %collective-permute-start.12 = (f32[72,128]{1,0:T(8,128)S(1)}, f32[72,128]{1,0:T(8,128)S(1)}, u32[]{:S(2)}, u32[]{:S(2)}) collective-permute-start(f32[72,128]{1,0:T(8,128)S(1)} %add.30.own_msg), channel_id=1, source_target_pairs={{0,1},{1,0},{2,3},{3,2},{4,5},{5,4},{6,7},{7,6},{8,9},{9,8},{10,11... | collective-permute-start | bytes 110600 | tf_op jit(solution)/shard_map/ppermute | solution.py:47
  26.8 0.2 collective-permute-done.8.far_own.refs_2_
  27.0 0.7 %far_grams.1.far_ref = f32[256,128]{1,0:T(8,128)S(1)} custom-call(bf16[256,2048]{1,0:T(8,128)(2,1)S(1)} %get-tuple-element.35.high_t, bf16[256,2048]{1,0:T(8,128)(2,1)S(1)} %get-tuple-element.36.low_t, f32[2048,128]{1,0:T(8,128)S(1)} %collective-permute-done.8.far_own.refs_2_), custom_call_target="tpu_custom_call" | custom-call | flops 700000000 | bytes 1 | tf_op jit(solution)/shard_map/far_grams/pallas_call | solution.py:430
  27.7 0.1 collective-permute-start.9
  27.8 0.6 %collective-permute-done.10.far_msg = f32[72,128]{1,0:T(8,128)S(1)} collective-permute-done((f32[72,128]{1,0:T(8,128)S(1)}, f32[72,128]{1,0:T(8,128)S(1)}, u32[]{:S(2)}, u32[]{:S(2)}) %collective-permute-start.10) | collective-permute-done | bytes 36896 | tf_op jit(solution)/shard_map/ppermute | solution.py:47
  28.4 0.8 %collective-permute-done.11.y_msg = f32[72,128]{1,0:T(8,128)S(1)} collective-permute-done((f32[72,128]{1,0:T(8,128)S(1)}, f32[72,128]{1,0:T(8,128)S(1)}, u32[]{:S(2)}, u32[]{:S(2)}) %collective-permute-start.11) | collective-permute-done | bytes 36896 | tf_op jit(solution)/shard_map/ppermute | solution.py:47
  29.2 0.0 collective-permute-done.12.core_msg
  29.2 2.1 %first_rotation.1 = (f32[128,256]{1,0:T(8,128)S(1)}, f32[128,256]{1,0:T(8,128)S(1)}) custom-call(f32[72,128]{1,0:T(8,128)S(1)} %collective-permute-done.10.far_msg, f32[72,128]{1,0:T(8,128)S(1)} %collective-permute-done.11.y_msg, f32[72,128]{1,0:T(8,128)S(1)} %collective-permute-done.12.core_msg, f32[72,128]{1,0:T(8,128)S(1)} %add.30.own_msg), custom_call_target="tpu_custom_call" | custom-call | flops 4000000000 | bytes 1 | tf_op jit(solution)/shard_map/first_rotation/pallas_call | solution.py:430
  31.3 0.0 collective-permute-done.9.far_peer_ref
  31.3 0.5 rotated_grams.1
  31.7 0.1 collective-permute-start.19
  31.8 2.6 %collective-permute-start.13 = (f32[72,128]{1,0:T(8,128)S(1)}, f32[72,128]{1,0:T(8,128)S(1)}, u32[]{:S(2)}, u32[]{:S(2)}) collective-permute-start(f32[72,128]{1,0:T(8,128)S(1)} %rotated_grams.1), channel_id=1, source_target_pairs={{0,12},{4,8},{8,4},{12,0},{16,28},{20,24},{24,20},{28,16},{1,13},{... | collective-permute-start | bytes 110600 | tf_op jit(solution)/shard_map/ppermute | solution.py:47
  34.4 0.1 collective-permute-start.14
  34.5 0.8 %collective-permute-start.15 = (f32[72,128]{1,0:T(8,128)S(1)}, f32[72,128]{1,0:T(8,128)S(1)}, u32[]{:S(2)}, u32[]{:S(2)}) collective-permute-start(f32[72,128]{1,0:T(8,128)S(1)} %rotated_grams.1), channel_id=1, source_target_pairs={{0,4},{4,0},{8,12},{12,8},{16,20},{20,16},{24,28},{28,24},{1,5},{5... | collective-permute-start | bytes 110600 | tf_op jit(solution)/shard_map/ppermute | solution.py:47
  35.4 1.4 %collective-permute-done.13 = f32[72,128]{1,0:T(8,128)S(1)} collective-permute-done((f32[72,128]{1,0:T(8,128)S(1)}, f32[72,128]{1,0:T(8,128)S(1)}, u32[]{:S(2)}, u32[]{:S(2)}) %collective-permute-start.13) | collective-permute-done | bytes 36896 | tf_op jit(solution)/shard_map/ppermute | solution.py:47
  36.7 1.6 %collective-permute-done.14 = f32[72,128]{1,0:T(8,128)S(1)} collective-permute-done((f32[72,128]{1,0:T(8,128)S(1)}, f32[72,128]{1,0:T(8,128)S(1)}, u32[]{:S(2)}, u32[]{:S(2)}) %collective-permute-start.14) | collective-permute-done | bytes 36896 | tf_op jit(solution)/shard_map/ppermute | solution.py:47
  38.4 0.1 collective-permute-done.15
  38.5 3.4 %collective-permute-start.16 = (f32[72,128]{1,0:T(8,128)S(1)}, f32[72,128]{1,0:T(8,128)S(1)}, u32[]{:S(2)}, u32[]{:S(2)}) collective-permute-start(f32[72,128]{1,0:T(8,128)S(1)} %add_add_fusion), channel_id=1, source_target_pairs={{0,18},{1,19},{2,16},{3,17},{4,22},{5,23},{6,20},{7,21},{8,26},{9,... | collective-permute-start | bytes 110600 | tf_op jit(solution)/shard_map/ppermute | solution.py:411
  41.9 0.5 %collective-permute-start.17 = (f32[72,128]{1,0:T(8,128)S(1)}, f32[72,128]{1,0:T(8,128)S(1)}, u32[]{:S(2)}, u32[]{:S(2)}) collective-permute-start(f32[72,128]{1,0:T(8,128)S(1)} %add_add_fusion), channel_id=1, source_target_pairs={{0,16},{4,20},{8,24},{12,28},{16,0},{20,4},{24,8},{28,12},{1,17},{... | collective-permute-start | bytes 110600 | tf_op jit(solution)/shard_map/ppermute | solution.py:47
  42.5 0.5 %collective-permute-start.18 = (f32[72,128]{1,0:T(8,128)S(1)}, f32[72,128]{1,0:T(8,128)S(1)}, u32[]{:S(2)}, u32[]{:S(2)}) collective-permute-start(f32[72,128]{1,0:T(8,128)S(1)} %add_add_fusion), channel_id=1, source_target_pairs={{0,2},{1,3},{2,0},{3,1},{4,6},{5,7},{6,4},{7,5},{8,10},{9,11},{10,... | collective-permute-start | bytes 110600 | tf_op jit(solution)/shard_map/ppermute | solution.py:47
  43.0 0.0 collective-permute-done.19.refs_3_
  43.0 1.4 %turned_blocks.1 = (bf16[2048,256]{1,0:T(8,128)(2,1)S(1)}, bf16[2048,256]{1,0:T(8,128)(2,1)S(1)}) custom-call(f32[2048,128]{1,0:T(8,128)S(1)} %bitcast.7, f32[2048,128]{1,0:T(8,128)S(1)} %collective-permute-done.refs_1_.p_ref, f32[2048,128]{1,0:T(8,128)S(1)} %collective-permute-done.8.far_own.refs_2_, f32[2048,128]{1,0:T(8,128)S(1)} %collective-permute-done.19.refs_3_, ...), custom_call_target="tpu_custom_call" | custom-call | flops 1400000000 | bytes 1 | tf_op jit(solution)/shard_map/turned_blocks/pallas_call | solution.py:430
  44.4 2.4 %collective-permute-done.17 = f32[72,128]{1,0:T(8,128)S(1)} collective-permute-done((f32[72,128]{1,0:T(8,128)S(1)}, f32[72,128]{1,0:T(8,128)S(1)}, u32[]{:S(2)}, u32[]{:S(2)}) %collective-permute-start.17) | collective-permute-done | bytes 36896 | tf_op jit(solution)/shard_map/ppermute | solution.py:47
  46.8 0.0 collective-permute-done.18
  46.8 3.3 %last_rotation.1 = f32[2048,128]{1,0:T(8,128)} custom-call(f32[72,128]{1,0:T(8,128)S(1)} %add.34.own_msg, f32[72,128]{1,0:T(8,128)S(1)} %add.35.y_msg, bf16[2048,256]{1,0:T(8,128)(2,1)S(1)} %get-tuple-element.42.high_ref, bf16[2048,256]{1,0:T(8,128)(2,1)S(1)} %get-tuple-element.46.low_ref), custom_call_target="tpu_custom_call" | custom-call | flops 4000000000 | bytes 1 | tf_op jit(solution)/shard_map/last_rotation/pallas_call | solution.py:498
  (8 shorter events, 0.0 us)
Async XLA Ops:
  0.0 6.3 %copy-start = (f32[8,16,16,128]{3,2,1,0:T(8,128)S(1)}, f32[8,16,16,128]{3,2,1,0:T(8,128)}, u32[]{:S(2)}) copy-start(f32[8,16,16,128]{3,2,1,0:T(8,128)} %param.1) | copy-start | bytes 3145732
  0.0 6.3 %collective-permute-start = (f32[2048,128]{1,0:T(8,128)}, f32[2048,128]{1,0:T(8,128)S(1)}, u32[]{:S(2)}, u32[]{:S(2)}) collective-permute-start(f32[2048,128]{1,0:T(8,128)} %bitcast.2), channel_id=1, source_target_pairs={{0,1},{1,0},{2,3},{3,2},{4,5},{5,4},{6,7},{7,6},{8,9},{9,8},{10,11... | collective-permute-start | bytes 3145736 | tf_op jit(solution)/shard_map/ppermute | solution.py:47
  0.5 26.6 %collective-permute-start.8 = (f32[2048,128]{1,0:T(8,128)}, f32[2048,128]{1,0:T(8,128)S(1)}, u32[]{:S(2)}, u32[]{:S(2)}) collective-permute-start(f32[2048,128]{1,0:T(8,128)} %bitcast.3), channel_id=1, source_target_pairs={{0,2},{1,3},{2,0},{3,1},{4,6},{5,7},{6,4},{7,5},{8,10},{9,11},{10,... | collective-permute-start | bytes 3145736 | tf_op jit(solution)/shard_map/ppermute | solution.py:47
  4.0 5.6 %collective-permute-start.1 = (f32[256,128]{1,0:T(8,128)S(1)}, f32[256,128]{1,0:T(8,128)S(1)}, u32[]{:S(2)}, u32[]{:S(2)}) collective-permute-start(f32[256,128]{1,0:T(8,128)S(1)} %get-tuple-element.27.edge_a), channel_id=1, source_target_pairs={{0,4},{4,0},{8,12},{12,8},{16,20},{20,16},{24,28},{28,24},{1,5},{5... | collective-permute-start | bytes 393224 | tf_op jit(solution)/shard_map/ppermute | solution.py:454
  5.6 4.1 %collective-permute-start.2 = (f32[256,128]{1,0:T(8,128)S(1)}, f32[256,128]{1,0:T(8,128)S(1)}, u32[]{:S(2)}, u32[]{:S(2)}) collective-permute-start(f32[256,128]{1,0:T(8,128)S(1)} %get-tuple-element.28.edge_b), channel_id=1, source_target_pairs={{4,8},{12,16},{20,24},{8,4},{16,12},{24,20},{5,9},{13,17},{21,25},... | collective-permute-start | bytes 393224 | tf_op jit(solution)/shard_map/ppermute | solution.py:455
  10.0 7.6 %collective-permute-start.4 = (f32[72,128]{1,0:T(8,128)S(1)}, f32[72,128]{1,0:T(8,128)S(1)}, u32[]{:S(2)}, u32[]{:S(2)}) collective-permute-start(f32[72,128]{1,0:T(8,128)S(1)} %get-tuple-element.33), channel_id=1, source_target_pairs={{0,12},{4,8},{8,4},{12,0},{16,28},{20,24},{24,20},{28,16},{1,13},{... | collective-permute-start | bytes 110600 | tf_op jit(solution)/shard_map/ppermute | solution.py:47
  15.6 4.0 %collective-permute-start.5 = (f32[72,128]{1,0:T(8,128)S(1)}, f32[72,128]{1,0:T(8,128)S(1)}, u32[]{:S(2)}, u32[]{:S(2)}) collective-permute-start(f32[72,128]{1,0:T(8,128)S(1)} %get-tuple-element.33), channel_id=1, source_target_pairs={{0,8},{4,12},{8,0},{12,4},{16,24},{20,28},{24,16},{28,20},{1,9},{5... | collective-permute-start | bytes 110600 | tf_op jit(solution)/shard_map/ppermute | solution.py:47
  16.1 4.0 %collective-permute-start.6 = (f32[72,128]{1,0:T(8,128)S(1)}, f32[72,128]{1,0:T(8,128)S(1)}, u32[]{:S(2)}, u32[]{:S(2)}) collective-permute-start(f32[72,128]{1,0:T(8,128)S(1)} %get-tuple-element.33), channel_id=1, source_target_pairs={{0,4},{4,0},{8,12},{12,8},{16,20},{20,16},{24,28},{28,24},{1,5},{5... | collective-permute-start | bytes 110600 | tf_op jit(solution)/shard_map/ppermute | solution.py:47
  17.1 5.6 %collective-permute-start.3 = (f32[512,128]{1,0:T(8,128)S(1)}, f32[512,128]{1,0:T(8,128)S(1)}, u32[]{:S(2)}, u32[]{:S(2)}) collective-permute-start(f32[512,128]{1,0:T(8,128)S(1)} %get-tuple-element.31.own_step), channel_id=1, source_target_pairs={{0,1},{1,0},{2,3},{3,2},{4,5},{5,4},{6,7},{7,6},{8,9},{9,8},{10,11... | collective-permute-start | bytes 786440 | tf_op jit(solution)/shard_map/ppermute | solution.py:47
  20.0 4.9 %collective-permute-start.7 = (f32[72,128]{1,0:T(8,128)S(1)}, f32[72,128]{1,0:T(8,128)S(1)}, u32[]{:S(2)}, u32[]{:S(2)}) collective-permute-start(f32[72,128]{1,0:T(8,128)S(1)} %add_add_fusion.1), channel_id=1, source_target_pairs={{0,16},{4,20},{8,24},{12,28},{16,0},{20,4},{24,8},{28,12},{1,17},{... | collective-permute-start | bytes 110600 | tf_op jit(solution)/shard_map/ppermute | solution.py:47
  25.0 3.4 %collective-permute-start.10 = (f32[72,128]{1,0:T(8,128)S(1)}, f32[72,128]{1,0:T(8,128)S(1)}, u32[]{:S(2)}, u32[]{:S(2)}) collective-permute-start(f32[72,128]{1,0:T(8,128)S(1)} %add.30.own_msg), channel_id=1, source_target_pairs={{0,3},{1,2},{2,1},{3,0},{4,7},{5,6},{6,5},{7,4},{8,11},{9,10},{10,... | collective-permute-start | bytes 110600 | tf_op jit(solution)/shard_map/ppermute | solution.py:47
  25.0 4.2 %collective-permute-start.11 = (f32[72,128]{1,0:T(8,128)S(1)}, f32[72,128]{1,0:T(8,128)S(1)}, u32[]{:S(2)}, u32[]{:S(2)}) collective-permute-start(f32[72,128]{1,0:T(8,128)S(1)} %add.30.own_msg), channel_id=1, source_target_pairs={{0,2},{1,3},{2,0},{3,1},{4,6},{5,7},{6,4},{7,5},{8,10},{9,11},{10,... | collective-permute-start | bytes 110600 | tf_op jit(solution)/shard_map/ppermute | solution.py:47
  25.4 3.7 %collective-permute-start.12 = (f32[72,128]{1,0:T(8,128)S(1)}, f32[72,128]{1,0:T(8,128)S(1)}, u32[]{:S(2)}, u32[]{:S(2)}) collective-permute-start(f32[72,128]{1,0:T(8,128)S(1)} %add.30.own_msg), channel_id=1, source_target_pairs={{0,1},{1,0},{2,3},{3,2},{4,5},{5,4},{6,7},{7,6},{8,9},{9,8},{10,11... | collective-permute-start | bytes 110600 | tf_op jit(solution)/shard_map/ppermute | solution.py:47
  27.7 3.5 %collective-permute-start.9 = (f32[256,128]{1,0:T(8,128)S(1)}, f32[256,128]{1,0:T(8,128)S(1)}, u32[]{:S(2)}, u32[]{:S(2)}) collective-permute-start(f32[256,128]{1,0:T(8,128)S(1)} %far_grams.1.far_ref), channel_id=1, source_target_pairs={{0,1},{1,0},{2,3},{3,2},{4,5},{5,4},{6,7},{7,6},{8,9},{9,8},{10,11... | collective-permute-start | bytes 393224 | tf_op jit(solution)/shard_map/ppermute | solution.py:47
  31.7 11.2 %collective-permute-start.19 = (f32[2048,128]{1,0:T(8,128)S(1)}, f32[2048,128]{1,0:T(8,128)S(1)}, u32[]{:S(2)}, u32[]{:S(2)}) collective-permute-start(f32[2048,128]{1,0:T(8,128)S(1)} %collective-permute-done.8.far_own.refs_2_), channel_id=1, source_target_pairs={{0,1},{1,0},{2,3},{3,2},{4,5},{5,4},{6,7},{7,6},{8,9},{9,8},{10,11... | collective-permute-start | bytes 3145736 | tf_op jit(solution)/shard_map/ppermute | solution.py:47
  31.8 4.9 %collective-permute-start.13 = (f32[72,128]{1,0:T(8,128)S(1)}, f32[72,128]{1,0:T(8,128)S(1)}, u32[]{:S(2)}, u32[]{:S(2)}) collective-permute-start(f32[72,128]{1,0:T(8,128)S(1)} %rotated_grams.1), channel_id=1, source_target_pairs={{0,12},{4,8},{8,4},{12,0},{16,28},{20,24},{24,20},{28,16},{1,13},{... | collective-permute-start | bytes 110600 | tf_op jit(solution)/shard_map/ppermute | solution.py:47
  34.4 4.0 %collective-permute-start.14 = (f32[72,128]{1,0:T(8,128)S(1)}, f32[72,128]{1,0:T(8,128)S(1)}, u32[]{:S(2)}, u32[]{:S(2)}) collective-permute-start(f32[72,128]{1,0:T(8,128)S(1)} %rotated_grams.1), channel_id=1, source_target_pairs={{0,8},{4,12},{8,0},{12,4},{16,24},{20,28},{24,16},{28,20},{1,9},{5... | collective-permute-start | bytes 110600 | tf_op jit(solution)/shard_map/ppermute | solution.py:47
  34.5 4.0 %collective-permute-start.15 = (f32[72,128]{1,0:T(8,128)S(1)}, f32[72,128]{1,0:T(8,128)S(1)}, u32[]{:S(2)}, u32[]{:S(2)}) collective-permute-start(f32[72,128]{1,0:T(8,128)S(1)} %rotated_grams.1), channel_id=1, source_target_pairs={{0,4},{4,0},{8,12},{12,8},{16,20},{20,16},{24,28},{28,24},{1,5},{5... | collective-permute-start | bytes 110600 | tf_op jit(solution)/shard_map/ppermute | solution.py:47
  38.5 5.9 %collective-permute-start.16 = (f32[72,128]{1,0:T(8,128)S(1)}, f32[72,128]{1,0:T(8,128)S(1)}, u32[]{:S(2)}, u32[]{:S(2)}) collective-permute-start(f32[72,128]{1,0:T(8,128)S(1)} %add_add_fusion), channel_id=1, source_target_pairs={{0,18},{1,19},{2,16},{3,17},{4,22},{5,23},{6,20},{7,21},{8,26},{9,... | collective-permute-start | bytes 110600 | tf_op jit(solution)/shard_map/ppermute | solution.py:411
  41.9 4.9 %collective-permute-start.17 = (f32[72,128]{1,0:T(8,128)S(1)}, f32[72,128]{1,0:T(8,128)S(1)}, u32[]{:S(2)}, u32[]{:S(2)}) collective-permute-start(f32[72,128]{1,0:T(8,128)S(1)} %add_add_fusion), channel_id=1, source_target_pairs={{0,16},{4,20},{8,24},{12,28},{16,0},{20,4},{24,8},{28,12},{1,17},{... | collective-permute-start | bytes 110600 | tf_op jit(solution)/shard_map/ppermute | solution.py:47
  42.5 4.3 %collective-permute-start.18 = (f32[72,128]{1,0:T(8,128)S(1)}, f32[72,128]{1,0:T(8,128)S(1)}, u32[]{:S(2)}, u32[]{:S(2)}) collective-permute-start(f32[72,128]{1,0:T(8,128)S(1)} %add_add_fusion), channel_id=1, source_target_pairs={{0,2},{1,3},{2,0},{3,1},{4,6},{5,7},{6,4},{7,5},{8,10},{9,11},{10,... | collective-permute-start | bytes 110600 | tf_op jit(solution)/shard_map/ppermute | solution.py:47
